TPU v7x, 256 devices: a whole 4x4x8 slice. The times are simulated.
256 devices in a mesh: win: 32 (over x, z), head: 8 (over y, core).
Axes of the slice: x: 4, y: 4, z: 8, core: 2. Of those that a mesh axis runs over, the one named last changes fastest.
Arguments:
- latents: bfloat16 [16384, 3072], P(('win', 'head'))
- modulation: float32 [3, 3072], replicated, may hold values from -2.5 to 2.5
- qkv_weight: bfloat16 [3072, 3, 3072], P(None, None, 'head'), may hold values from -0.109375 to 0.109375
- qkv_bias: float32 [3, 3072], P(None, 'head'), may hold values from -3 to 3
- norm_gain: float32 [2, 128], replicated, may hold values from 1 to 2.5
- out_weight: bfloat16 [3072, 3072], P('head'), may hold values from -0.109375 to 0.109375
- out_bias: float32 [3072], replicated, may hold values from -3 to 3
- key_tiles: int32 [32, 16], P('win'), may hold values from 0 to 127, as said below
- key_count: int32 [32], P('win'), may hold values from 8 to 16, as said below
- strip_rows: int32 [32], replicated, may hold values from 16 to 64, as said below
Outputs:
- blended_out: bfloat16 [16384, 3072], P(('win', 'head'))
Inputs may be any that keep to these rules, and one draw needn't show every extreme that they name: `key_tiles`: entries 2 * j to 2 * j + 1 of window w's row are distinct tiles of window (w + o) mod 32, with o = j // 2 + 1 for even j and o = -(j // 2 + 1) for odd j. `key_count`: some window reads all 16 entries. `strip_rows`: some pair of windows shares 64 rows.
All inputs are finite; a program needn't handle non-finite values.
Results may differ from a plain program's by a relative error of at most 0.0028.
Values may be sent and summed in bfloat16 or wider, within the bound.
No kernel may reach another device: no remote copies, remote signals or barrier semaphores. Data moves between devices by JAX's collectives and lax.ppermute only.
A program may use at most 128 MiB of HBM per device.

v0:
```python
import jax
import jax.numpy as jnp
from jax import lax
from jax.sharding import PartitionSpec as P

TILE = 128
TW = 4
NB = 8
OV = 64


def passed_along(value, axis, steps):
    count = lax.axis_size(axis)
    pairs = [(source, (source + steps) % count) for source in range(count)]
    return lax.ppermute(value, axis, pairs)


def with_halo(cells, sides, width):
    for axis, dim in sides:
        count = lax.axis_size(axis)
        head = lax.slice_in_dim(cells, 0, width, axis=dim)
        tail = lax.slice_in_dim(cells, cells.shape[dim] - width, cells.shape[dim], axis=dim)
        cells = jnp.concatenate(
            [
                lax.ppermute(tail, axis, [(i, (i + 1) % count) for i in range(count)]),
                cells,
                lax.ppermute(head, axis, [((i + 1) % count, i) for i in range(count)]),
            ],
            axis=dim,
        )
    return cells


def modulate(token_rows, modulation):
    rows_wide = token_rows.astype(jnp.float32)
    row_mean = jnp.mean(rows_wide, axis=-1, keepdims=True)
    centred = rows_wide - row_mean
    spread = jnp.mean(centred * centred, axis=-1, keepdims=True)
    normed = centred * lax.rsqrt(spread + 1e-06)
    return ((1.0 + modulation[1]) * normed + modulation[0]).astype(jnp.bfloat16)


def head_norm(raw_proj, norm_gain, head_count):
    row_total = raw_proj.shape[0]
    split_heads = raw_proj.reshape(row_total, 3, head_count, norm_gain.shape[1])
    pair_heads = split_heads[:, :2]
    mean_square = jnp.mean(pair_heads * pair_heads, axis=-1, keepdims=True)
    pair_heads = pair_heads * lax.rsqrt(mean_square + 1e-06) * norm_gain[None, :, None, :]
    joined = jnp.concatenate([pair_heads, split_heads[:, 2:]], axis=1)
    return joined.reshape(row_total, 3, head_count * norm_gain.shape[1]).astype(jnp.bfloat16)


def shards(
    latents,
    modulation,
    qkv_weight,
    qkv_bias,
    norm_gain,
    out_weight,
    out_bias,
    key_tiles,
    key_count,
    strip_rows,
):
    groups = lax.axis_size("head")
    local_rows = latents.shape[0]
    window_rows = local_rows * groups
    features = qkv_weight.shape[0]
    local_width = qkv_weight.shape[2]
    head_dim = norm_gain.shape[1]
    local_heads = local_width // head_dim
    flat_weight = qkv_weight.reshape(features, 3 * local_width)
    raw_proj = jnp.dot(
        modulate(lax.all_gather(latents, "head", axis=0, tiled=True), modulation),
        flat_weight,
        preferred_element_type=jnp.float32,
    )
    raw_proj = raw_proj.reshape(-1, 3, local_width) + qkv_bias
    qkv_rows = head_norm(raw_proj, norm_gain, local_heads)
    kv_tiles = qkv_rows[:, 1:].reshape(TW, TILE, 2, local_width)
    per_window = key_tiles.shape[1] // NB
    wanted_all = (key_tiles[0] % TW).reshape(NB, per_window)
    blocks = [kv_tiles]
    for neighbour in range(NB):
        offset = (neighbour // 2 + 1) * (1 - 2 * (neighbour % 2))
        remote = passed_along(kv_tiles, "win", -offset)
        blocks.append(jnp.take(remote, wanted_all[neighbour], axis=0))
    all_kv = jnp.concatenate(blocks, axis=0).reshape(-1, 2, local_width)
    key_total = all_kv.shape[0]
    live_keys = jnp.arange(key_total, dtype=jnp.int32) // TILE < TW + key_count[0]
    key_heads = all_kv[:, 0].reshape(key_total, local_heads, head_dim)
    value_heads = all_kv[:, 1].reshape(key_total, local_heads, head_dim)

    def attend_block(query_rows):
        query_heads = query_rows.reshape(-1, local_heads, head_dim)
        scores = jnp.einsum(
            "qhd,khd->hqk", query_heads, key_heads, preferred_element_type=jnp.float32
        ) * head_dim ** (-0.5)
        weights = jnp.where(live_keys[None, None, :], jnp.exp(scores), jnp.float32(0.0))
        denominator = jnp.sum(weights, axis=-1)
        mixed = jnp.einsum(
            "hqk,khd->qhd",
            weights.astype(jnp.bfloat16),
            value_heads,
            preferred_element_type=jnp.float32,
        )
        return (
            (mixed / jnp.transpose(denominator)[:, :, None])
            .reshape(-1, local_width)
            .astype(jnp.bfloat16)
        )

    block_rows = min(512, window_rows)
    queries = qkv_rows[:, 0].reshape(window_rows // block_rows, block_rows, local_width)
    attended = lax.map(attend_block, queries).reshape(window_rows, local_width)
    edge_rows = jnp.concatenate([attended[:OV], attended[window_rows - OV :]], axis=0)
    edge_terms = jnp.dot(edge_rows, out_weight, preferred_element_type=jnp.float32)
    padded = with_halo(edge_terms, (("win", 0),), OV)
    prev_rim = padded[:OV]
    next_rim = padded[3 * OV :]
    window = lax.axis_index("win")
    window_count = strip_rows.shape[0]
    lead_rows = strip_rows[(window + window_count - 1) % window_count]
    tail_rows = strip_rows[window]
    filler = jnp.zeros((window_rows, features), jnp.float32)
    prev_padded = jnp.concatenate([prev_rim, filler], axis=0)
    next_padded = jnp.concatenate([filler, next_rim], axis=0)
    own_term = jnp.dot(attended, out_weight, preferred_element_type=jnp.float32)
    prev_part = lax.dynamic_slice_in_dim(
        prev_padded, OV - lead_rows, local_rows * lax.axis_size("head"), 0
    )
    next_part = lax.dynamic_slice_in_dim(
        next_padded, tail_rows, local_rows * lax.axis_size("head"), 0
    )
    row_place = jnp.arange(local_rows * lax.axis_size("head"), dtype=jnp.int32)
    in_top = (row_place < lead_rows)[:, None]
    in_bottom = (row_place >= window_rows - tail_rows)[:, None]
    blended_proj = lax.psum_scatter(
        jnp.where(
            in_top,
            (own_term + prev_part) * 0.5,
            jnp.where(in_bottom, (own_term + next_part) * 0.5, own_term),
        ),
        "head",
        scatter_dimension=0,
        tiled=True,
    )
    result = latents.astype(jnp.float32) + modulation[2] * (blended_proj + out_bias)
    return result.astype(jnp.bfloat16)


def solution(mesh):
    in_specs = (
        P(("win", "head"), None),
        P(),
        P(None, None, "head"),
        P(None, "head"),
        P(),
        P("head", None),
        P(),
        P("win", None),
        P("win"),
        P(),
    )
    out_specs = P(("win", "head"), None)
    return jax.shard_map(shards, mesh=mesh, in_specs=in_specs, out_specs=out_specs, check_vma=False)
```

profile of v0, /device:TPU:24, one launch (start us, length us, event | category | flops | bytes accessed | tf_op | source)
XLA Modules:
  0.0 355.1 jit_solution(5531110353625841328)
XLA Ops:
  7.3 10.3 %copy.40 = bf16[3072,3,384]{0,2,1:T(8,128)(2,1)} copy(bf16[3072,3,384]{2,0,1:T(8,128)(2,1)} %param.14) | data formatting | bytes 14155776 | tf_op args[2]
  19.1 22.0 %all-gather.2.cloned.1.call-done = bf16[512,3072]{1,0:T(8,128)(2,1)} async-done(((bf16[64,3072]{1,0:T(8,128)(2,1)}), bf16[512,3072]{1,0:T(8,128)(2,1)}) %all-gather.2.cloned.1.call-update) | async-done | bytes 3145744 | tf_op jit(solution)/shard_map/all_gather | solution.py:74
  41.1 2.5 convert_reduce_fusion
  44.9 6.7 %fusion.27 = f32[512,3,384]{0,2,1:T(8,128)S(1)} fusion(bf16[3072,3,384]{0,2,1:T(8,128)(2,1)} %copy.40, bf16[512,3072]{1,0:T(8,128)(2,1)S(1)} %copy-done.1, f32[3072]{0:T(1024)S(1)} %bitcast.60, f32[512]{0:T(512)S(1)} %add_rsqrt_fusion.1, f32[512]{0:T(512)S(1)} %broadcast_multiply_fusion, f32[3072]{0:T(1024)S(1)} %bitcast.61, f32[3,384]{1,0:T(4,128)S(1)} %copy-done.12), kind=kOutput, calls=%fused_computation.40 | convolution fusion | flops 3633905664 | bytes 12616192 | tf_op jit(solution)/shard_map/dot_general | solution.py:73
  56.7 5.4 %collective-permute-start = (bf16[4,128,2,384]{3,1,2,0:T(8,128)(2,1)}, bf16[4,128,2,384]{3,1,2,0:T(8,128)(2,1)S(1)}, u32[]{:S(2)}, u32[]{:S(2)}) collective-permute-start(bf16[4,128,2,384]{3,1,2,0:T(8,128)(2,1)} %copy.42), channel_id=1, source_target_pairs={{0,248},{8,0},{16,8},{24,16},{32,24},{40,32},{48,40},{56,48},{64,5... | collective-permute-start | bytes 2359304 | tf_op jit(solution)/shard_map/ppermute | solution.py:15
  63.4 2.8 collective-permute-start.2
  68.1 4.8 %collective-permute-start.4 = (bf16[4,128,2,384]{3,1,2,0:T(8,128)(2,1)}, bf16[4,128,2,384]{3,1,2,0:T(8,128)(2,1)}, u32[]{:S(2)}, u32[]{:S(2)}) collective-permute-start(bf16[4,128,2,384]{3,1,2,0:T(8,128)(2,1)} %copy.42), channel_id=1, source_target_pairs={{0,232},{8,240},{16,248},{24,0},{32,8},{40,16},{48,24},{56,32},{64... | collective-permute-start | bytes 2359304 | tf_op jit(solution)/shard_map/ppermute | solution.py:15
  75.6 22.7 %collective-permute-done = bf16[4,128,2,384]{3,1,2,0:T(8,128)(2,1)S(1)} collective-permute-done((bf16[4,128,2,384]{3,1,2,0:T(8,128)(2,1)}, bf16[4,128,2,384]{3,1,2,0:T(8,128)(2,1)S(1)}, u32[]{:S(2)}, u32[]{:S(2)}) %collective-permute-start) | collective-permute-done | bytes 786464 | tf_op jit(solution)/shard_map/ppermute | solution.py:15
  101.0 3.0 collective-permute-done.1
  104.0 6.0 %collective-permute-start.6 = (bf16[4,128,2,384]{3,1,2,0:T(8,128)(2,1)}, bf16[4,128,2,384]{3,1,2,0:T(8,128)(2,1)}, u32[]{:S(2)}, u32[]{:S(2)}) collective-permute-start(bf16[4,128,2,384]{3,1,2,0:T(8,128)(2,1)} %copy.42), channel_id=1, source_target_pairs={{0,224},{8,232},{16,240},{24,248},{32,0},{40,8},{48,16},{56,24},{6... | collective-permute-start | bytes 2359304 | tf_op jit(solution)/shard_map/ppermute | solution.py:15
  112.7 9.7 %collective-permute-done.2 = bf16[4,128,2,384]{3,1,2,0:T(8,128)(2,1)} collective-permute-done((bf16[4,128,2,384]{3,1,2,0:T(8,128)(2,1)}, bf16[4,128,2,384]{3,1,2,0:T(8,128)(2,1)}, u32[]{:S(2)}, u32[]{:S(2)}) %collective-permute-start.2) | collective-permute-done | bytes 786464 | tf_op jit(solution)/shard_map/ppermute | solution.py:15
  124.2 1.9 gather_fusion.3
  130.6 100.7 %collective-permute-done.4 = bf16[4,128,2,384]{3,1,2,0:T(8,128)(2,1)} collective-permute-done((bf16[4,128,2,384]{3,1,2,0:T(8,128)(2,1)}, bf16[4,128,2,384]{3,1,2,0:T(8,128)(2,1)}, u32[]{:S(2)}, u32[]{:S(2)}) %collective-permute-start.4) | collective-permute-done | bytes 786464 | tf_op jit(solution)/shard_map/ppermute | solution.py:15
  233.3 1.9 gather_fusion.5
  244.9 4.4 %fusion.53 = (bf16[2560,1,384]{2,0,1:T(8,128)(2,1)}, bf16[2560,1,384]{2,0,1:T(8,128)(2,1)}) fusion(bf16[2560,2,384]{2,0,1:T(8,128)(2,1)} %bitcast.47), kind=kLoop, calls=%fused_computation.113 | loop fusion | bytes 7864320 | tf_op jit(solution)/shard_map/slice | solution.py:91
  249.3 4.0 %copy.59 = bf16[2560,1,384]{0,2,1:T(8,128)(2,1)} copy(bf16[2560,1,384]{2,0,1:T(8,128)(2,1)} %get-tuple-element.40) | data formatting | bytes 3932160 | tf_op jit(solution)/shard_map/slice | solution.py:91
  253.3 4.0 %copy.58 = bf16[2560,1,384]{0,2,1:T(8,128)(2,1)} copy(bf16[2560,1,384]{2,0,1:T(8,128)(2,1)} %get-tuple-element.41) | data formatting | bytes 3932160 | tf_op jit(solution)/shard_map/slice | solution.py:92
  257.3 9.2 %fusion = (f32[3,512]{1,0:T(4,128)S(1)}, f32[3,512,2560]{2,1,0:T(8,128)}) fusion(pred[2560]{0:T(1024)(128)(4,1)S(1)} %copy-done.9, bf16[512,3,128]{0,2,1:T(8,128)(2,1)S(1)} %bitcast.55, bf16[2560,3,128]{0,2,1:T(8,128)(2,1)} %bitcast.54), kind=kOutput, calls=%fused_computation.9 | convolution fusion | flops 1018427904 | bytes 18096640 | tf_op jit(solution)/shard_map/while/body/eval_jaxpr/qhd,khd->hqk/dot_general | solution.py:96
  266.5 8.0 %fusion.38 = bf16[512,3,128]{0,2,1:T(8,128)(2,1)S(1)} fusion(bf16[2560,3,128]{0,2,1:T(8,128)(2,1)S(1)} %bitcast.53, f32[3,512,2560]{2,1,0:T(8,128)} %get-tuple-element.66, pred[2560]{0:T(1024)(128)(4,1)S(1)} %copy-done.9, f32[512,3]{0,1:T(4,128)S(1)} %bitcast.62), kind=kOutput, calls=%fused_computation.44 | convolution fusion | flops 1018822656 | bytes 18096640 | tf_op jit(solution)/shard_map/while/body/eval_jaxpr/hqk,khd->qhd/dot_general | solution.py:101
  276.4 5.3 %collective-permute-start.9 = (f32[64,3072]{1,0:T(8,128)S(1)}, f32[64,3072]{1,0:T(8,128)}, u32[]{:S(2)}, u32[]{:S(2)}) collective-permute-start(f32[64,3072]{1,0:T(8,128)S(1)} %get-tuple-element.42), channel_id=1, source_target_pairs={{8,0},{16,8},{24,16},{32,24},{40,32},{48,40},{56,48},{64,56},{72,6... | collective-permute-start | bytes 2359304 | tf_op jit(solution)/shard_map/ppermute | solution.py:27
  286.8 12.0 %collective-permute-done.8 = f32[64,3072]{1,0:T(8,128)} collective-permute-done((f32[64,3072]{1,0:T(8,128)}, f32[64,3072]{1,0:T(8,128)}, u32[]{:S(2)}, u32[]{:S(2)}) %collective-permute-start.8) | collective-permute-done | bytes 786464 | tf_op jit(solution)/shard_map/ppermute | solution.py:25
  299.5 5.9 %fusion.13 = f32[512,3072]{1,0:T(8,128)} fusion(s32[]{:T(128)S(6)} %select_n.58, f32[64,3072]{1,0:T(8,128)} %collective-permute-done.8, s32[]{:T(128)S(6)} %select_n.60, f32[64,3072]{1,0:T(8,128)} %collective-permute-done.9, pred[512]{0:T(512)(128)(4,1)S(1)} %get-tuple-element.67, pred[512]{0:T(512)(128)(4,1)S(1)} %get-tuple-element.68, ...), kind=kOutput, calls=%fused_computation.25 | convolution fusion | flops 1217396736 | bytes 10617864 | tf_op jit(solution)/shard_map/dot_general | solution.py:128
  305.4 40.9 %reduce-scatter.2.cloned.1.call-done = f32[64,3072]{1,0:T(8,128)} async-done(((f32[512,3072]{1,0:T(8,128)}), f32[64,3072]{1,0:T(8,128)}) %reduce-scatter.2.cloned.1.call-update) | async-done | bytes 786448 | tf_op jit(solution)/shard_map/reduce_scatter | solution.py:138
  346.3 2.0 add_convert_fusion
  (86 shorter events, 40.6 us)
Async XLA Ops:
  6.5 268.1 %copy-start = (bf16[384,3072]{1,0:T(8,128)(2,1)S(1)}, bf16[384,3072]{1,0:T(8,128)(2,1)}, u32[]{:S(2)}) copy-start(bf16[384,3072]{1,0:T(8,128)(2,1)} %param.17) | copy-start | bytes 7077892
  6.5 34.6 %all-gather.2.cloned.1.call-start = ((), (), s32[]{:S(2)}) async-start(), calls=%async_computation.1 | async-start | bytes 3538944 | tf_op jit(solution)/shard_map/all_gather | solution.py:74
  7.3 11.0 %copy-start.13 = (s32[1,16]{1,0:T(1,128)S(1)}, s32[1,16]{1,0:T(1,128)}, u32[]{:S(2)}) copy-start(s32[1,16]{1,0:T(1,128)} %param.19) | copy-start | bytes 196
  7.3 11.8 %copy-start.7 = (f32[3,3072]{1,0:T(4,128)S(1)}, f32[3,3072]{1,0:T(4,128)}, u32[]{:S(2)}) copy-start(f32[3,3072]{1,0:T(4,128)} %param.13) | copy-start | bytes 110596
  7.3 339.0 %reduce-scatter.2.cloned.1.call-start = ((), (), s32[]{:S(2)}) async-start(), calls=%async_computation.2 | async-start | bytes 7077888 | tf_op jit(solution)/shard_map/reduce_scatter | solution.py:138
  17.6 27.3 %copy-start.12 = (f32[3,384]{1,0:T(4,128)S(1)}, f32[3,384]{1,0:T(4,128)}, u32[]{:S(2)}) copy-start(f32[3,384]{1,0:T(4,128)} %param.15) | copy-start | bytes 13828
  41.1 2.8 copy-start.1
  44.9 7.1 %copy-start.11 = (f32[2,128]{1,0:T(2,128)S(1)}, f32[2,128]{1,0:T(2,128)}, u32[]{:S(2)}) copy-start(f32[2,128]{1,0:T(2,128)} %param.16) | copy-start | bytes 3076
  56.7 41.6 %collective-permute-start = (bf16[4,128,2,384]{3,1,2,0:T(8,128)(2,1)}, bf16[4,128,2,384]{3,1,2,0:T(8,128)(2,1)S(1)}, u32[]{:S(2)}, u32[]{:S(2)}) collective-permute-start(bf16[4,128,2,384]{3,1,2,0:T(8,128)(2,1)} %copy.42), channel_id=1, source_target_pairs={{0,248},{8,0},{16,8},{24,16},{32,24},{40,32},{48,40},{56,48},{64,5... | collective-permute-start | bytes 2359304 | tf_op jit(solution)/shard_map/ppermute | solution.py:15
  62.2 41.8 %collective-permute-start.1 = (bf16[4,128,2,384]{3,1,2,0:T(8,128)(2,1)}, bf16[4,128,2,384]{3,1,2,0:T(8,128)(2,1)}, u32[]{:S(2)}, u32[]{:S(2)}) collective-permute-start(bf16[4,128,2,384]{3,1,2,0:T(8,128)(2,1)} %copy.42), channel_id=1, source_target_pairs={{0,8},{8,16},{16,24},{24,32},{32,40},{40,48},{48,56},{56,64},{64,7... | collective-permute-start | bytes 2359304 | tf_op jit(solution)/shard_map/ppermute | solution.py:15
  63.4 59.1 %collective-permute-start.2 = (bf16[4,128,2,384]{3,1,2,0:T(8,128)(2,1)}, bf16[4,128,2,384]{3,1,2,0:T(8,128)(2,1)}, u32[]{:S(2)}, u32[]{:S(2)}) collective-permute-start(bf16[4,128,2,384]{3,1,2,0:T(8,128)(2,1)} %copy.42), channel_id=1, source_target_pairs={{0,240},{8,248},{16,0},{24,8},{32,16},{40,24},{48,32},{56,40},{64,... | collective-permute-start | bytes 2359304 | tf_op jit(solution)/shard_map/ppermute | solution.py:15
  66.2 58.0 %collective-permute-start.3 = (bf16[4,128,2,384]{3,1,2,0:T(8,128)(2,1)}, bf16[4,128,2,384]{3,1,2,0:T(8,128)(2,1)}, u32[]{:S(2)}, u32[]{:S(2)}) collective-permute-start(bf16[4,128,2,384]{3,1,2,0:T(8,128)(2,1)} %copy.42), channel_id=1, source_target_pairs={{0,16},{8,24},{16,32},{24,40},{32,48},{40,56},{48,64},{56,72},{64,... | collective-permute-start | bytes 2359304 | tf_op jit(solution)/shard_map/ppermute | solution.py:15
  68.1 163.3 %collective-permute-start.4 = (bf16[4,128,2,384]{3,1,2,0:T(8,128)(2,1)}, bf16[4,128,2,384]{3,1,2,0:T(8,128)(2,1)}, u32[]{:S(2)}, u32[]{:S(2)}) collective-permute-start(bf16[4,128,2,384]{3,1,2,0:T(8,128)(2,1)} %copy.42), channel_id=1, source_target_pairs={{0,232},{8,240},{16,248},{24,0},{32,8},{40,16},{48,24},{56,32},{64... | collective-permute-start | bytes 2359304 | tf_op jit(solution)/shard_map/ppermute | solution.py:15
  99.2 134.1 %collective-permute-start.5 = (bf16[4,128,2,384]{3,1,2,0:T(8,128)(2,1)}, bf16[4,128,2,384]{3,1,2,0:T(8,128)(2,1)}, u32[]{:S(2)}, u32[]{:S(2)}) collective-permute-start(bf16[4,128,2,384]{3,1,2,0:T(8,128)(2,1)} %copy.42), channel_id=1, source_target_pairs={{0,24},{8,32},{16,40},{24,48},{32,56},{40,64},{48,72},{56,80},{64,... | collective-permute-start | bytes 2359304 | tf_op jit(solution)/shard_map/ppermute | solution.py:15
  104.0 131.2 %collective-permute-start.6 = (bf16[4,128,2,384]{3,1,2,0:T(8,128)(2,1)}, bf16[4,128,2,384]{3,1,2,0:T(8,128)(2,1)}, u32[]{:S(2)}, u32[]{:S(2)}) collective-permute-start(bf16[4,128,2,384]{3,1,2,0:T(8,128)(2,1)} %copy.42), channel_id=1, source_target_pairs={{0,224},{8,232},{16,240},{24,248},{32,0},{40,8},{48,16},{56,24},{6... | collective-permute-start | bytes 2359304 | tf_op jit(solution)/shard_map/ppermute | solution.py:15
  122.5 119.1 %collective-permute-start.7 = (bf16[4,128,2,384]{3,1,2,0:T(8,128)(2,1)}, bf16[4,128,2,384]{3,1,2,0:T(8,128)(2,1)}, u32[]{:S(2)}, u32[]{:S(2)}) collective-permute-start(bf16[4,128,2,384]{3,1,2,0:T(8,128)(2,1)} %copy.42), channel_id=1, source_target_pairs={{0,32},{8,40},{16,48},{24,56},{32,64},{40,72},{48,80},{56,88},{64,... | collective-permute-start | bytes 2359304 | tf_op jit(solution)/shard_map/ppermute | solution.py:15
  249.3 8.0 %copy-start.5 = (bf16[512,1,384]{0,2,1:T(8,128)(2,1)S(1)}, bf16[512,1,384]{0,2,1:T(8,128)(2,1)}, u32[]{:S(2)}) copy-start(bf16[512,1,384]{0,2,1:T(8,128)(2,1)} %slice.121) | copy-start | bytes 1179652
  249.3 8.0 %copy-start.9 = (pred[2560]{0:T(1024)(128)(4,1)S(1)}, pred[2560]{0:T(1024)(128)(4,1)}, u32[]{:S(2)}) copy-start(pred[2560]{0:T(1024)(128)(4,1)} %fusion.45) | copy-start | bytes 7684
  257.3 9.2 %copy-start.3 = (bf16[2560,1,384]{0,2,1:T(8,128)(2,1)S(1)}, bf16[2560,1,384]{0,2,1:T(8,128)(2,1)}, u32[]{:S(2)}) copy-start(bf16[2560,1,384]{0,2,1:T(8,128)(2,1)} %copy.58) | copy-start | bytes 5898244
  274.5 7.2 %copy-start.10 = (s32[32]{0:T(128)S(1)}, s32[32]{0:T(128)}, u32[]{:S(2)}) copy-start(s32[32]{0:T(128)} %param.21) | copy-start | bytes 388
  276.4 22.5 %collective-permute-start.8 = (f32[64,3072]{1,0:T(8,128)}, f32[64,3072]{1,0:T(8,128)}, u32[]{:S(2)}, u32[]{:S(2)}) collective-permute-start(f32[64,3072]{1,0:T(8,128)} %get-tuple-element.43), channel_id=1, source_target_pairs={{0,8},{8,16},{16,24},{24,32},{32,40},{40,48},{48,56},{56,64},{64,7... | collective-permute-start | bytes 2359304 | tf_op jit(solution)/shard_map/ppermute | solution.py:25
  276.4 23.2 %collective-permute-start.9 = (f32[64,3072]{1,0:T(8,128)S(1)}, f32[64,3072]{1,0:T(8,128)}, u32[]{:S(2)}, u32[]{:S(2)}) collective-permute-start(f32[64,3072]{1,0:T(8,128)S(1)} %get-tuple-element.42), channel_id=1, source_target_pairs={{8,0},{16,8},{24,16},{32,24},{40,32},{48,40},{56,48},{64,56},{72,6... | collective-permute-start | bytes 2359304 | tf_op jit(solution)/shard_map/ppermute | solution.py:27
  305.4 40.9 %copy-start.4 = (bf16[64,3072]{1,0:T(8,128)(2,1)S(1)}, bf16[64,3072]{1,0:T(8,128)(2,1)}, u32[]{:S(2)}) copy-start(bf16[64,3072]{1,0:T(8,128)(2,1)} %param.12) | copy-start | bytes 1179652
  305.4 40.9 %copy-start.8 = (f32[3072]{0:T(1024)S(1)}, f32[3072]{0:T(1024)}, u32[]{:S(2)}) copy-start(f32[3072]{0:T(1024)} %param.18) | copy-start | bytes 36868
  (2 other events, 1.9 us)
Sparse Core Ops, SparseCore 0:
  9.2 31.8 all-gather.1
  305.6 40.6 reduce-scatter.1
where the time goes:
time: 359 us; the launch traced here: 355 us
  waiting for transfers between devices  213 us (59%)
  local copies, waits for them, and re-layouts  47.6 us (13%)
  matrix products  30.5 us (8%)
  starting transfers between devices  24.6 us (7%)
  other arithmetic  21.8 us (6%)
  between operations  18.2 us (5%)
    ppermute x8, waiting for transfers between devices, passed_along(): return lax.ppermute(value, axis, pairs)  136 us
    reduce_scatter x1, waiting for transfers between devices, shards(): lax.psum_scatter(jnp.where(in_top, (own_term + prev_part) * 0.5, jnp.wher...  40.9 us
    all_gather x1, waiting for transfers between devices, shards(): lax.all_gather(latents, 'head', axis=0, tiled=True)  22 us
    ppermute x8, starting transfers between devices, passed_along(): return lax.ppermute(value, axis, pairs)  19.2 us
    gather x8, local copies, waits for them, and re-layouts, shards(): blocks.append(jnp.take(remote, wanted_all[neighbour], axis=0))  14.6 us
    unnamed x30, local copies, waits for them, and re-layouts  13.5 us
    ppermute x1, waiting for transfers between devices, with_halo(): lax.ppermute(tail, axis, [(i, (i + 1) % count) for i in range(count)])  12 us
    unnamed x7, other arithmetic  9.85 us
  transfers between devices with their start and end apart: 12, of which 8 were waited for; matrix products, arithmetic and copies ran while one was open for 11% of the time, Pallas kernels for 0%

commit v1 on v0

v1 whole, which is shorter than its diff:
```python
import functools
import math

import jax
import jax.numpy as jnp
from jax import lax
from jax.experimental import pallas as pl
from jax.experimental.pallas import tpu as pltpu
from jax.sharding import PartitionSpec as P

TILE = 128
TW = 4
NB = 8
OV = 64
ROWS = 64
D = 3072
HD = 128
HEADS = 3
LW = HEADS * HD
WINDOWS = 32
GROUPS = 8
MIB = 1 << 20
SMEM = functools.partial(pl.BlockSpec, memory_space=pltpu.SMEM)
VMEM = functools.partial(pl.BlockSpec, memory_space=pltpu.VMEM)


def along_win(value, steps):
    return lax.ppermute(value, "win", [(i, (i + steps) % WINDOWS) for i in range(WINDOWS)])


def to_y(value, steps):
    return lax.ppermute(value, "head", [(h, ((h // 2 + steps) % 4) * 2 + h % 2) for h in range(GROUPS)])


def swap_core(value):
    return lax.ppermute(value, "head", [(h, h ^ 1) for h in range(GROUPS)])


def strip_pairs(bottom_core):
    pairs = []
    for w in range(WINDOWS):
        for h in range(GROUPS):
            y, c = h // 2, h % 2
            if c == bottom_core:
                pairs.append((w * GROUPS + h, (w + 1) % WINDOWS * GROUPS + 2 * y))
            else:
                pairs.append((w * GROUPS + h, (w - 1) % WINDOWS * GROUPS + 2 * y + 1))
    return pairs


def project_kernel(parts, *refs):
    lat = refs[:parts]
    modulation, weight, bias, gain, kv_ref, q_ref, mod_ref = refs[parts:]
    step = pl.program_id(0)

    @pl.when(step == 0)
    def _():
        for i in range(parts):

            def body(g, carry, i=i):
                rows = pl.ds(pl.multiple_of(g * 16, 16), 16)
                wide = lat[i][rows, :].astype(jnp.float32)
                mean = jnp.sum(wide, axis=-1, keepdims=True) * (1.0 / D)
                centred = wide - mean
                spread = jnp.sum(centred * centred, axis=-1, keepdims=True) * (1.0 / D)
                normed = centred * lax.rsqrt(spread + 1e-06)
                out = (1.0 + modulation[1:2, :]) * normed + modulation[0:1, :]
                mod_ref[pl.ds(pl.multiple_of(i * ROWS + g * 16, 16), 16), :] = out.astype(jnp.bfloat16)
                return carry

            lax.fori_loop(0, ROWS // 16, body, 0)

    raw = jnp.dot(mod_ref[...], weight[0], preferred_element_type=jnp.float32)

    def normed_heads(raw, which):
        out = []
        for h in range(HEADS):
            part = raw[:, h * HD : (h + 1) * HD]
            mean_square = jnp.sum(part * part, axis=-1, keepdims=True) * (1.0 / HD)
            out.append((part * lax.rsqrt(mean_square + 1e-06) * gain[which : which + 1, :]).astype(jnp.bfloat16))
        return out

    @pl.when(step == 0)
    def _():
        for h, part in enumerate(normed_heads(raw + bias[1:2, :], 1)):
            kv_ref[:, h * HD : (h + 1) * HD] = part

    @pl.when(step == 1)
    def _():
        kv_ref[:, LW:] = (raw + bias[2:3, :]).astype(jnp.bfloat16)

    @pl.when(step == 2)
    def _():
        for h, part in enumerate(normed_heads(raw + bias[0:1, :], 0)):
            q_ref[:, h * HD : (h + 1) * HD] = part


def project(lat, modulation, weight, bias, gain):
    parts = len(lat)
    rows = parts * ROWS
    whole = lambda shape: pl.BlockSpec(shape, lambda c: (0,) * len(shape))
    return pl.pallas_call(
        functools.partial(project_kernel, parts),
        grid=(3,),
        in_specs=[whole((ROWS, D))] * parts
        + [
            whole((3, D)),
            pl.BlockSpec((1, D, LW), lambda c: ((c + 1) % 3, 0, 0)),
            whole((3, LW)),
            whole((2, HD)),
        ],
        out_specs=[whole((rows, 2 * LW)), whole((rows, LW))],
        out_shape=[
            jax.ShapeDtypeStruct((rows, 2 * LW), jnp.bfloat16),
            jax.ShapeDtypeStruct((rows, LW), jnp.bfloat16),
        ],
        scratch_shapes=[pltpu.VMEM((rows, D), jnp.bfloat16)],
        compiler_params=pltpu.CompilerParams(vmem_limit_bytes=24 * MIB),
        cost_estimate=pl.CostEstimate(
            flops=2 * rows * D * 3 * LW, bytes_accessed=3 * D * LW * 2 + rows * D * 2, transcendentals=0
        ),
        name="project",
    )(*lat, modulation, weight, bias, gain)


def pick_tile(dst, row, chunks, place):
    a, b, c = chunks

    @pl.when(place == 0)
    def _():
        dst[row : row + TILE, :] = a[...]

    @pl.when(jnp.logical_or(place == 1, place == 2))
    def _():
        dst[row : row + TILE, :] = b[pl.ds(pl.multiple_of((place - 1) * TILE, TILE), TILE), :]

    @pl.when(place == 3)
    def _():
        dst[row : row + TILE, :] = c[...]


def select_kernel(place, a, b, c, out):
    for k in range(2):
        pick_tile(out, k * TILE, (a, b, c), place[k])


def select_tiles(place, chunks):
    return pl.pallas_call(
        select_kernel,
        in_specs=[SMEM()] + [VMEM()] * 3,
        out_specs=VMEM(),
        out_shape=jax.ShapeDtypeStruct((2 * TILE, 2 * LW), jnp.bfloat16),
        cost_estimate=pl.CostEstimate(flops=0, bytes_accessed=1 * MIB, transcendentals=0),
        name="select_tiles",
    )(place, *chunks)


def accumulate(kv, q_block, live, num, den, first):
    scale = HD**-0.5 * math.log2(math.e)
    for h in range(HEADS):
        cols = slice(h * HD, (h + 1) * HD)
        scores = lax.dot_general(
            q_block(cols), kv[:, cols], (((1,), (1,)), ((), ())), preferred_element_type=jnp.float32
        )
        weights = jnp.exp2(scores * scale)
        parts = []
        for t in range(weights.shape[1] // TILE):
            w = weights[:, t * TILE : (t + 1) * TILE]
            if live is not None:
                w = jnp.where(live(t), w, 0.0)
            parts.append(w)
        total = functools.reduce(jnp.add, parts)
        rounded = jnp.concatenate([w.astype(jnp.bfloat16) for w in parts], axis=1)
        mixed = jnp.dot(rounded, kv[:, LW + h * HD : LW + (h + 1) * HD], preferred_element_type=jnp.float32)
        if first:
            num[0][:, cols] = mixed
            den[0][:, cols] = total
        else:
            num[0][:, cols] = num[1][:, cols] + mixed
            den[0][:, cols] = den[1][:, cols] + total


QB = 256


def own_kernel(q, a, b, c, num, den, kbuf):
    @pl.when(pl.program_id(0) == 0)
    def _():
        kbuf[0:TILE, :] = a[...]
        kbuf[TILE : 3 * TILE, :] = b[...]
        kbuf[3 * TILE :, :] = c[...]

    accumulate(kbuf, lambda cols: q[:, cols], None, (num,), (den,), True)


def hop_kernel(base, place, count, q, la, lb, lc, ra, rb, rc, num_in, den_in, num, den, kbuf):
    @pl.when(pl.program_id(0) == 0)
    def _():
        for k in range(2):
            pick_tile(kbuf, k * TILE, (la, lb, lc), place[base + k])
            pick_tile(kbuf, (2 + k) * TILE, (ra, rb, rc), place[base + 2 + k])

    live = lambda t: base + t < count[0]
    accumulate(kbuf, lambda cols: q[:, cols], live, (num, num_in), (den, den_in), False)


def rows_spec(width):
    return pl.BlockSpec((QB, width), lambda i: (i, 0))


def whole_spec(shape):
    return pl.BlockSpec(shape, lambda i: (0,) * len(shape))


ATT_COST = pl.CostEstimate(flops=4 * 512 * 512 * LW, bytes_accessed=5 * MIB, transcendentals=512 * 512 * HEADS)
ACC = [jax.ShapeDtypeStruct((512, LW), jnp.float32)] * 2
KBUF = [pltpu.VMEM((4 * TILE, 2 * LW), jnp.bfloat16)]
CHUNK_SPECS = [whole_spec((n, 2 * LW)) for n in (TILE, 2 * TILE, TILE)]


def attend_own(q, chunks):
    return pl.pallas_call(
        own_kernel,
        grid=(512 // QB,),
        in_specs=[rows_spec(LW)] + CHUNK_SPECS,
        out_specs=[rows_spec(LW)] * 2,
        out_shape=ACC,
        scratch_shapes=KBUF,
        compiler_params=pltpu.CompilerParams(vmem_limit_bytes=24 * MIB),
        cost_estimate=ATT_COST,
        name="attend_own",
    )(q, *chunks)


def attend_hop(hop, place, count, q, left, right, num, den):
    return pl.pallas_call(
        functools.partial(hop_kernel, 4 * (hop - 1)),
        grid=(512 // QB,),
        in_specs=[SMEM(), SMEM(), rows_spec(LW)] + CHUNK_SPECS * 2 + [rows_spec(LW)] * 2,
        out_specs=[rows_spec(LW)] * 2,
        out_shape=ACC,
        scratch_shapes=KBUF,
        compiler_params=pltpu.CompilerParams(vmem_limit_bytes=24 * MIB),
        cost_estimate=ATT_COST,
        name="attend_hop",
    )(place, count, q, *left, *right, num, den)


def last_kernel(base, strip, count, q, left, right, num_in, den_in, own, sib, edge_a, edge_b, kbuf, num, den):
    kbuf[0 : 2 * TILE, :] = left[...]
    kbuf[2 * TILE :, :] = right[...]
    live = lambda t: base + t < count[0]
    for half in range(512 // QB):
        rows = slice(half * QB, (half + 1) * QB)
        accumulate(
            kbuf,
            lambda cols: q[rows, cols],
            live,
            (num, num_in.at[rows, :]),
            (den, den_in.at[rows, :]),
            False,
        )
        for h in range(HEADS):
            cols = slice(h * HD, (h + 1) * HD)
            total = jnp.sum(den[:, cols], axis=-1, keepdims=True)
            out = (num[:, cols] / total).astype(jnp.bfloat16)
            for t in range(QB // TILE):
                at = (half * (QB // TILE) + t) * ROWS
                own[at : at + ROWS, cols] = out[t * TILE : t * TILE + ROWS]
                sib[at : at + ROWS, cols] = out[t * TILE + ROWS : (t + 1) * TILE]
    edge_a[...] = sib[pl.ds(pl.multiple_of(strip[0] * ROWS, ROWS), ROWS), :]
    edge_b[...] = own[pl.ds(pl.multiple_of(strip[1] * ROWS, ROWS), ROWS), :]


def attend_last(strip, count, q, left, right, num, den):
    half = jax.ShapeDtypeStruct((256, LW), jnp.bfloat16)
    edge = jax.ShapeDtypeStruct((ROWS, LW), jnp.bfloat16)
    return pl.pallas_call(
        functools.partial(last_kernel, 12),
        in_specs=[SMEM()] * 2 + [VMEM()] * 5,
        out_specs=[VMEM()] * 4,
        out_shape=[half, half, edge, edge],
        scratch_shapes=KBUF + [pltpu.VMEM((QB, LW), jnp.float32)] * 2,
        compiler_params=pltpu.CompilerParams(vmem_limit_bytes=24 * MIB),
        cost_estimate=ATT_COST,
        name="attend_last",
    )(strip, count, q, left, right, num, den)


NCOL = 768


def out_kernel(strip, own, sib, edge_own, edge_sib, w_own, w_sib, o0, o1, o3, o2, a_own, a_sib, e_own, e_sib):
    place, shared, top = strip[1], strip[2], strip[3]

    @pl.when(pl.program_id(0) == 0)
    def _():
        a_own[...] = own[...]
        a_sib[...] = sib[...]
        row = lax.broadcasted_iota(jnp.int32, (ROWS, 1), 0)
        low = jnp.where(top == 1, 0, OV - shared)
        keep = jnp.where(jnp.logical_and(row >= low, row < low + shared), 0.5, 1.0)
        at = pl.ds(pl.multiple_of(place * ROWS, ROWS), ROWS)
        a_own[at, :] = (own[at, :].astype(jnp.float32) * keep).astype(jnp.bfloat16)
        a_sib[at, :] = (sib[at, :].astype(jnp.float32) * keep).astype(jnp.bfloat16)
        i = lax.broadcasted_iota(jnp.int32, (ROWS, ROWS), 0)
        j = lax.broadcasted_iota(jnp.int32, (ROWS, ROWS), 1)
        offset = jnp.where(top == 1, OV - shared, shared - OV)
        shift = jnp.where(j == i + offset, 0.5, 0.0).astype(jnp.bfloat16)
        e_own[...] = jnp.dot(shift, edge_own[...], preferred_element_type=jnp.float32).astype(jnp.bfloat16)
        e_sib[...] = jnp.dot(shift, edge_sib[...], preferred_element_type=jnp.float32).astype(jnp.bfloat16)

    dot = functools.partial(jnp.dot, preferred_element_type=jnp.float32)
    main = dot(a_own[...], w_own[...]) + dot(a_sib[...], w_sib[...])
    extra = dot(e_own[...], w_own[...]) + dot(e_sib[...], w_sib[...])
    for k, ref in enumerate((o0, o1, o3, o2)):
        block = main[k * ROWS : (k + 1) * ROWS]
        ref[...] = (block + jnp.where(place == k, extra, 0.0)).astype(ref.dtype)


def out_project(strip, own, sib, edge_own, edge_sib, w_own, w_sib):
    cols = lambda rows: pl.BlockSpec((rows, NCOL), lambda i: (0, i))
    sent = jax.ShapeDtypeStruct((ROWS, D), jnp.bfloat16)
    return pl.pallas_call(
        out_kernel,
        grid=(D // NCOL,),
        in_specs=[SMEM()]
        + [whole_spec((256, LW))] * 2
        + [whole_spec((ROWS, LW))] * 2
        + [cols(LW)] * 2,
        out_specs=[cols(ROWS)] * 4,
        out_shape=[jax.ShapeDtypeStruct((ROWS, D), jnp.float32), sent, sent, sent],
        scratch_shapes=[pltpu.VMEM((256, LW), jnp.bfloat16)] * 2 + [pltpu.VMEM((ROWS, LW), jnp.bfloat16)] * 2,
        compiler_params=pltpu.CompilerParams(vmem_limit_bytes=24 * MIB),
        cost_estimate=pl.CostEstimate(flops=2 * 320 * 2 * LW * D, bytes_accessed=7 * MIB, transcendentals=0),
        name="out_project",
    )(strip, own, sib, edge_own, edge_sib, w_own, w_sib)


def shards(
    latents,
    modulation,
    qkv_weight,
    qkv_bias,
    norm_gain,
    out_weight,
    out_bias,
    key_tiles,
    key_count,
    strip_rows,
):
    head = lax.axis_index("head")
    y, core = head // 2, head % 2
    window = lax.axis_index("win")
    weight = jnp.transpose(qkv_weight, (1, 0, 2))
    args = (modulation, weight, qkv_bias, norm_gain)
    order = jnp.array([0, 1, 3, 2], jnp.int32)

    def places(tiles):
        return order[(tiles % TW - y) % 4]

    lat1, lat3 = to_y(latents, -1), to_y(latents, 1)
    lat2 = to_y(latents, 2)
    kv_a, q_a = project([latents, swap_core(latents)], *args)
    kv_b, q_b = project([lat1, swap_core(lat1), lat3, swap_core(lat3)], *args)
    kv_c, q_c = project([lat2, swap_core(lat2)], *args)
    q = jnp.concatenate([q_a, q_b, q_c], axis=0)

    place = places(key_tiles[0])
    tiles_next, tiles_prev = along_win(key_tiles, -1), along_win(key_tiles, 1)
    w_sib = swap_core(out_weight)

    right = left = (kv_a, kv_b, kv_c)
    num, den = attend_own(q, right)
    for hop in range(1, 4):
        right = tuple(along_win(chunk, 1) for chunk in right)
        left = tuple(along_win(chunk, -1) for chunk in left)
        num, den = attend_hop(hop, place, key_count, q, left, right, num, den)
    last_left = along_win(select_tiles(places(tiles_prev[0, 12:14]), left), -1)
    last_right = along_win(select_tiles(places(tiles_next[0, 14:16]), right), 1)

    shared = jnp.where(core == 0, strip_rows[(window + WINDOWS - 1) % WINDOWS], strip_rows[window])
    strip = jnp.stack(
        [
            order[(jnp.where(core == 0, 3, 0) - y) % 4],
            order[(jnp.where(core == 1, 3, 0) - y) % 4],
            shared,
            (core == 0).astype(jnp.int32),
        ]
    )
    own, sib, edge_a, edge_b = attend_last(strip, key_count, q, last_left, last_right, num, den)
    edge_own = lax.ppermute(edge_a, ("win", "head"), strip_pairs(0))
    edge_sib = lax.ppermute(edge_b, ("win", "head"), strip_pairs(1))
    sib = swap_core(sib)
    o0, o1, o3, o2 = out_project(strip, own, sib, edge_own, edge_sib, out_weight, w_sib)
    total = o0
    for part in (to_y(o1, 1), to_y(o3, -1), to_y(o2, 2)):
        total = total + part.astype(jnp.float32)
    result = latents.astype(jnp.float32) + modulation[2] * (total + out_bias)
    return result.astype(jnp.bfloat16)


def solution(mesh):
    in_specs = (
        P(("win", "head"), None),
        P(),
        P(None, None, "head"),
        P(None, "head"),
        P(),
        P("head", None),
        P(),
        P("win", None),
        P("win"),
        P(),
    )
    out_specs = P(("win", "head"), None)
    return jax.shard_map(shards, mesh=mesh, in_specs=in_specs, out_specs=out_specs, check_vma=False)
```

time: 359 us -> 177 us (0.49)
  waiting for transfers between devices: 213 us -> 61.5 us
  Pallas kernels: 0 us -> 38.4 us
  matrix products: 30.5 us -> 0 us
  local copies, waits for them, and re-layouts: 47.6 us -> 19.7 us
  starting transfers between devices: 24.6 us -> 52 us
  other arithmetic: 21.8 us -> 2.51 us
  between operations: 18.2 us -> 2.49 us
    ppermute x10 -> x36, waiting for transfers between devices: 149 us -> 61.5 us  [the longest x6 32.6 us: to_y(): lax.ppermute(value, 'head', [(h, (h // 2 + steps) % 4 * 2 + h % 2) for h...]
    reduce_scatter x1 -> x0, waiting for transfers between devices: 40.9 us -> none  [shards(): lax.psum_scatter(jnp.where(in_top, (own_term + prev_part) * 0.5, jnp.wher...]
    pallas_call x0 -> x11, Pallas kernels: none -> 38.4 us  [the longest x3 16.7 us: project(): pl.pallas_call(functools.partial(project_kernel, parts), grid=(3,), in_sp...]
    dot_general x5 -> x0, matrix products: 30.5 us -> none  [the longest x1 9.18 us: attend_block(): jnp.einsum('qhd,khd->hqk', query_heads, key_heads, preferred_element_type...]
    ppermute x10 -> x36, starting transfers between devices: 24.5 us -> 52 us  [the longest x22 42.7 us: along_win(): lax.ppermute(value, 'win', [(i, (i + steps) % WINDOWS) for i in range(WIN...]
    all_gather x1 -> x0, waiting for transfers between devices: 22 us -> none  [shards(): lax.all_gather(latents, 'head', axis=0, tiled=True)]
    slice x9 -> x1, local copies, waits for them, and re-layouts: 17.8 us -> 0.02 us  [shards(): result = latents.astype(jnp.float32) + modulation[2] * (total + out_bias)]
    gather x8 -> x3, local copies, waits for them, and re-layouts: 14.6 us -> 3.01 us  [places(): return order[(tiles % TW - y) % 4]]
  transfers between devices with their start and end apart: 12 -> 36, of which waited for: 8 -> 8; matrix products, arithmetic and copies ran while one was open for 11% -> 4% of each run, Pallas kernels for 0% -> 19%
where the time goes in v1:
time: 177 us
  waiting for transfers between devices  61.5 us (35%)
  starting transfers between devices  52 us (29%)
  Pallas kernels  38.4 us (22%)
  local copies, waits for them, and re-layouts  19.7 us (11%)
  other arithmetic  2.51 us (1%)
  between operations  2.49 us (1%)
    ppermute x22, starting transfers between devices, along_win(): lax.ppermute(value, 'win', [(i, (i + steps) % WINDOWS) for i in range(WIN...  42.7 us
    ppermute x6, waiting for transfers between devices, to_y(): lax.ppermute(value, 'head', [(h, (h // 2 + steps) % 4 * 2 + h % 2) for h...  32.6 us
    ppermute x22, waiting for transfers between devices, along_win(): lax.ppermute(value, 'win', [(i, (i + steps) % WINDOWS) for i in range(WIN...  21.6 us
    pallas_call x3, Pallas kernels, project(): pl.pallas_call(functools.partial(project_kernel, parts), grid=(3,), in_sp...  16.7 us
    unnamed x88, local copies, waits for them, and re-layouts  14.5 us
    ppermute x6, starting transfers between devices, to_y(): lax.ppermute(value, 'head', [(h, (h // 2 + steps) % 4 * 2 + h % 2) for h...  7.94 us
    pallas_call x3, Pallas kernels, attend_hop(): pl.pallas_call(functools.partial(hop_kernel, 4 * (hop - 1)), grid=(512 //...  7.86 us
    ppermute x1, waiting for transfers between devices, shards(): edge_own = lax.ppermute(edge_a, ('win', 'head'), strip_pairs(0))  7.3 us
  transfers between devices with their start and end apart: 36, of which 8 were waited for; matrix products, arithmetic and copies ran while one was open for 4% of the time, Pallas kernels for 19%

profile of v1, /device:TPU:24, one launch (start us, length us, event | category | flops | bytes accessed | tf_op | source)
XLA Modules:
  0.0 176.6 jit_solution(7583740591179277187)
XLA Ops:
  0.7 2.5 %collective-permute-start.3 = (bf16[64,3072]{1,0:T(8,128)(2,1)}, bf16[64,3072]{1,0:T(8,128)(2,1)S(1)}, u32[]{:S(2)}, u32[]{:S(2)}) collective-permute-start(bf16[64,3072]{1,0:T(8,128)(2,1)} %refs_0_.1), channel_id=1, source_target_pairs={{0,2},{1,3},{2,4},{3,5},{4,6},{5,7},{6,0},{7,1},{8,10},{9,11},{10,... | collective-permute-start | bytes 1179656 | tf_op jit(solution)/shard_map/ppermute | solution.py:32
  3.4 17.3 %collective-permute-done.1.refs_0_ = bf16[64,3072]{1,0:T(8,128)(2,1)S(1)} collective-permute-done((bf16[64,3072]{1,0:T(8,128)(2,1)}, bf16[64,3072]{1,0:T(8,128)(2,1)S(1)}, u32[]{:S(2)}, u32[]{:S(2)}) %collective-permute-start.1) | collective-permute-done | bytes 393248 | tf_op jit(solution)/shard_map/ppermute | solution.py:32
  21.7 8.1 %collective-permute-start.18 = (s32[1,16]{1,0:T(1,128)}, s32[1,16]{1,0:T(1,128)S(1)}, u32[]{:S(2)}, u32[]{:S(2)}) collective-permute-start(s32[1,16]{1,0:T(1,128)} %param.18), channel_id=1, source_target_pairs={{0,248},{8,0},{16,8},{24,16},{32,24},{40,32},{48,40},{56,48},{64,5... | collective-permute-start | bytes 200 | tf_op jit(solution)/shard_map/ppermute | solution.py:28
  29.8 3.0 %copy-done = bf16[3072,3,384]{2,0,1:T(8,128)(2,1)S(1)} copy-done((bf16[3072,3,384]{2,0,1:T(8,128)(2,1)S(1)}, bf16[3072,3,384]{2,0,1:T(8,128)(2,1)}, u32[]{:S(2)}) %copy-start) | copy-done | bytes 7077912
  36.0 4.0 %project.3 = (bf16[128,768]{1,0:T(8,128)(2,1)S(1)}, bf16[128,384]{1,0:T(8,128)(2,1)S(1)}) custom-call(bf16[64,3072]{1,0:T(8,128)(2,1)S(1)} %copy-done.3, bf16[64,3072]{1,0:T(8,128)(2,1)S(1)} %collective-permute-done.refs_1_, f32[3,3072]{1,0:T(4,128)S(1)} %copy-done.17, bf16[3,3072,384]{2,1,0:T(8,128)(2,1)S(1)} %bitcast.18, f32[3,384]{1,0:T(4,128)S(1)} %copy-done.32, ...), custom_call_target="tpu_custom_call" | custom-call | flops 905969664 | bytes 7864320 | tf_op jit(solution)/shard_map/project/pallas_call | solution.py:102
  40.2 5.3 %collective-permute-start.8 = (bf16[128,768]{1,0:T(8,128)(2,1)S(1)}, bf16[128,768]{1,0:T(8,128)(2,1)S(1)}, u32[]{:S(2)}, u32[]{:S(2)}) collective-permute-start(bf16[128,768]{1,0:T(8,128)(2,1)S(1)} %get-tuple-element.30.a), channel_id=1, source_target_pairs={{0,248},{8,0},{16,8},{24,16},{32,24},{40,32},{48,40},{56,48},{64,5... | collective-permute-start | bytes 589832 | tf_op jit(solution)/shard_map/ppermute | solution.py:28
  45.6 8.1 %project.4 = (bf16[256,768]{1,0:T(8,128)(2,1)}, bf16[256,384]{1,0:T(8,128)(2,1)S(1)}) custom-call(bf16[64,3072]{1,0:T(8,128)(2,1)S(1)} %collective-permute-done.1.refs_0_, bf16[64,3072]{1,0:T(8,128)(2,1)S(1)} %collective-permute-done.2.refs_1_, bf16[64,3072]{1,0:T(8,128)(2,1)S(1)} %collective-permute-done.3.refs_2_, ...), custom_call_target="tpu_custom_call" | custom-call | flops 1811939328 | bytes 8650752 | tf_op jit(solution)/shard_map/project/pallas_call | solution.py:102
  55.8 5.2 %collective-permute-start.9 = (bf16[128,768]{1,0:T(8,128)(2,1)S(1)}, bf16[128,768]{1,0:T(8,128)(2,1)}, u32[]{:S(2)}, u32[]{:S(2)}) collective-permute-start(bf16[128,768]{1,0:T(8,128)(2,1)S(1)} %collective-permute-done.8.la), channel_id=1, source_target_pairs={{0,248},{8,0},{16,8},{24,16},{32,24},{40,32},{48,40},{56,48},{64,5... | collective-permute-start | bytes 589832 | tf_op jit(solution)/shard_map/ppermute | solution.py:28
  61.1 3.0 %copy-done.2 = bf16[3072,3,384]{2,0,1:T(8,128)(2,1)S(1)} copy-done((bf16[3072,3,384]{2,0,1:T(8,128)(2,1)S(1)}, bf16[3072,3,384]{2,0,1:T(8,128)(2,1)}, u32[]{:S(2)}) %copy-start.2) | copy-done | bytes 7077912
  64.1 4.7 %project.5 = (bf16[128,768]{1,0:T(8,128)(2,1)}, bf16[128,384]{1,0:T(8,128)(2,1)S(1)}) custom-call(bf16[64,3072]{1,0:T(8,128)(2,1)S(1)} %collective-permute-done.5.refs_0_, bf16[64,3072]{1,0:T(8,128)(2,1)S(1)} %collective-permute-done.6.refs_1_, f32[3,3072]{1,0:T(4,128)S(1)} %copy-done.18, bf16[3,3072,384]{2,1,0:T(8,128)(2,1)S(1)} %bitcast.20, ...), custom_call_target="tpu_custom_call" | custom-call | flops 905969664 | bytes 7864320 | tf_op jit(solution)/shard_map/project/pallas_call | solution.py:102
  68.8 4.2 %collective-permute-done.20.ra = bf16[128,768]{1,0:T(8,128)(2,1)S(1)} collective-permute-done((bf16[128,768]{1,0:T(8,128)(2,1)S(1)}, bf16[128,768]{1,0:T(8,128)(2,1)S(1)}, u32[]{:S(2)}, u32[]{:S(2)}) %collective-permute-start.20) | collective-permute-done | bytes 196640 | tf_op jit(solution)/shard_map/ppermute | solution.py:28
  75.0 3.4 %collective-permute-start.12 = (bf16[256,768]{1,0:T(8,128)(2,1)S(1)}, bf16[256,768]{1,0:T(8,128)(2,1)S(1)}, u32[]{:S(2)}, u32[]{:S(2)}) collective-permute-start(bf16[256,768]{1,0:T(8,128)(2,1)S(1)} %collective-permute-done.11.lb), channel_id=1, source_target_pairs={{0,248},{8,0},{16,8},{24,16},{32,24},{40,32},{48,40},{56,48},{64,5... | collective-permute-start | bytes 1179656 | tf_op jit(solution)/shard_map/ppermute | solution.py:28
  84.5 12.5 %collective-permute-done.21.a.ra = bf16[128,768]{1,0:T(8,128)(2,1)S(1)} collective-permute-done((bf16[128,768]{1,0:T(8,128)(2,1)S(1)}, bf16[128,768]{1,0:T(8,128)(2,1)S(1)}, u32[]{:S(2)}, u32[]{:S(2)}) %collective-permute-start.21) | collective-permute-done | bytes 196640 | tf_op jit(solution)/shard_map/ppermute | solution.py:28
  100.4 4.7 %collective-permute-start.13 = (bf16[256,768]{1,0:T(8,128)(2,1)S(1)}, bf16[256,768]{1,0:T(8,128)(2,1)S(1)}, u32[]{:S(2)}, u32[]{:S(2)}) collective-permute-start(bf16[256,768]{1,0:T(8,128)(2,1)S(1)} %collective-permute-done.12.lb), channel_id=1, source_target_pairs={{0,248},{8,0},{16,8},{24,16},{32,24},{40,32},{48,40},{56,48},{64,5... | collective-permute-start | bytes 1179656 | tf_op jit(solution)/shard_map/ppermute | solution.py:28
  105.3 5.4 %collective-permute-start.10 = (bf16[128,768]{1,0:T(8,128)(2,1)}, bf16[128,768]{1,0:T(8,128)(2,1)S(1)}, u32[]{:S(2)}, u32[]{:S(2)}) collective-permute-start(bf16[128,768]{1,0:T(8,128)(2,1)} %collective-permute-done.9.la), channel_id=1, source_target_pairs={{0,248},{8,0},{16,8},{24,16},{32,24},{40,32},{48,40},{56,48},{64,5... | collective-permute-start | bytes 589832 | tf_op jit(solution)/shard_map/ppermute | solution.py:28
  113.2 3.4 %collective-permute-done.24.b.rb = bf16[256,768]{1,0:T(8,128)(2,1)S(1)} collective-permute-done((bf16[256,768]{1,0:T(8,128)(2,1)S(1)}, bf16[256,768]{1,0:T(8,128)(2,1)S(1)}, u32[]{:S(2)}, u32[]{:S(2)}) %collective-permute-start.24) | collective-permute-done | bytes 393248 | tf_op jit(solution)/shard_map/ppermute | solution.py:28
  122.7 5.3 %collective-permute-start.17 = (bf16[256,768]{1,0:T(8,128)(2,1)}, bf16[256,768]{1,0:T(8,128)(2,1)S(1)}, u32[]{:S(2)}, u32[]{:S(2)}) collective-permute-start(bf16[256,768]{1,0:T(8,128)(2,1)} %select_tiles.2), channel_id=1, source_target_pairs={{0,248},{8,0},{16,8},{24,16},{32,24},{40,32},{48,40},{56,48},{64,5... | collective-permute-start | bytes 1179656 | tf_op jit(solution)/shard_map/ppermute | solution.py:28
  130.0 2.8 %attend_own.1 = (f32[512,384]{1,0:T(8,128)S(1)}, f32[512,384]{1,0:T(8,128)S(1)}) custom-call(bf16[512,384]{1,0:T(8,128)(2,1)S(1)} %constant_dynamic-update-slice_fusion.q, bf16[128,768]{1,0:T(8,128)(2,1)S(1)} %copy-done.38, bf16[256,768]{1,0:T(8,128)(2,1)} %get-tuple-element.31.b, bf16[128,768]{1,0:T(8,128)(2,1)} %get-tuple-element.32.c), custom_call_target="tpu_custom_call" | custom-call | flops 402653184 | bytes 5242880 | tf_op jit(solution)/shard_map/attend_own/pallas_call | solution.py:222
  135.3 3.0 %attend_hop.4 = (f32[512,384]{1,0:T(8,128)S(1)}, f32[512,384]{1,0:T(8,128)S(1)}) custom-call(s32[16]{0:T(128)S(1)} %gather_fusion.2, s32[1]{0:T(128)S(6)} %copy.14.count, bf16[512,384]{1,0:T(8,128)(2,1)S(1)} %constant_dynamic-update-slice_fusion.q, bf16[128,768]{1,0:T(8,128)(2,1)} %collective-permute-done.9.la, ...), custom_call_target="tpu_custom_call" | custom-call | flops 402653184 | bytes 5242880 | tf_op jit(solution)/shard_map/attend_hop/pallas_call | solution.py:236
  143.3 7.3 %collective-permute-done.30.edge_own = bf16[64,384]{1,0:T(8,128)(2,1)S(1)} collective-permute-done((bf16[64,384]{1,0:T(8,128)(2,1)S(1)}, bf16[64,384]{1,0:T(8,128)(2,1)S(1)}, u32[]{:S(2)}, u32[]{:S(2)}) %collective-permute-start.30) | collective-permute-done | bytes 49184 | tf_op jit(solution)/shard_map/ppermute | solution.py:392
  150.7 5.0 %out_project.1 = (f32[64,3072]{1,0:T(8,128)S(1)}, bf16[64,3072]{1,0:T(8,128)(2,1)S(1)}, bf16[64,3072]{1,0:T(8,128)(2,1)S(1)}, bf16[64,3072]{1,0:T(8,128)(2,1)S(1)}) custom-call(s32[4]{0:T(128)S(1)} %pad_add_fusion.strip, bf16[256,384]{1,0:T(8,128)(2,1)S(1)} %get-tuple-element.41.own, bf16[256,384]{1,0:T(8,128)(2,1)S(1)} %collective-permute-done.29.sib, ...), custom_call_target="tpu_custom_call" | custom-call | flops 1509949440 | bytes 7340032 | tf_op jit(solution)/shard_map/out_project/pallas_call | solution.py:324
  155.7 3.0 %collective-permute-start.33 = (bf16[64,3072]{1,0:T(8,128)(2,1)S(1)}, bf16[64,3072]{1,0:T(8,128)(2,1)S(1)}, u32[]{:S(2)}, u32[]{:S(2)}) collective-permute-start(bf16[64,3072]{1,0:T(8,128)(2,1)S(1)} %get-tuple-element.46), channel_id=1, source_target_pairs={{0,2},{1,3},{2,4},{3,5},{4,6},{5,7},{6,0},{7,1},{8,10},{9,11},{10,... | collective-permute-start | bytes 1179656 | tf_op jit(solution)/shard_map/ppermute | solution.py:32
  160.2 11.9 %collective-permute-done.33 = bf16[64,3072]{1,0:T(8,128)(2,1)S(1)} collective-permute-done((bf16[64,3072]{1,0:T(8,128)(2,1)S(1)}, bf16[64,3072]{1,0:T(8,128)(2,1)S(1)}, u32[]{:S(2)}, u32[]{:S(2)}) %collective-permute-start.33) | collective-permute-done | bytes 393248 | tf_op jit(solution)/shard_map/ppermute | solution.py:32
  172.2 3.4 %collective-permute-done.34 = bf16[64,3072]{1,0:T(8,128)(2,1)S(1)} collective-permute-done((bf16[64,3072]{1,0:T(8,128)(2,1)S(1)}, bf16[64,3072]{1,0:T(8,128)(2,1)S(1)}, u32[]{:S(2)}, u32[]{:S(2)}) %collective-permute-start.34) | collective-permute-done | bytes 393248 | tf_op jit(solution)/shard_map/ppermute | solution.py:32
  (162 shorter events, 37.5 us)
Async XLA Ops:
  0.0 20.7 %collective-permute-start.1 = (bf16[64,3072]{1,0:T(8,128)(2,1)}, bf16[64,3072]{1,0:T(8,128)(2,1)S(1)}, u32[]{:S(2)}, u32[]{:S(2)}) collective-permute-start(bf16[64,3072]{1,0:T(8,128)(2,1)} %refs_0_.1), channel_id=1, source_target_pairs={{0,6},{1,7},{2,0},{3,1},{4,2},{5,3},{6,4},{7,5},{8,14},{9,15},{10,... | collective-permute-start | bytes 1179656 | tf_op jit(solution)/shard_map/ppermute | solution.py:32
  0.7 20.0 %collective-permute-start.3 = (bf16[64,3072]{1,0:T(8,128)(2,1)}, bf16[64,3072]{1,0:T(8,128)(2,1)S(1)}, u32[]{:S(2)}, u32[]{:S(2)}) collective-permute-start(bf16[64,3072]{1,0:T(8,128)(2,1)} %refs_0_.1), channel_id=1, source_target_pairs={{0,2},{1,3},{2,4},{3,5},{4,6},{5,7},{6,0},{7,1},{8,10},{9,11},{10,... | collective-permute-start | bytes 1179656 | tf_op jit(solution)/shard_map/ppermute | solution.py:32
  3.2 18.0 %collective-permute-start.5 = (bf16[64,3072]{1,0:T(8,128)(2,1)}, bf16[64,3072]{1,0:T(8,128)(2,1)S(1)}, u32[]{:S(2)}, u32[]{:S(2)}) collective-permute-start(bf16[64,3072]{1,0:T(8,128)(2,1)} %refs_0_.1), channel_id=1, source_target_pairs={{0,4},{1,5},{2,6},{3,7},{4,0},{5,1},{6,2},{7,3},{8,12},{9,13},{10,... | collective-permute-start | bytes 1179656 | tf_op jit(solution)/shard_map/ppermute | solution.py:32
  3.4 18.3 %collective-permute-start = (bf16[64,3072]{1,0:T(8,128)(2,1)}, bf16[64,3072]{1,0:T(8,128)(2,1)S(1)}, u32[]{:S(2)}, u32[]{:S(2)}) collective-permute-start(bf16[64,3072]{1,0:T(8,128)(2,1)} %refs_0_.1), channel_id=1, source_target_pairs={{0,1},{1,0},{2,3},{3,2},{4,5},{5,4},{6,7},{7,6},{8,9},{9,8},{10,11... | collective-permute-start | bytes 1179656 | tf_op jit(solution)/shard_map/ppermute | solution.py:36
  20.7 19.4 %collective-permute-start.2 = (bf16[64,3072]{1,0:T(8,128)(2,1)S(1)}, bf16[64,3072]{1,0:T(8,128)(2,1)S(1)}, u32[]{:S(2)}, u32[]{:S(2)}) collective-permute-start(bf16[64,3072]{1,0:T(8,128)(2,1)S(1)} %collective-permute-done.1.refs_0_), channel_id=1, source_target_pairs={{0,1},{1,0},{2,3},{3,2},{4,5},{5,4},{6,7},{7,6},{8,9},{9,8},{10,11... | collective-permute-start | bytes 1179656 | tf_op jit(solution)/shard_map/ppermute | solution.py:36
  20.7 19.5 %collective-permute-start.4 = (bf16[64,3072]{1,0:T(8,128)(2,1)S(1)}, bf16[64,3072]{1,0:T(8,128)(2,1)S(1)}, u32[]{:S(2)}, u32[]{:S(2)}) collective-permute-start(bf16[64,3072]{1,0:T(8,128)(2,1)S(1)} %collective-permute-done.3.refs_2_), channel_id=1, source_target_pairs={{0,1},{1,0},{2,3},{3,2},{4,5},{5,4},{6,7},{7,6},{8,9},{9,8},{10,11... | collective-permute-start | bytes 1179656 | tf_op jit(solution)/shard_map/ppermute | solution.py:36
  21.2 122.1 %collective-permute-start.32 = (bf16[384,3072]{1,0:T(8,128)(2,1)}, bf16[384,3072]{1,0:T(8,128)(2,1)}, u32[]{:S(2)}, u32[]{:S(2)}) collective-permute-start(bf16[384,3072]{1,0:T(8,128)(2,1)} %w_own.1), channel_id=1, source_target_pairs={{0,1},{1,0},{2,3},{3,2},{4,5},{5,4},{6,7},{7,6},{8,9},{9,8},{10,11... | collective-permute-start | bytes 7077896 | tf_op jit(solution)/shard_map/ppermute | solution.py:36
  21.2 34.6 %collective-permute-start.6 = (bf16[64,3072]{1,0:T(8,128)(2,1)S(1)}, bf16[64,3072]{1,0:T(8,128)(2,1)S(1)}, u32[]{:S(2)}, u32[]{:S(2)}) collective-permute-start(bf16[64,3072]{1,0:T(8,128)(2,1)S(1)} %collective-permute-done.5.refs_0_), channel_id=1, source_target_pairs={{0,1},{1,0},{2,3},{3,2},{4,5},{5,4},{6,7},{7,6},{8,9},{9,8},{10,11... | collective-permute-start | bytes 1179656 | tf_op jit(solution)/shard_map/ppermute | solution.py:36
  21.7 18.2 %collective-permute-start.18 = (s32[1,16]{1,0:T(1,128)}, s32[1,16]{1,0:T(1,128)S(1)}, u32[]{:S(2)}, u32[]{:S(2)}) collective-permute-start(s32[1,16]{1,0:T(1,128)} %param.18), channel_id=1, source_target_pairs={{0,248},{8,0},{16,8},{24,16},{32,24},{40,32},{48,40},{56,48},{64,5... | collective-permute-start | bytes 200 | tf_op jit(solution)/shard_map/ppermute | solution.py:28
  40.0 15.5 %collective-permute-start.19 = (bf16[128,768]{1,0:T(8,128)(2,1)S(1)}, bf16[128,768]{1,0:T(8,128)(2,1)S(1)}, u32[]{:S(2)}, u32[]{:S(2)}) collective-permute-start(bf16[128,768]{1,0:T(8,128)(2,1)S(1)} %get-tuple-element.30.a), channel_id=1, source_target_pairs={{0,8},{8,16},{16,24},{24,32},{32,40},{40,48},{48,56},{56,64},{64,7... | collective-permute-start | bytes 589832 | tf_op jit(solution)/shard_map/ppermute | solution.py:28
  40.2 15.4 %collective-permute-start.8 = (bf16[128,768]{1,0:T(8,128)(2,1)S(1)}, bf16[128,768]{1,0:T(8,128)(2,1)S(1)}, u32[]{:S(2)}, u32[]{:S(2)}) collective-permute-start(bf16[128,768]{1,0:T(8,128)(2,1)S(1)} %get-tuple-element.30.a), channel_id=1, source_target_pairs={{0,248},{8,0},{16,8},{24,16},{32,24},{40,32},{48,40},{56,48},{64,5... | collective-permute-start | bytes 589832 | tf_op jit(solution)/shard_map/ppermute | solution.py:28
  53.6 21.4 %collective-permute-start.11 = (bf16[256,768]{1,0:T(8,128)(2,1)}, bf16[256,768]{1,0:T(8,128)(2,1)S(1)}, u32[]{:S(2)}, u32[]{:S(2)}) collective-permute-start(bf16[256,768]{1,0:T(8,128)(2,1)} %get-tuple-element.31.b), channel_id=1, source_target_pairs={{0,248},{8,0},{16,8},{24,16},{32,24},{40,32},{48,40},{56,48},{64,5... | collective-permute-start | bytes 1179656 | tf_op jit(solution)/shard_map/ppermute | solution.py:28
  55.6 22.9 %collective-permute-start.22 = (bf16[256,768]{1,0:T(8,128)(2,1)}, bf16[256,768]{1,0:T(8,128)(2,1)S(1)}, u32[]{:S(2)}, u32[]{:S(2)}) collective-permute-start(bf16[256,768]{1,0:T(8,128)(2,1)} %get-tuple-element.31.b), channel_id=1, source_target_pairs={{0,8},{8,16},{16,24},{24,32},{32,40},{40,48},{48,56},{56,64},{64,7... | collective-permute-start | bytes 1179656 | tf_op jit(solution)/shard_map/ppermute | solution.py:28
  55.7 17.3 %collective-permute-start.20 = (bf16[128,768]{1,0:T(8,128)(2,1)S(1)}, bf16[128,768]{1,0:T(8,128)(2,1)S(1)}, u32[]{:S(2)}, u32[]{:S(2)}) collective-permute-start(bf16[128,768]{1,0:T(8,128)(2,1)S(1)} %collective-permute-done.19.ra), channel_id=1, source_target_pairs={{0,8},{8,16},{16,24},{24,32},{32,40},{40,48},{48,56},{56,64},{64,7... | collective-permute-start | bytes 589832 | tf_op jit(solution)/shard_map/ppermute | solution.py:28
  55.8 17.2 %collective-permute-start.9 = (bf16[128,768]{1,0:T(8,128)(2,1)S(1)}, bf16[128,768]{1,0:T(8,128)(2,1)}, u32[]{:S(2)}, u32[]{:S(2)}) collective-permute-start(bf16[128,768]{1,0:T(8,128)(2,1)S(1)} %collective-permute-done.8.la), channel_id=1, source_target_pairs={{0,248},{8,0},{16,8},{24,16},{32,24},{40,32},{48,40},{56,48},{64,5... | collective-permute-start | bytes 589832 | tf_op jit(solution)/shard_map/ppermute | solution.py:28
  75.0 25.4 %collective-permute-start.12 = (bf16[256,768]{1,0:T(8,128)(2,1)S(1)}, bf16[256,768]{1,0:T(8,128)(2,1)S(1)}, u32[]{:S(2)}, u32[]{:S(2)}) collective-permute-start(bf16[256,768]{1,0:T(8,128)(2,1)S(1)} %collective-permute-done.11.lb), channel_id=1, source_target_pairs={{0,248},{8,0},{16,8},{24,16},{32,24},{40,32},{48,40},{56,48},{64,5... | collective-permute-start | bytes 1179656 | tf_op jit(solution)/shard_map/ppermute | solution.py:28
  78.4 26.7 %collective-permute-start.23 = (bf16[256,768]{1,0:T(8,128)(2,1)S(1)}, bf16[256,768]{1,0:T(8,128)(2,1)S(1)}, u32[]{:S(2)}, u32[]{:S(2)}) collective-permute-start(bf16[256,768]{1,0:T(8,128)(2,1)S(1)} %collective-permute-done.22.rb), channel_id=1, source_target_pairs={{0,8},{8,16},{16,24},{24,32},{32,40},{40,48},{48,56},{56,64},{64,7... | collective-permute-start | bytes 1179656 | tf_op jit(solution)/shard_map/ppermute | solution.py:28
  83.6 15.5 %collective-permute-start.26 = (bf16[128,768]{1,0:T(8,128)(2,1)S(1)}, bf16[128,768]{1,0:T(8,128)(2,1)S(1)}, u32[]{:S(2)}, u32[]{:S(2)}) collective-permute-start(bf16[128,768]{1,0:T(8,128)(2,1)S(1)} %collective-permute-done.25.rc), channel_id=1, source_target_pairs={{0,8},{8,16},{16,24},{24,32},{32,40},{40,48},{48,56},{56,64},{64,7... | collective-permute-start | bytes 589832 | tf_op jit(solution)/shard_map/ppermute | solution.py:28
  100.4 18.9 %collective-permute-start.13 = (bf16[256,768]{1,0:T(8,128)(2,1)S(1)}, bf16[256,768]{1,0:T(8,128)(2,1)S(1)}, u32[]{:S(2)}, u32[]{:S(2)}) collective-permute-start(bf16[256,768]{1,0:T(8,128)(2,1)S(1)} %collective-permute-done.12.lb), channel_id=1, source_target_pairs={{0,248},{8,0},{16,8},{24,16},{32,24},{40,32},{48,40},{56,48},{64,5... | collective-permute-start | bytes 1179656 | tf_op jit(solution)/shard_map/ppermute | solution.py:28
  119.3 21.6 %collective-permute-start.28 = (bf16[256,768]{1,0:T(8,128)(2,1)}, bf16[256,768]{1,0:T(8,128)(2,1)S(1)}, u32[]{:S(2)}, u32[]{:S(2)}) collective-permute-start(bf16[256,768]{1,0:T(8,128)(2,1)} %select_tiles.3), channel_id=1, source_target_pairs={{0,8},{8,16},{16,24},{24,32},{32,40},{40,48},{48,56},{56,64},{64,7... | collective-permute-start | bytes 1179656 | tf_op jit(solution)/shard_map/ppermute | solution.py:28
  122.7 18.2 %collective-permute-start.17 = (bf16[256,768]{1,0:T(8,128)(2,1)}, bf16[256,768]{1,0:T(8,128)(2,1)S(1)}, u32[]{:S(2)}, u32[]{:S(2)}) collective-permute-start(bf16[256,768]{1,0:T(8,128)(2,1)} %select_tiles.2), channel_id=1, source_target_pairs={{0,248},{8,0},{16,8},{24,16},{32,24},{40,32},{48,40},{56,48},{64,5... | collective-permute-start | bytes 1179656 | tf_op jit(solution)/shard_map/ppermute | solution.py:28
  155.7 16.5 %collective-permute-start.33 = (bf16[64,3072]{1,0:T(8,128)(2,1)S(1)}, bf16[64,3072]{1,0:T(8,128)(2,1)S(1)}, u32[]{:S(2)}, u32[]{:S(2)}) collective-permute-start(bf16[64,3072]{1,0:T(8,128)(2,1)S(1)} %get-tuple-element.46), channel_id=1, source_target_pairs={{0,2},{1,3},{2,4},{3,5},{4,6},{5,7},{6,0},{7,1},{8,10},{9,11},{10,... | collective-permute-start | bytes 1179656 | tf_op jit(solution)/shard_map/ppermute | solution.py:32
  158.7 16.9 %collective-permute-start.34 = (bf16[64,3072]{1,0:T(8,128)(2,1)S(1)}, bf16[64,3072]{1,0:T(8,128)(2,1)S(1)}, u32[]{:S(2)}, u32[]{:S(2)}) collective-permute-start(bf16[64,3072]{1,0:T(8,128)(2,1)S(1)} %get-tuple-element.47), channel_id=1, source_target_pairs={{0,6},{1,7},{2,0},{3,1},{4,2},{5,3},{6,4},{7,5},{8,14},{9,15},{10,... | collective-permute-start | bytes 1179656 | tf_op jit(solution)/shard_map/ppermute | solution.py:32
  158.7 16.9 %collective-permute-start.35 = (bf16[64,3072]{1,0:T(8,128)(2,1)S(1)}, bf16[64,3072]{1,0:T(8,128)(2,1)S(1)}, u32[]{:S(2)}, u32[]{:S(2)}) collective-permute-start(bf16[64,3072]{1,0:T(8,128)(2,1)S(1)} %get-tuple-element.48), channel_id=1, source_target_pairs={{0,4},{1,5},{2,6},{3,7},{4,0},{5,1},{6,2},{7,3},{8,12},{9,13},{10,... | collective-permute-start | bytes 1179656 | tf_op jit(solution)/shard_map/ppermute | solution.py:32
  (55 other events, 490.4 us)

commit v2 on v1

v2 whole, which is shorter than its diff:
```python
import functools
import math

import jax
import jax.numpy as jnp
from jax import lax
from jax.experimental import pallas as pl
from jax.experimental.pallas import tpu as pltpu
from jax.sharding import PartitionSpec as P

TILE = 128
TW = 4
NB = 8
OV = 64
ROWS = 64
D = 3072
HD = 128
HEADS = 3
LW = HEADS * HD
WINDOWS = 32
GROUPS = 8
MIB = 1 << 20
BIG = 24
COST = pl.CostEstimate(flops=1, bytes_accessed=1, transcendentals=0)
SMEM = functools.partial(pl.BlockSpec, memory_space=pltpu.SMEM)
VMEM = functools.partial(pl.BlockSpec, memory_space=pltpu.VMEM)


def along_win(value, steps):
    return lax.ppermute(value, "win", [(i, (i + steps) % WINDOWS) for i in range(WINDOWS)])


def to_y(value, steps):
    return lax.ppermute(value, "head", [(h, ((h // 2 + steps) % 4) * 2 + h % 2) for h in range(GROUPS)])


def swap_core(value):
    return lax.ppermute(value, "head", [(h, h ^ 1) for h in range(GROUPS)])


def strip_pairs(bottom_core):
    pairs = []
    for w in range(WINDOWS):
        for h in range(GROUPS):
            y, c = h // 2, h % 2
            if c == bottom_core:
                pairs.append((w * GROUPS + h, (w + 1) % WINDOWS * GROUPS + 2 * y))
            else:
                pairs.append((w * GROUPS + h, (w - 1) % WINDOWS * GROUPS + 2 * y + 1))
    return pairs


def modulate_kernel(lat, modulation, out):
    for g in range(ROWS // 16):
        rows = slice(g * 16, (g + 1) * 16)
        wide = lat[rows, :].astype(jnp.float32)
        mean = jnp.sum(wide, axis=-1, keepdims=True) * (1.0 / D)
        centred = wide - mean
        spread = jnp.sum(centred * centred, axis=-1, keepdims=True) * (1.0 / D)
        normed = centred * lax.rsqrt(spread + 1e-06)
        out[rows, :] = ((1.0 + modulation[1:2, :]) * normed + modulation[0:1, :]).astype(jnp.bfloat16)


def modulate(lat, modulation):
    return pl.pallas_call(
        modulate_kernel,
        in_specs=[VMEM()] * 2,
        out_specs=VMEM(),
        out_shape=jax.ShapeDtypeStruct((ROWS, D), jnp.bfloat16),
        compiler_params=pltpu.CompilerParams(vmem_limit_bytes=BIG * MIB),
        cost_estimate=COST,
        name="modulate",
    )(lat, modulation)


def normed_heads(raw, gain):
    out = []
    for h in range(HEADS):
        part = raw[:, h * HD : (h + 1) * HD]
        mean_square = jnp.sum(part * part, axis=-1, keepdims=True) * (1.0 / HD)
        out.append((part * lax.rsqrt(mean_square + 1e-06) * gain).astype(jnp.bfloat16))
    return out


def kv_kernel(parts, carried, *refs):
    weight, bias, gain = refs[parts : parts + 3]
    carry = refs[parts + 3 : parts + 3 + carried]
    outs, mod_ref = refs[parts + 3 + carried : -1], refs[-1]
    step = pl.program_id(0)
    split = parts * ROWS - (TILE if carried else 0)

    def store(part, cols):
        outs[0][:, cols] = part[:split]
        for out in outs[1:]:
            out[TILE:, cols] = part[split:]

    @pl.when(step == 0)
    def _():
        for i in range(parts):
            mod_ref[i * ROWS : (i + 1) * ROWS, :] = refs[i][...]
        for ref, out in zip(carry, outs[1:]):
            out[0:TILE, :] = ref[...]
        raw = jnp.dot(mod_ref[...], weight[0], preferred_element_type=jnp.float32)
        for h, part in enumerate(normed_heads(raw + bias[1:2, :], gain[1:2, :])):
            store(part, slice(h * HD, (h + 1) * HD))

    @pl.when(step == 1)
    def _():
        raw = jnp.dot(mod_ref[...], weight[0], preferred_element_type=jnp.float32)
        store((raw + bias[2:3, :]).astype(jnp.bfloat16), slice(LW, 2 * LW))


def q_kernel(parts, *refs):
    weight, bias, gain, q_ref, mod_ref = refs[parts:]
    for i in range(parts):
        mod_ref[i * ROWS : (i + 1) * ROWS, :] = refs[i][...]
    raw = jnp.dot(mod_ref[...], weight[0], preferred_element_type=jnp.float32)
    for h, part in enumerate(normed_heads(raw + bias[0:1, :], gain[0:1, :])):
        q_ref[:, h * HD : (h + 1) * HD] = part


def project(kernel, first, count, mod, weight, bias, gain, carry=()):
    parts = len(mod)
    rows = parts * ROWS
    out_rows = [rows - TILE] + [2 * TILE] * len(carry) if carry else [rows]
    whole = lambda shape: pl.BlockSpec(shape, lambda c: (0,) * len(shape))
    out = pl.pallas_call(
        kernel,
        grid=(count,),
        in_specs=[whole((ROWS, D))] * parts
        + [pl.BlockSpec((1, D, LW), lambda c: (first + c, 0, 0)), whole((3, LW)), whole((2, HD))]
        + [whole((TILE, 2 * LW))] * len(carry),
        out_specs=[whole((n, count * LW)) for n in out_rows],
        out_shape=[jax.ShapeDtypeStruct((n, count * LW), jnp.bfloat16) for n in out_rows],
        scratch_shapes=[pltpu.VMEM((rows, D), jnp.bfloat16)],
        compiler_params=pltpu.CompilerParams(vmem_limit_bytes=BIG * MIB),
        cost_estimate=COST,
        name="project",
    )(*mod, weight, bias, gain, *carry)
    return out if carry else out[0]


def project_kv(mod, *args, carry=()):
    return project(functools.partial(kv_kernel, len(mod), len(carry)), 1, 2, mod, *args, carry=carry)


def project_q(mod, *args):
    return project(functools.partial(q_kernel, len(mod)), 0, 1, mod, *args)


def pick_tile(dst, row, chunks, place):
    a, b, c = chunks

    @pl.when(place == 0)
    def _():
        dst[row : row + TILE, :] = a[...]

    @pl.when(jnp.logical_or(place == 1, place == 2))
    def _():
        dst[row : row + TILE, :] = b[pl.ds(pl.multiple_of((place - 1) * TILE, TILE), TILE), :]

    @pl.when(place == 3)
    def _():
        dst[row : row + TILE, :] = c[...]


def place_of(tile, head):
    step = ((tile & 3) - (head >> 1)) & 3
    return step ^ (step >> 1)


def select_kernel(head, want_left, want_right, la, lb, lc, ra, rb, rc, left, right):
    for k in range(2):
        pick_tile(left, k * TILE, (la, lb, lc), place_of(want_left[0, 12 + k], head[0]))
        pick_tile(right, k * TILE, (ra, rb, rc), place_of(want_right[0, 14 + k], head[0]))


def select_tiles(head, want_left, want_right, left, right):
    return pl.pallas_call(
        select_kernel,
        grid=(1,),
        in_specs=[SMEM()] * 3 + chunk_specs((0, 0)) * 2,
        out_specs=[whole_spec((2 * TILE, 2 * LW))] * 2,
        out_shape=[jax.ShapeDtypeStruct((2 * TILE, 2 * LW), jnp.bfloat16)] * 2,
        compiler_params=pltpu.CompilerParams(vmem_limit_bytes=BIG * MIB),
        cost_estimate=COST,
        name="select_tiles",
    )(head, want_left, want_right, *left, *right)


def accumulate(kv, q_block, live, num, den, first):
    scale = HD**-0.5 * math.log2(math.e)
    for h in range(HEADS):
        cols = slice(h * HD, (h + 1) * HD)
        scores = lax.dot_general(
            q_block(cols), kv[:, cols], (((1,), (1,)), ((), ())), preferred_element_type=jnp.float32
        )
        weights = jnp.exp2(scores * scale)
        parts = []
        for t in range(weights.shape[1] // TILE):
            w = weights[:, t * TILE : (t + 1) * TILE]
            if live is not None:
                w = jnp.where(live(t), w, 0.0)
            parts.append(w)
        total = functools.reduce(jnp.add, parts)
        rounded = jnp.concatenate([w.astype(jnp.bfloat16) for w in parts], axis=1)
        mixed = jnp.dot(rounded, kv[:, LW + h * HD : LW + (h + 1) * HD], preferred_element_type=jnp.float32)
        if first:
            num[0][:, cols] = mixed
            den[0][:, cols] = total
        else:
            num[0][:, cols] = num[1][:, cols] + mixed
            den[0][:, cols] = den[1][:, cols] + total


QB = 256


def own_kernel(q, a, b, c, num, den, kbuf):
    @pl.when(pl.program_id(0) == 0)
    def _():
        kbuf[0:TILE, :] = a[...]
        kbuf[TILE : 3 * TILE, :] = b[...]
        kbuf[3 * TILE :, :] = c[...]

    accumulate(kbuf, lambda cols: q[:, cols], None, (num,), (den,), True)


def hop_kernel(base, head, tiles, count, q, la, lb, lc, ra, rb, rc, num_in, den_in, num, den, kbuf):
    @pl.when(pl.program_id(0) == 0)
    def _():
        for k in range(2):
            pick_tile(kbuf, k * TILE, (la, lb, lc), place_of(tiles[0, base + k], head[0]))
            pick_tile(kbuf, (2 + k) * TILE, (ra, rb, rc), place_of(tiles[0, base + 2 + k], head[0]))

    live = lambda t: base + t < count[0]
    accumulate(kbuf, lambda cols: q[:, cols], live, (num, num_in), (den, den_in), False)


def rows_spec(width):
    return pl.BlockSpec((QB, width), lambda i: (i, 0))


def whole_spec(shape):
    return pl.BlockSpec(shape, lambda i: (0,) * len(shape))


ACC = [jax.ShapeDtypeStruct((512, LW), jnp.float32)] * 2
KBUF = [pltpu.VMEM((4 * TILE, 2 * LW), jnp.bfloat16)]


def chunk_specs(halves):
    a, c = halves
    return [
        pl.BlockSpec((TILE, 2 * LW), lambda i: (a, 0)),
        pl.BlockSpec((2 * TILE, 2 * LW), lambda i: (0, 0)),
        pl.BlockSpec((TILE, 2 * LW), lambda i: (c, 0)),
    ]


def attend_own(q, chunks):
    return pl.pallas_call(
        own_kernel,
        grid=(512 // QB,),
        in_specs=[rows_spec(LW)] + chunk_specs((0, 1)),
        out_specs=[rows_spec(LW)] * 2,
        out_shape=ACC,
        scratch_shapes=KBUF,
        compiler_params=pltpu.CompilerParams(vmem_limit_bytes=BIG * MIB),
        cost_estimate=COST,
        name="attend_own",
    )(q, *chunks)


def attend_hop(hop, halves, head, tiles, count, q, left, right, num, den):
    return pl.pallas_call(
        functools.partial(hop_kernel, 4 * (hop - 1)),
        grid=(512 // QB,),
        in_specs=[SMEM()] * 3 + [rows_spec(LW)] + chunk_specs(halves) * 2 + [rows_spec(LW)] * 2,
        out_specs=[rows_spec(LW)] * 2,
        out_shape=ACC,
        scratch_shapes=KBUF,
        compiler_params=pltpu.CompilerParams(vmem_limit_bytes=BIG * MIB),
        cost_estimate=COST,
        name="attend_hop",
    )(head, tiles, count, q, *left, *right, num, den)


def last_kernel(base, head, count, q, left, right, num_in, den_in, own, sib, edge_a, edge_b, kbuf, num, den):
    step = pl.program_id(0)

    @pl.when(step == 0)
    def _():
        kbuf[0 : 2 * TILE, :] = left[...]
        kbuf[2 * TILE :, :] = right[...]

    live = lambda t: base + t < count[0]
    accumulate(kbuf, lambda cols: q[:, cols], live, (num, num_in), (den, den_in), False)
    for h in range(HEADS):
        cols = slice(h * HD, (h + 1) * HD)
        total = jnp.sum(den[:, cols], axis=-1, keepdims=True)
        out = (num[:, cols] / total).astype(jnp.bfloat16)
        for t in range(QB // TILE):
            at = pl.ds(pl.multiple_of(step * (QB // 2) + t * ROWS, ROWS), ROWS)
            own[at, cols] = out[t * TILE : t * TILE + ROWS]
            sib[at, cols] = out[t * TILE + ROWS : (t + 1) * TILE]

    @pl.when(step == 512 // QB - 1)
    def _():
        core = head[0] & 1
        edge_a[...] = sib[pl.ds(pl.multiple_of(place_of(3 * (1 - core), head[0]) * ROWS, ROWS), ROWS), :]
        edge_b[...] = own[pl.ds(pl.multiple_of(place_of(3 * core, head[0]) * ROWS, ROWS), ROWS), :]


def attend_last(head, count, q, left, right, num, den):
    half = jax.ShapeDtypeStruct((256, LW), jnp.bfloat16)
    edge = jax.ShapeDtypeStruct((ROWS, LW), jnp.bfloat16)
    return pl.pallas_call(
        functools.partial(last_kernel, 12),
        grid=(512 // QB,),
        in_specs=[SMEM()] * 2
        + [rows_spec(LW)]
        + [whole_spec((2 * TILE, 2 * LW))] * 2
        + [rows_spec(LW)] * 2,
        out_specs=[whole_spec((256, LW))] * 2 + [whole_spec((ROWS, LW))] * 2,
        out_shape=[half, half, edge, edge],
        scratch_shapes=KBUF + [pltpu.VMEM((QB, LW), jnp.float32)] * 2,
        compiler_params=pltpu.CompilerParams(vmem_limit_bytes=BIG * MIB),
        cost_estimate=COST,
        name="attend_last",
    )(head, count, q, left, right, num, den)


NCOL = 768


def out_kernel(head, window, strips, own, sib, edge_own, edge_sib, w_own, w_sib, o0, o1, o3, o2, a_own, a_sib, e_own, e_sib):
    core = head[0] & 1
    place = place_of(3 * core, head[0])
    shared = strips[(window[0] + core + WINDOWS - 1) & (WINDOWS - 1)]
    top = 1 - core

    @pl.when(pl.program_id(0) == 0)
    def _():
        a_own[...] = own[...]
        a_sib[...] = sib[...]
        row = lax.broadcasted_iota(jnp.int32, (ROWS, 1), 0)
        low = jnp.where(top == 1, 0, OV - shared)
        keep = jnp.where(jnp.logical_and(row >= low, row < low + shared), 0.5, 1.0)
        at = pl.ds(pl.multiple_of(place * ROWS, ROWS), ROWS)
        a_own[at, :] = (own[at, :].astype(jnp.float32) * keep).astype(jnp.bfloat16)
        a_sib[at, :] = (sib[at, :].astype(jnp.float32) * keep).astype(jnp.bfloat16)
        i = lax.broadcasted_iota(jnp.int32, (ROWS, ROWS), 0)
        j = lax.broadcasted_iota(jnp.int32, (ROWS, ROWS), 1)
        offset = jnp.where(top == 1, OV - shared, shared - OV)
        shift = jnp.where(j == i + offset, 0.5, 0.0).astype(jnp.bfloat16)
        e_own[...] = jnp.dot(shift, edge_own[...], preferred_element_type=jnp.float32).astype(jnp.bfloat16)
        e_sib[...] = jnp.dot(shift, edge_sib[...], preferred_element_type=jnp.float32).astype(jnp.bfloat16)

    dot = functools.partial(jnp.dot, preferred_element_type=jnp.float32)
    main = dot(a_own[...], w_own[...]) + dot(a_sib[...], w_sib[...])
    extra = dot(e_own[...], w_own[...]) + dot(e_sib[...], w_sib[...])
    for k, ref in enumerate((o0, o1, o3, o2)):
        block = main[k * ROWS : (k + 1) * ROWS]
        ref[...] = (block + jnp.where(place == k, extra, 0.0)).astype(ref.dtype)


def out_project(head, window, strips, own, sib, edge_own, edge_sib, w_own, w_sib):
    cols = lambda rows: pl.BlockSpec((rows, NCOL), lambda i: (0, i))
    sent = jax.ShapeDtypeStruct((ROWS, D), jnp.bfloat16)
    return pl.pallas_call(
        out_kernel,
        grid=(D // NCOL,),
        in_specs=[SMEM()] * 3
        + [whole_spec((256, LW))] * 2
        + [whole_spec((ROWS, LW))] * 2
        + [cols(LW)] * 2,
        out_specs=[cols(ROWS)] * 4,
        out_shape=[jax.ShapeDtypeStruct((ROWS, D), jnp.float32), sent, sent, sent],
        scratch_shapes=[pltpu.VMEM((256, LW), jnp.bfloat16)] * 2 + [pltpu.VMEM((ROWS, LW), jnp.bfloat16)] * 2,
        compiler_params=pltpu.CompilerParams(vmem_limit_bytes=24 * MIB),
        cost_estimate=COST,
        name="out_project",
    )(head, window, strips, own, sib, edge_own, edge_sib, w_own, w_sib)


def shards(
    latents,
    modulation,
    qkv_weight,
    qkv_bias,
    norm_gain,
    out_weight,
    out_bias,
    key_tiles,
    key_count,
    strip_rows,
):
    head = lax.axis_index("head").reshape(1)
    window = lax.axis_index("win").reshape(1)
    weight = jnp.transpose(qkv_weight, (1, 0, 2))
    args = (weight, qkv_bias, norm_gain)
    barrier = lax.optimization_barrier

    mod0 = modulate(latents, modulation)
    sib0 = swap_core(mod0)
    mod1, mod3 = to_y(mod0, -1), to_y(mod0, 1)
    mod2 = to_y(mod0, 2)
    kv_a = project_kv([mod0, sib0], *args)
    ra1, la1 = along_win(kv_a, 1), along_win(kv_a, -1)
    mod1, mod3, mod2, ra1, la1, wanted = barrier((mod1, mod3, mod2, ra1, la1, key_tiles))
    sib1, sib3, sib2 = swap_core(mod1), swap_core(mod3), swap_core(mod2)
    tiles_next, tiles_prev = along_win(wanted, -1), along_win(wanted, 1)
    sib1, sib3, sib2, tiles_next, tiles_prev = barrier((sib1, sib3, sib2, tiles_next, tiles_prev))
    kv_b, right_ac, left_ac = project_kv([mod1, sib1, mod3, sib3, mod2, sib2], *args, carry=(ra1, la1))
    rb1, lb1 = along_win(kv_b, 1), along_win(kv_b, -1)
    rac2, lac2 = along_win(right_ac, 1), along_win(left_ac, -1)
    kv_b, w_sent = barrier((kv_b, out_weight))
    w_sib = swap_core(w_sent)
    q = project_q([mod0, sib0, mod1, sib1, mod3, sib3, mod2, sib2], *args)
    hop_args = (head, key_tiles, key_count, q)
    num, den = attend_own(q, (kv_a, kv_b, right_ac))
    rb1, lb1, num, den, w_sib = barrier((rb1, lb1, num, den, w_sib))
    rb2, lb2 = along_win(rb1, 1), along_win(lb1, -1)
    rac3, lac3 = along_win(rac2, 1), along_win(lac2, -1)
    num, den = attend_hop(1, (0, 1), *hop_args, (la1, lb1, lac2), (ra1, rb1, rac2), num, den)
    rb2, lb2, num, den = barrier((rb2, lb2, num, den))
    rb3, lb3 = along_win(rb2, 1), along_win(lb2, -1)
    rc3, lc3 = along_win(rac3[TILE:], 1), along_win(lac3[TILE:], -1)
    num, den = attend_hop(2, (0, 1), *hop_args, (lac2, lb2, lac3), (rac2, rb2, rac3), num, den)
    rb3, lb3, rc3, lc3, num, den = barrier((rb3, lb3, rc3, lc3, num, den))
    right, left = (rac3, rb3, rc3), (lac3, lb3, lc3)
    last_left, last_right = select_tiles(head, tiles_prev, tiles_next, left, right)
    last_left, last_right = along_win(last_left, -1), along_win(last_right, 1)
    num, den = attend_hop(3, (0, 0), *hop_args, right=right, left=left, num=num, den=den)

    own, sib, edge_a, edge_b = attend_last(head, key_count, q, last_left, last_right, num, den)
    edge_own = lax.ppermute(edge_a, ("win", "head"), strip_pairs(0))
    edge_sib = lax.ppermute(edge_b, ("win", "head"), strip_pairs(1))
    sib = swap_core(sib)
    o0, o1, o3, o2 = out_project(head, window, strip_rows, own, sib, edge_own, edge_sib, out_weight, w_sib)
    total = o0
    for part in (to_y(o1, 1), to_y(o3, -1), to_y(o2, 2)):
        total = total + part.astype(jnp.float32)
    result = latents.astype(jnp.float32) + modulation[2] * (total + out_bias)
    return result.astype(jnp.bfloat16)


def solution(mesh):
    in_specs = (
        P(("win", "head"), None),
        P(),
        P(None, None, "head"),
        P(None, "head"),
        P(),
        P("head", None),
        P(),
        P("win", None),
        P("win"),
        P(),
    )
    out_specs = P(("win", "head"), None)
    return jax.shard_map(shards, mesh=mesh, in_specs=in_specs, out_specs=out_specs, check_vma=False)
```

time: 177 us -> 147 us (0.83)
  waiting for transfers between devices: 61.5 us -> 41.7 us
  Pallas kernels: 38.4 us -> 23.8 us
  starting transfers between devices: 52 us -> 62.7 us
  local copies, waits for them, and re-layouts: 19.7 us -> 16 us
    pallas_call x7, Pallas kernels: 27.7 us -> 13.3 us  [the longest x3 6.24 us: project(): pl.pallas_call(kernel, grid=(count,), in_specs=[whole((ROWS, D))] * parts...]
    ppermute x6, waiting for transfers between devices: 32.6 us -> 18.6 us  [to_y(): lax.ppermute(value, 'head', [(h, (h // 2 + steps) % 4 * 2 + h % 2) for h...]
    ppermute x22 -> x18, starting transfers between devices: 42.7 us -> 53.2 us  [along_win(): lax.ppermute(value, 'win', [(i, (i + steps) % WINDOWS) for i in range(WIN...]
    ppermute x22 -> x18, waiting for transfers between devices: 21.6 us -> 16 us  [along_win(): lax.ppermute(value, 'win', [(i, (i + steps) % WINDOWS) for i in range(WIN...]
    gather x3 -> x0, local copies, waits for them, and re-layouts: 3.01 us -> none  [places(): return order[(tiles % TW - y) % 4]]
    unnamed x88 -> x42, local copies, waits for them, and re-layouts: 14.5 us -> 15.1 us
  transfers between devices with their start and end apart: 36 -> 32, of which waited for: 8 -> 11; matrix products, arithmetic and copies ran while one was open for 4% -> 1% of each run, Pallas kernels for 19% -> 9%
where the time goes in v2:
time: 147 us; the launch traced here: 146 us
  starting transfers between devices  62.7 us (43%)
  waiting for transfers between devices  41.7 us (28%)
  Pallas kernels  23.8 us (16%)
  local copies, waits for them, and re-layouts  16 us (11%)
    ppermute x18, starting transfers between devices, along_win(): lax.ppermute(value, 'win', [(i, (i + steps) % WINDOWS) for i in range(WIN...  53.2 us
    ppermute x6, waiting for transfers between devices, to_y(): lax.ppermute(value, 'head', [(h, (h // 2 + steps) % 4 * 2 + h % 2) for h...  18.6 us
    ppermute x18, waiting for transfers between devices, along_win(): lax.ppermute(value, 'win', [(i, (i + steps) % WINDOWS) for i in range(WIN...  16 us
    unnamed x42, local copies, waits for them, and re-layouts  15.1 us
    pallas_call x3, Pallas kernels, attend_hop(): pl.pallas_call(functools.partial(hop_kernel, 4 * (hop - 1)), grid=(512 //...  8.75 us
    ppermute x6, starting transfers between devices, to_y(): lax.ppermute(value, 'head', [(h, (h // 2 + steps) % 4 * 2 + h % 2) for h...  8.14 us
    ppermute x1, waiting for transfers between devices, shards(): edge_own = lax.ppermute(edge_a, ('win', 'head'), strip_pairs(0))  7.13 us
    pallas_call x3, Pallas kernels, project(): pl.pallas_call(kernel, grid=(count,), in_specs=[whole((ROWS, D))] * parts...  6.24 us
  transfers between devices with their start and end apart: 32, of which 11 were waited for; matrix products, arithmetic and copies ran while one was open for 1% of the time, Pallas kernels for 9%

profile of v2, /device:TPU:24, one launch (start us, length us, event | category | flops | bytes accessed | tf_op | source)
XLA Modules:
  0.0 146.2 jit_solution(9849646264891188289)
XLA Ops:
  3.1 2.5 %collective-permute-start.2 = (bf16[64,3072]{1,0:T(8,128)(2,1)S(1)}, bf16[64,3072]{1,0:T(8,128)(2,1)S(1)}, u32[]{:S(2)}, u32[]{:S(2)}) collective-permute-start(bf16[64,3072]{1,0:T(8,128)(2,1)S(1)} %modulate.1.refs_0_), channel_id=1, source_target_pairs={{0,2},{1,3},{2,4},{3,5},{4,6},{5,7},{6,0},{7,1},{8,10},{9,11},{10,... | collective-permute-start | bytes 1179656 | tf_op jit(solution)/shard_map/ppermute | solution.py:34
  5.8 3.0 %copy-done = bf16[3072,3,384]{2,0,1:T(8,128)(2,1)S(1)} copy-done((bf16[3072,3,384]{2,0,1:T(8,128)(2,1)S(1)}, bf16[3072,3,384]{2,0,1:T(8,128)(2,1)}, u32[]{:S(2)}) %copy-start) | copy-done | bytes 7077912
  13.3 6.2 %collective-permute-start.5 = (bf16[128,768]{1,0:T(8,128)(2,1)S(1)}, bf16[128,768]{1,0:T(8,128)(2,1)S(1)}, u32[]{:S(2)}, u32[]{:S(2)}) collective-permute-start(bf16[128,768]{1,0:T(8,128)(2,1)S(1)} %project.3.a), channel_id=1, source_target_pairs={{0,248},{8,0},{16,8},{24,16},{32,24},{40,32},{48,40},{56,48},{64,5... | collective-permute-start | bytes 589832 | tf_op jit(solution)/shard_map/ppermute | solution.py:30
  19.5 3.2 %collective-permute-done.2.refs_4_.refs_2_ = bf16[64,3072]{1,0:T(8,128)(2,1)S(1)} collective-permute-done((bf16[64,3072]{1,0:T(8,128)(2,1)S(1)}, bf16[64,3072]{1,0:T(8,128)(2,1)S(1)}, u32[]{:S(2)}, u32[]{:S(2)}) %collective-permute-start.2) | collective-permute-done | bytes 393248 | tf_op jit(solution)/shard_map/ppermute | solution.py:34
  26.1 6.1 %collective-permute-start.9 = (s32[1,16]{1,0:T(1,128)S(1)}, s32[1,16]{1,0:T(1,128)S(1)}, u32[]{:S(2)}, u32[]{:S(2)}) collective-permute-start(s32[1,16]{1,0:T(1,128)S(1)} %copy-done.18), channel_id=1, source_target_pairs={{0,248},{8,0},{16,8},{24,16},{32,24},{40,32},{48,40},{56,48},{64,5... | collective-permute-start | bytes 200 | tf_op jit(solution)/shard_map/ppermute | solution.py:30
  33.8 3.0 %project.5 = (bf16[256,768]{1,0:T(8,128)(2,1)S(1)}, bf16[256,768]{1,0:T(8,128)(2,1)S(1)}, bf16[256,768]{1,0:T(8,128)(2,1)S(1)}) custom-call(bf16[64,3072]{1,0:T(8,128)(2,1)S(1)} %collective-permute-done.1.refs_2_.refs_0_, bf16[64,3072]{1,0:T(8,128)(2,1)S(1)} %collective-permute-done.6.refs_3_.refs_1_, ...), custom_call_target="tpu_custom_call" | custom-call | flops 1 | bytes 1 | tf_op jit(solution)/shard_map/project/pallas_call | solution.py:127
  37.2 5.4 %collective-permute-start.14 = (bf16[256,768]{1,0:T(8,128)(2,1)S(1)}, bf16[256,768]{1,0:T(8,128)(2,1)}, u32[]{:S(2)}, u32[]{:S(2)}) collective-permute-start(bf16[256,768]{1,0:T(8,128)(2,1)S(1)} %get-tuple-element.67.b), channel_id=1, source_target_pairs={{0,248},{8,0},{16,8},{24,16},{32,24},{40,32},{48,40},{56,48},{64,5... | collective-permute-start | bytes 1179656 | tf_op jit(solution)/shard_map/ppermute | solution.py:30
  42.6 5.3 %collective-permute-start.11 = (bf16[256,768]{1,0:T(8,128)(2,1)S(1)}, bf16[256,768]{1,0:T(8,128)(2,1)}, u32[]{:S(2)}, u32[]{:S(2)}) collective-permute-start(bf16[256,768]{1,0:T(8,128)(2,1)S(1)} %get-tuple-element.65), channel_id=1, source_target_pairs={{0,248},{8,0},{16,8},{24,16},{32,24},{40,32},{48,40},{56,48},{64,5... | collective-permute-start | bytes 1179656 | tf_op jit(solution)/shard_map/ppermute | solution.py:30
  54.8 5.3 %collective-permute-start.17 = (bf16[256,768]{1,0:T(8,128)(2,1)}, bf16[256,768]{1,0:T(8,128)(2,1)}, u32[]{:S(2)}, u32[]{:S(2)}) collective-permute-start(bf16[256,768]{1,0:T(8,128)(2,1)} %collective-permute-done.14.lb), channel_id=1, source_target_pairs={{0,248},{8,0},{16,8},{24,16},{32,24},{40,32},{48,40},{56,48},{64,5... | collective-permute-start | bytes 1179656 | tf_op jit(solution)/shard_map/ppermute | solution.py:30
  60.7 5.3 %collective-permute-start.12 = (bf16[256,768]{1,0:T(8,128)(2,1)}, bf16[256,768]{1,0:T(8,128)(2,1)S(1)}, u32[]{:S(2)}, u32[]{:S(2)}) collective-permute-start(bf16[256,768]{1,0:T(8,128)(2,1)} %collective-permute-done.11.lc.la), channel_id=1, source_target_pairs={{0,248},{8,0},{16,8},{24,16},{32,24},{40,32},{48,40},{56,48},{64,5... | collective-permute-start | bytes 1179656 | tf_op jit(solution)/shard_map/ppermute | solution.py:30
  70.8 3.2 %attend_hop.3 = (f32[512,384]{1,0:T(8,128)S(1)}, f32[512,384]{1,0:T(8,128)S(1)}) custom-call(s32[1]{0:T(128)} %bitcast.1.head, s32[1,16]{1,0:T(1,128)S(1)} %copy-done.18, s32[1]{0:T(128)S(6)} %copy.11.count, bf16[512,384]{1,0:T(8,128)(2,1)S(1)} %project.4.q, bf16[128,768]{1,0:T(8,128)(2,1)S(1)} %copy-done.14, bf16[256,768]{1,0:T(8,128)(2,1)} %collective-permute-done.14.lb, ...), custom_call_target="tpu_custom_call" | custom-call | flops 1 | bytes 1 | tf_op jit(solution)/shard_map/attend_hop/pallas_call | solution.py:276
  74.1 5.3 %collective-permute-start.20 = (bf16[256,768]{1,0:T(8,128)(2,1)}, bf16[256,768]{1,0:T(8,128)(2,1)S(1)}, u32[]{:S(2)}, u32[]{:S(2)}) collective-permute-start(bf16[256,768]{1,0:T(8,128)(2,1)} %collective-permute-done.17.lb), channel_id=1, source_target_pairs={{0,248},{8,0},{16,8},{24,16},{32,24},{40,32},{48,40},{56,48},{64,5... | collective-permute-start | bytes 1179656 | tf_op jit(solution)/shard_map/ppermute | solution.py:30
  79.5 5.4 %collective-permute-start.23 = (bf16[128,768]{1,0:T(8,128)(2,1)S(1)}, bf16[128,768]{1,0:T(8,128)(2,1)S(1)}, u32[]{:S(2)}, u32[]{:S(2)}) collective-permute-start(bf16[128,768]{1,0:T(8,128)(2,1)S(1)} %slice.13), channel_id=1, source_target_pairs={{0,248},{8,0},{16,8},{24,16},{32,24},{40,32},{48,40},{56,48},{64,5... | collective-permute-start | bytes 589832 | tf_op jit(solution)/shard_map/ppermute | solution.py:30
  84.9 3.2 %attend_hop.4 = (f32[512,384]{1,0:T(8,128)S(1)}, f32[512,384]{1,0:T(8,128)S(1)}) custom-call(s32[1]{0:T(128)} %bitcast.1.head, s32[1,16]{1,0:T(1,128)S(1)} %copy-done.18, s32[1]{0:T(128)S(6)} %copy.11.count, bf16[512,384]{1,0:T(8,128)(2,1)S(1)} %project.4.q, bf16[256,768]{1,0:T(8,128)(2,1)} %collective-permute-done.11.lc.la, ...), custom_call_target="tpu_custom_call" | custom-call | flops 1 | bytes 1 | tf_op jit(solution)/shard_map/attend_hop/pallas_call | solution.py:276
  88.1 3.7 %collective-permute-done.22.rc = bf16[128,768]{1,0:T(8,128)(2,1)S(1)} collective-permute-done((bf16[128,768]{1,0:T(8,128)(2,1)S(1)}, bf16[128,768]{1,0:T(8,128)(2,1)S(1)}, u32[]{:S(2)}, u32[]{:S(2)}) %collective-permute-start.22) | collective-permute-done | bytes 196640 | tf_op jit(solution)/shard_map/ppermute | solution.py:30
  92.5 5.4 %collective-permute-start.24 = (bf16[256,768]{1,0:T(8,128)(2,1)S(1)}, bf16[256,768]{1,0:T(8,128)(2,1)S(1)}, u32[]{:S(2)}, u32[]{:S(2)}) collective-permute-start(bf16[256,768]{1,0:T(8,128)(2,1)S(1)} %get-tuple-element.88), channel_id=1, source_target_pairs={{0,248},{8,0},{16,8},{24,16},{32,24},{40,32},{48,40},{56,48},{64,5... | collective-permute-start | bytes 1179656 | tf_op jit(solution)/shard_map/ppermute | solution.py:30
  97.9 2.4 %attend_hop.5 = (f32[512,384]{1,0:T(8,128)S(1)}, f32[512,384]{1,0:T(8,128)S(1)}) custom-call(s32[1]{0:T(128)} %bitcast.1.head, s32[1,16]{1,0:T(1,128)S(1)} %copy-done.18, s32[1]{0:T(128)S(6)} %copy.11.count, bf16[512,384]{1,0:T(8,128)(2,1)S(1)} %project.4.q, bf16[256,768]{1,0:T(8,128)(2,1)S(1)} %collective-permute-done.12.lc.la, ...), custom_call_target="tpu_custom_call" | custom-call | flops 1 | bytes 1 | tf_op jit(solution)/shard_map/attend_hop/pallas_call | solution.py:276
  100.3 3.9 %collective-permute-done.24.left = bf16[256,768]{1,0:T(8,128)(2,1)S(1)} collective-permute-done((bf16[256,768]{1,0:T(8,128)(2,1)S(1)}, bf16[256,768]{1,0:T(8,128)(2,1)S(1)}, u32[]{:S(2)}, u32[]{:S(2)}) %collective-permute-start.24) | collective-permute-done | bytes 393248 | tf_op jit(solution)/shard_map/ppermute | solution.py:30
  104.3 5.5 %collective-permute-done.25.right = bf16[256,768]{1,0:T(8,128)(2,1)S(1)} collective-permute-done((bf16[256,768]{1,0:T(8,128)(2,1)S(1)}, bf16[256,768]{1,0:T(8,128)(2,1)S(1)}, u32[]{:S(2)}, u32[]{:S(2)}) %collective-permute-start.25) | collective-permute-done | bytes 393248 | tf_op jit(solution)/shard_map/ppermute | solution.py:30
  112.1 7.1 %collective-permute-done.27.edge_own = bf16[64,384]{1,0:T(8,128)(2,1)S(1)} collective-permute-done((bf16[64,384]{1,0:T(8,128)(2,1)S(1)}, bf16[64,384]{1,0:T(8,128)(2,1)S(1)}, u32[]{:S(2)}, u32[]{:S(2)}) %collective-permute-start.27) | collective-permute-done | bytes 49184 | tf_op jit(solution)/shard_map/ppermute | solution.py:438
  120.9 4.3 %out_project.1 = (f32[64,3072]{1,0:T(8,128)S(1)}, bf16[64,3072]{1,0:T(8,128)(2,1)S(1)}, bf16[64,3072]{1,0:T(8,128)(2,1)S(1)}, bf16[64,3072]{1,0:T(8,128)(2,1)S(1)}) custom-call(s32[1]{0:T(128)} %bitcast.1.head, s32[1]{0:T(128)} %bitcast.2.window, s32[32]{0:T(128)S(1)} %copy-done.19, bf16[256,384]{1,0:T(8,128)(2,1)S(1)} %get-tuple-element.94.own, ...), custom_call_target="tpu_custom_call" | custom-call | flops 1 | bytes 1 | tf_op jit(solution)/shard_map/out_project/pallas_call | solution.py:371
  125.2 3.1 %collective-permute-start.29 = (bf16[64,3072]{1,0:T(8,128)(2,1)S(1)}, bf16[64,3072]{1,0:T(8,128)(2,1)S(1)}, u32[]{:S(2)}, u32[]{:S(2)}) collective-permute-start(bf16[64,3072]{1,0:T(8,128)(2,1)S(1)} %get-tuple-element.100), channel_id=1, source_target_pairs={{0,2},{1,3},{2,4},{3,5},{4,6},{5,7},{6,0},{7,1},{8,10},{9,11},{10,... | collective-permute-start | bytes 1179656 | tf_op jit(solution)/shard_map/ppermute | solution.py:34
  130.6 11.1 %collective-permute-done.29 = bf16[64,3072]{1,0:T(8,128)(2,1)S(1)} collective-permute-done((bf16[64,3072]{1,0:T(8,128)(2,1)S(1)}, bf16[64,3072]{1,0:T(8,128)(2,1)S(1)}, u32[]{:S(2)}, u32[]{:S(2)}) %collective-permute-start.29) | collective-permute-done | bytes 393248 | tf_op jit(solution)/shard_map/ppermute | solution.py:34
  141.8 3.4 %collective-permute-done.30 = bf16[64,3072]{1,0:T(8,128)(2,1)S(1)} collective-permute-done((bf16[64,3072]{1,0:T(8,128)(2,1)S(1)}, bf16[64,3072]{1,0:T(8,128)(2,1)S(1)}, u32[]{:S(2)}, u32[]{:S(2)}) %collective-permute-start.30) | collective-permute-done | bytes 393248 | tf_op jit(solution)/shard_map/ppermute | solution.py:34
  (97 shorter events, 32.6 us)
Async XLA Ops:
  2.3 17.3 %collective-permute-start.1 = (bf16[64,3072]{1,0:T(8,128)(2,1)S(1)}, bf16[64,3072]{1,0:T(8,128)(2,1)S(1)}, u32[]{:S(2)}, u32[]{:S(2)}) collective-permute-start(bf16[64,3072]{1,0:T(8,128)(2,1)S(1)} %modulate.1.refs_0_), channel_id=1, source_target_pairs={{0,6},{1,7},{2,0},{3,1},{4,2},{5,3},{6,4},{7,5},{8,14},{9,15},{10,... | collective-permute-start | bytes 1179656 | tf_op jit(solution)/shard_map/ppermute | solution.py:34
  3.1 19.6 %collective-permute-start.2 = (bf16[64,3072]{1,0:T(8,128)(2,1)S(1)}, bf16[64,3072]{1,0:T(8,128)(2,1)S(1)}, u32[]{:S(2)}, u32[]{:S(2)}) collective-permute-start(bf16[64,3072]{1,0:T(8,128)(2,1)S(1)} %modulate.1.refs_0_), channel_id=1, source_target_pairs={{0,2},{1,3},{2,4},{3,5},{4,6},{5,7},{6,0},{7,1},{8,10},{9,11},{10,... | collective-permute-start | bytes 1179656 | tf_op jit(solution)/shard_map/ppermute | solution.py:34
  5.6 18.0 %collective-permute-start.3 = (bf16[64,3072]{1,0:T(8,128)(2,1)S(1)}, bf16[64,3072]{1,0:T(8,128)(2,1)S(1)}, u32[]{:S(2)}, u32[]{:S(2)}) collective-permute-start(bf16[64,3072]{1,0:T(8,128)(2,1)S(1)} %modulate.1.refs_0_), channel_id=1, source_target_pairs={{0,4},{1,5},{2,6},{3,7},{4,0},{5,1},{6,2},{7,3},{8,12},{9,13},{10,... | collective-permute-start | bytes 1179656 | tf_op jit(solution)/shard_map/ppermute | solution.py:34
  11.4 12.9 %collective-permute-start.4 = (bf16[128,768]{1,0:T(8,128)(2,1)S(1)}, bf16[128,768]{1,0:T(8,128)(2,1)S(1)}, u32[]{:S(2)}, u32[]{:S(2)}) collective-permute-start(bf16[128,768]{1,0:T(8,128)(2,1)S(1)} %project.3.a), channel_id=1, source_target_pairs={{0,8},{8,16},{16,24},{24,32},{32,40},{40,48},{48,56},{56,64},{64,7... | collective-permute-start | bytes 589832 | tf_op jit(solution)/shard_map/ppermute | solution.py:30
  13.3 11.1 %collective-permute-start.5 = (bf16[128,768]{1,0:T(8,128)(2,1)S(1)}, bf16[128,768]{1,0:T(8,128)(2,1)S(1)}, u32[]{:S(2)}, u32[]{:S(2)}) collective-permute-start(bf16[128,768]{1,0:T(8,128)(2,1)S(1)} %project.3.a), channel_id=1, source_target_pairs={{0,248},{8,0},{16,8},{24,16},{32,24},{40,32},{48,40},{56,48},{64,5... | collective-permute-start | bytes 589832 | tf_op jit(solution)/shard_map/ppermute | solution.py:30
  24.3 9.4 %collective-permute-start.6 = (bf16[64,3072]{1,0:T(8,128)(2,1)S(1)}, bf16[64,3072]{1,0:T(8,128)(2,1)S(1)}, u32[]{:S(2)}, u32[]{:S(2)}) collective-permute-start(bf16[64,3072]{1,0:T(8,128)(2,1)S(1)} %collective-permute-done.1.refs_2_.refs_0_), channel_id=1, source_target_pairs={{0,1},{1,0},{2,3},{3,2},{4,5},{5,4},{6,7},{7,6},{8,9},{9,8},{10,11... | collective-permute-start | bytes 1179656 | tf_op jit(solution)/shard_map/ppermute | solution.py:38
  36.8 16.6 %collective-permute-start.15 = (bf16[384,3072]{1,0:T(8,128)(2,1)S(1)}, bf16[384,3072]{1,0:T(8,128)(2,1)S(1)}, u32[]{:S(2)}, u32[]{:S(2)}) collective-permute-start(bf16[384,3072]{1,0:T(8,128)(2,1)S(1)} %copy-done.2), channel_id=1, source_target_pairs={{0,1},{1,0},{2,3},{3,2},{4,5},{5,4},{6,7},{7,6},{8,9},{9,8},{10,11... | collective-permute-start | bytes 7077896 | tf_op jit(solution)/shard_map/ppermute | solution.py:38
  36.9 16.5 %collective-permute-start.13 = (bf16[256,768]{1,0:T(8,128)(2,1)S(1)}, bf16[256,768]{1,0:T(8,128)(2,1)}, u32[]{:S(2)}, u32[]{:S(2)}) collective-permute-start(bf16[256,768]{1,0:T(8,128)(2,1)S(1)} %get-tuple-element.67.b), channel_id=1, source_target_pairs={{0,8},{8,16},{16,24},{24,32},{32,40},{40,48},{48,56},{56,64},{64,7... | collective-permute-start | bytes 1179656 | tf_op jit(solution)/shard_map/ppermute | solution.py:30
  37.2 16.2 %collective-permute-start.14 = (bf16[256,768]{1,0:T(8,128)(2,1)S(1)}, bf16[256,768]{1,0:T(8,128)(2,1)}, u32[]{:S(2)}, u32[]{:S(2)}) collective-permute-start(bf16[256,768]{1,0:T(8,128)(2,1)S(1)} %get-tuple-element.67.b), channel_id=1, source_target_pairs={{0,248},{8,0},{16,8},{24,16},{32,24},{40,32},{48,40},{56,48},{64,5... | collective-permute-start | bytes 1179656 | tf_op jit(solution)/shard_map/ppermute | solution.py:30
  42.6 18.1 %collective-permute-start.18 = (bf16[256,768]{1,0:T(8,128)(2,1)S(1)}, bf16[256,768]{1,0:T(8,128)(2,1)}, u32[]{:S(2)}, u32[]{:S(2)}) collective-permute-start(bf16[256,768]{1,0:T(8,128)(2,1)S(1)} %get-tuple-element.68.c), channel_id=1, source_target_pairs={{0,8},{8,16},{16,24},{24,32},{32,40},{40,48},{48,56},{56,64},{64,7... | collective-permute-start | bytes 1179656 | tf_op jit(solution)/shard_map/ppermute | solution.py:30
  42.6 18.1 %collective-permute-start.11 = (bf16[256,768]{1,0:T(8,128)(2,1)S(1)}, bf16[256,768]{1,0:T(8,128)(2,1)}, u32[]{:S(2)}, u32[]{:S(2)}) collective-permute-start(bf16[256,768]{1,0:T(8,128)(2,1)S(1)} %get-tuple-element.65), channel_id=1, source_target_pairs={{0,248},{8,0},{16,8},{24,16},{32,24},{40,32},{48,40},{56,48},{64,5... | collective-permute-start | bytes 1179656 | tf_op jit(solution)/shard_map/ppermute | solution.py:30
  54.8 19.1 %collective-permute-start.16 = (bf16[256,768]{1,0:T(8,128)(2,1)}, bf16[256,768]{1,0:T(8,128)(2,1)}, u32[]{:S(2)}, u32[]{:S(2)}) collective-permute-start(bf16[256,768]{1,0:T(8,128)(2,1)} %collective-permute-done.13.rb), channel_id=1, source_target_pairs={{0,8},{8,16},{16,24},{24,32},{32,40},{40,48},{48,56},{56,64},{64,7... | collective-permute-start | bytes 1179656 | tf_op jit(solution)/shard_map/ppermute | solution.py:30
  54.8 19.1 %collective-permute-start.17 = (bf16[256,768]{1,0:T(8,128)(2,1)}, bf16[256,768]{1,0:T(8,128)(2,1)}, u32[]{:S(2)}, u32[]{:S(2)}) collective-permute-start(bf16[256,768]{1,0:T(8,128)(2,1)} %collective-permute-done.14.lb), channel_id=1, source_target_pairs={{0,248},{8,0},{16,8},{24,16},{32,24},{40,32},{48,40},{56,48},{64,5... | collective-permute-start | bytes 1179656 | tf_op jit(solution)/shard_map/ppermute | solution.py:30
  60.6 18.7 %collective-permute-start.21 = (bf16[256,768]{1,0:T(8,128)(2,1)}, bf16[256,768]{1,0:T(8,128)(2,1)S(1)}, u32[]{:S(2)}, u32[]{:S(2)}) collective-permute-start(bf16[256,768]{1,0:T(8,128)(2,1)} %collective-permute-done.18.rc.ra), channel_id=1, source_target_pairs={{0,8},{8,16},{16,24},{24,32},{32,40},{40,48},{48,56},{56,64},{64,7... | collective-permute-start | bytes 1179656 | tf_op jit(solution)/shard_map/ppermute | solution.py:30
  60.7 18.9 %collective-permute-start.12 = (bf16[256,768]{1,0:T(8,128)(2,1)}, bf16[256,768]{1,0:T(8,128)(2,1)S(1)}, u32[]{:S(2)}, u32[]{:S(2)}) collective-permute-start(bf16[256,768]{1,0:T(8,128)(2,1)} %collective-permute-done.11.lc.la), channel_id=1, source_target_pairs={{0,248},{8,0},{16,8},{24,16},{32,24},{40,32},{48,40},{56,48},{64,5... | collective-permute-start | bytes 1179656 | tf_op jit(solution)/shard_map/ppermute | solution.py:30
  74.0 17.9 %collective-permute-start.19 = (bf16[256,768]{1,0:T(8,128)(2,1)}, bf16[256,768]{1,0:T(8,128)(2,1)S(1)}, u32[]{:S(2)}, u32[]{:S(2)}) collective-permute-start(bf16[256,768]{1,0:T(8,128)(2,1)} %collective-permute-done.16.rb), channel_id=1, source_target_pairs={{0,8},{8,16},{16,24},{24,32},{32,40},{40,48},{48,56},{56,64},{64,7... | collective-permute-start | bytes 1179656 | tf_op jit(solution)/shard_map/ppermute | solution.py:30
  74.1 17.8 %collective-permute-start.20 = (bf16[256,768]{1,0:T(8,128)(2,1)}, bf16[256,768]{1,0:T(8,128)(2,1)S(1)}, u32[]{:S(2)}, u32[]{:S(2)}) collective-permute-start(bf16[256,768]{1,0:T(8,128)(2,1)} %collective-permute-done.17.lb), channel_id=1, source_target_pairs={{0,248},{8,0},{16,8},{24,16},{32,24},{40,32},{48,40},{56,48},{64,5... | collective-permute-start | bytes 1179656 | tf_op jit(solution)/shard_map/ppermute | solution.py:30
  79.4 12.4 %collective-permute-start.22 = (bf16[128,768]{1,0:T(8,128)(2,1)S(1)}, bf16[128,768]{1,0:T(8,128)(2,1)S(1)}, u32[]{:S(2)}, u32[]{:S(2)}) collective-permute-start(bf16[128,768]{1,0:T(8,128)(2,1)S(1)} %slice.12), channel_id=1, source_target_pairs={{0,8},{8,16},{16,24},{24,32},{32,40},{40,48},{48,56},{56,64},{64,7... | collective-permute-start | bytes 589832 | tf_op jit(solution)/shard_map/ppermute | solution.py:30
  79.5 12.3 %collective-permute-start.23 = (bf16[128,768]{1,0:T(8,128)(2,1)S(1)}, bf16[128,768]{1,0:T(8,128)(2,1)S(1)}, u32[]{:S(2)}, u32[]{:S(2)}) collective-permute-start(bf16[128,768]{1,0:T(8,128)(2,1)S(1)} %slice.13), channel_id=1, source_target_pairs={{0,248},{8,0},{16,8},{24,16},{32,24},{40,32},{48,40},{56,48},{64,5... | collective-permute-start | bytes 589832 | tf_op jit(solution)/shard_map/ppermute | solution.py:30
  92.5 11.7 %collective-permute-start.24 = (bf16[256,768]{1,0:T(8,128)(2,1)S(1)}, bf16[256,768]{1,0:T(8,128)(2,1)S(1)}, u32[]{:S(2)}, u32[]{:S(2)}) collective-permute-start(bf16[256,768]{1,0:T(8,128)(2,1)S(1)} %get-tuple-element.88), channel_id=1, source_target_pairs={{0,248},{8,0},{16,8},{24,16},{32,24},{40,32},{48,40},{56,48},{64,5... | collective-permute-start | bytes 1179656 | tf_op jit(solution)/shard_map/ppermute | solution.py:30
  97.9 11.9 %collective-permute-start.25 = (bf16[256,768]{1,0:T(8,128)(2,1)S(1)}, bf16[256,768]{1,0:T(8,128)(2,1)S(1)}, u32[]{:S(2)}, u32[]{:S(2)}) collective-permute-start(bf16[256,768]{1,0:T(8,128)(2,1)S(1)} %get-tuple-element.89), channel_id=1, source_target_pairs={{0,8},{8,16},{16,24},{24,32},{32,40},{40,48},{48,56},{56,64},{64,7... | collective-permute-start | bytes 1179656 | tf_op jit(solution)/shard_map/ppermute | solution.py:30
  125.2 16.6 %collective-permute-start.29 = (bf16[64,3072]{1,0:T(8,128)(2,1)S(1)}, bf16[64,3072]{1,0:T(8,128)(2,1)S(1)}, u32[]{:S(2)}, u32[]{:S(2)}) collective-permute-start(bf16[64,3072]{1,0:T(8,128)(2,1)S(1)} %get-tuple-element.100), channel_id=1, source_target_pairs={{0,2},{1,3},{2,4},{3,5},{4,6},{5,7},{6,0},{7,1},{8,10},{9,11},{10,... | collective-permute-start | bytes 1179656 | tf_op jit(solution)/shard_map/ppermute | solution.py:34
  128.3 16.9 %collective-permute-start.30 = (bf16[64,3072]{1,0:T(8,128)(2,1)S(1)}, bf16[64,3072]{1,0:T(8,128)(2,1)S(1)}, u32[]{:S(2)}, u32[]{:S(2)}) collective-permute-start(bf16[64,3072]{1,0:T(8,128)(2,1)S(1)} %get-tuple-element.101), channel_id=1, source_target_pairs={{0,6},{1,7},{2,0},{3,1},{4,2},{5,3},{6,4},{7,5},{8,14},{9,15},{10,... | collective-permute-start | bytes 1179656 | tf_op jit(solution)/shard_map/ppermute | solution.py:34
  128.3 16.9 %collective-permute-start.31 = (bf16[64,3072]{1,0:T(8,128)(2,1)S(1)}, bf16[64,3072]{1,0:T(8,128)(2,1)S(1)}, u32[]{:S(2)}, u32[]{:S(2)}) collective-permute-start(bf16[64,3072]{1,0:T(8,128)(2,1)S(1)} %get-tuple-element.102), channel_id=1, source_target_pairs={{0,4},{1,5},{2,6},{3,7},{4,0},{5,1},{6,2},{7,3},{8,12},{9,13},{10,... | collective-permute-start | bytes 1179656 | tf_op jit(solution)/shard_map/ppermute | solution.py:34
  (29 other events, 232.0 us)

commit v3 on v2

--- a/solution.py
+++ b/solution.py
@@ -13,6 +13,7 @@
 NB = 8
 OV = 64
 ROWS = 64
+NOTE = 16
 D = 3072
 HD = 128
 HEADS = 3
@@ -84,13 +85,14 @@
 
 def kv_kernel(parts, carried, *refs):
     weight, bias, gain = refs[parts : parts + 3]
-    carry = refs[parts + 3 : parts + 3 + carried]
-    outs, mod_ref = refs[parts + 3 + carried : -1], refs[-1]
+    extra = carried or 1
+    carry = refs[parts + 3 : parts + 3 + extra]
+    outs, mod_ref = refs[parts + 3 + extra : -1], refs[-1]
     step = pl.program_id(0)
     split = parts * ROWS - (TILE if carried else 0)
 
     def store(part, cols):
-        outs[0][:, cols] = part[:split]
+        outs[0][:split, cols] = part[:split]
         for out in outs[1:]:
             out[TILE:, cols] = part[split:]
 
@@ -100,6 +102,12 @@
             mod_ref[i * ROWS : (i + 1) * ROWS, :] = refs[i][...]
         for ref, out in zip(carry, outs[1:]):
             out[0:TILE, :] = ref[...]
+        if not carried:
+            lane = lax.broadcasted_iota(jnp.int32, (NOTE, 2 * LW), 1)
+            row = jnp.zeros((NOTE, 2 * LW), jnp.int32)
+            for e in range(2 * NB):
+                row = jnp.where(lane == e, carry[0][0, e], row)
+            outs[0][split:, :] = row.astype(jnp.float32).astype(jnp.bfloat16)
         raw = jnp.dot(mod_ref[...], weight[0], preferred_element_type=jnp.float32)
         for h, part in enumerate(normed_heads(raw + bias[1:2, :], gain[1:2, :])):
             store(part, slice(h * HD, (h + 1) * HD))
@@ -119,29 +127,31 @@
         q_ref[:, h * HD : (h + 1) * HD] = part
 
 
-def project(kernel, first, count, mod, weight, bias, gain, carry=()):
+def project(kernel, first, count, mod, weight, bias, gain, carry=(), tiles=None):
     parts = len(mod)
     rows = parts * ROWS
-    out_rows = [rows - TILE] + [2 * TILE] * len(carry) if carry else [rows]
+    out_rows = [rows - TILE] + [2 * TILE] * len(carry) if carry else [rows + (NOTE if tiles is not None else 0)]
+    noted = [tiles] if tiles is not None else []
     whole = lambda shape: pl.BlockSpec(shape, lambda c: (0,) * len(shape))
     out = pl.pallas_call(
         kernel,
         grid=(count,),
         in_specs=[whole((ROWS, D))] * parts
         + [pl.BlockSpec((1, D, LW), lambda c: (first + c, 0, 0)), whole((3, LW)), whole((2, HD))]
-        + [whole((TILE, 2 * LW))] * len(carry),
+        + [whole((TILE, 2 * LW))] * len(carry)
+        + [SMEM()] * len(noted),
         out_specs=[whole((n, count * LW)) for n in out_rows],
         out_shape=[jax.ShapeDtypeStruct((n, count * LW), jnp.bfloat16) for n in out_rows],
         scratch_shapes=[pltpu.VMEM((rows, D), jnp.bfloat16)],
         compiler_params=pltpu.CompilerParams(vmem_limit_bytes=BIG * MIB),
         cost_estimate=COST,
         name="project",
-    )(*mod, weight, bias, gain, *carry)
+    )(*mod, weight, bias, gain, *carry, *noted)
     return out if carry else out[0]
 
 
-def project_kv(mod, *args, carry=()):
-    return project(functools.partial(kv_kernel, len(mod), len(carry)), 1, 2, mod, *args, carry=carry)
+def project_kv(mod, *args, carry=(), tiles=None):
+    return project(functools.partial(kv_kernel, len(mod), len(carry)), 1, 2, mod, *args, carry=carry, tiles=tiles)
 
 
 def project_q(mod, *args):
@@ -334,54 +344,85 @@
 NCOL = 768
 
 
-def out_kernel(head, window, strips, own, sib, edge_own, edge_sib, w_own, w_sib, o0, o1, o3, o2, a_own, a_sib, e_own, e_sib):
+def strip_of(head, window, strips):
     core = head[0] & 1
-    place = place_of(3 * core, head[0])
-    shared = strips[(window[0] + core + WINDOWS - 1) & (WINDOWS - 1)]
-    top = 1 - core
-
+    return place_of(3 * core, head[0]), strips[(window[0] + core + WINDOWS - 1) & (WINDOWS - 1)], 1 - core
+
+
+def halve_shared(a, rows, place, shared, top):
+    a[...] = rows[...]
+    row = lax.broadcasted_iota(jnp.int32, (ROWS, 1), 0)
+    low = jnp.where(top == 1, 0, OV - shared)
+    keep = jnp.where(jnp.logical_and(row >= low, row < low + shared), 0.5, 1.0)
+    at = pl.ds(pl.multiple_of(place * ROWS, ROWS), ROWS)
+    a[at, :] = (rows[at, :].astype(jnp.float32) * keep).astype(jnp.bfloat16)
+
+
+dot = functools.partial(jnp.dot, preferred_element_type=jnp.float32)
+
+
+def out_own_kernel(head, window, strips, own, w_own, part, a_own):
     @pl.when(pl.program_id(0) == 0)
     def _():
-        a_own[...] = own[...]
-        a_sib[...] = sib[...]
-        row = lax.broadcasted_iota(jnp.int32, (ROWS, 1), 0)
-        low = jnp.where(top == 1, 0, OV - shared)
-        keep = jnp.where(jnp.logical_and(row >= low, row < low + shared), 0.5, 1.0)
-        at = pl.ds(pl.multiple_of(place * ROWS, ROWS), ROWS)
-        a_own[at, :] = (own[at, :].astype(jnp.float32) * keep).astype(jnp.bfloat16)
-        a_sib[at, :] = (sib[at, :].astype(jnp.float32) * keep).astype(jnp.bfloat16)
+        halve_shared(a_own, own, *strip_of(head, window, strips))
+
+    part[...] = dot(a_own[...], w_own[...])
+
+
+def out_kernel(head, window, strips, part, sib, edge_own, edge_sib, w_own, w_sib, o0, o1, o3, o2, a_sib, e_own, e_sib):
+    place, shared, top = strip_of(head, window, strips)
+
+    @pl.when(pl.program_id(0) == 0)
+    def _():
+        halve_shared(a_sib, sib, place, shared, top)
         i = lax.broadcasted_iota(jnp.int32, (ROWS, ROWS), 0)
         j = lax.broadcasted_iota(jnp.int32, (ROWS, ROWS), 1)
         offset = jnp.where(top == 1, OV - shared, shared - OV)
         shift = jnp.where(j == i + offset, 0.5, 0.0).astype(jnp.bfloat16)
-        e_own[...] = jnp.dot(shift, edge_own[...], preferred_element_type=jnp.float32).astype(jnp.bfloat16)
-        e_sib[...] = jnp.dot(shift, edge_sib[...], preferred_element_type=jnp.float32).astype(jnp.bfloat16)
-
-    dot = functools.partial(jnp.dot, preferred_element_type=jnp.float32)
-    main = dot(a_own[...], w_own[...]) + dot(a_sib[...], w_sib[...])
+        e_own[...] = dot(shift, edge_own[...]).astype(jnp.bfloat16)
+        e_sib[...] = dot(shift, edge_sib[...]).astype(jnp.bfloat16)
+
+    main = part[...] + dot(a_sib[...], w_sib[...])
     extra = dot(e_own[...], w_own[...]) + dot(e_sib[...], w_sib[...])
     for k, ref in enumerate((o0, o1, o3, o2)):
         block = main[k * ROWS : (k + 1) * ROWS]
         ref[...] = (block + jnp.where(place == k, extra, 0.0)).astype(ref.dtype)
 
 
-def out_project(head, window, strips, own, sib, edge_own, edge_sib, w_own, w_sib):
-    cols = lambda rows: pl.BlockSpec((rows, NCOL), lambda i: (0, i))
+def out_cols(rows):
+    return pl.BlockSpec((rows, NCOL), lambda i: (0, i))
+
+
+def out_own(head, window, strips, own, w_own):
+    return pl.pallas_call(
+        out_own_kernel,
+        grid=(D // NCOL,),
+        in_specs=[SMEM()] * 3 + [whole_spec((256, LW)), out_cols(LW)],
+        out_specs=out_cols(256),
+        out_shape=jax.ShapeDtypeStruct((256, D), jnp.float32),
+        scratch_shapes=[pltpu.VMEM((256, LW), jnp.bfloat16)],
+        compiler_params=pltpu.CompilerParams(vmem_limit_bytes=BIG * MIB),
+        cost_estimate=COST,
+        name="out_own",
+    )(head, window, strips, own, w_own)
+
+
+def out_project(head, window, strips, part, sib, edge_own, edge_sib, w_own, w_sib):
     sent = jax.ShapeDtypeStruct((ROWS, D), jnp.bfloat16)
     return pl.pallas_call(
         out_kernel,
         grid=(D // NCOL,),
         in_specs=[SMEM()] * 3
-        + [whole_spec((256, LW))] * 2
+        + [out_cols(256), whole_spec((256, LW))]
         + [whole_spec((ROWS, LW))] * 2
-        + [cols(LW)] * 2,
-        out_specs=[cols(ROWS)] * 4,
+        + [out_cols(LW)] * 2,
+        out_specs=[out_cols(ROWS)] * 4,
         out_shape=[jax.ShapeDtypeStruct((ROWS, D), jnp.float32), sent, sent, sent],
-        scratch_shapes=[pltpu.VMEM((256, LW), jnp.bfloat16)] * 2 + [pltpu.VMEM((ROWS, LW), jnp.bfloat16)] * 2,
-        compiler_params=pltpu.CompilerParams(vmem_limit_bytes=24 * MIB),
+        scratch_shapes=[pltpu.VMEM((256, LW), jnp.bfloat16)] + [pltpu.VMEM((ROWS, LW), jnp.bfloat16)] * 2,
+        compiler_params=pltpu.CompilerParams(vmem_limit_bytes=BIG * MIB),
         cost_estimate=COST,
         name="out_project",
-    )(head, window, strips, own, sib, edge_own, edge_sib, w_own, w_sib)
+    )(head, window, strips, part, sib, edge_own, edge_sib, w_own, w_sib)
 
 
 def shards(
@@ -406,12 +447,10 @@
     sib0 = swap_core(mod0)
     mod1, mod3 = to_y(mod0, -1), to_y(mod0, 1)
     mod2 = to_y(mod0, 2)
-    kv_a = project_kv([mod0, sib0], *args)
+    kv_a = project_kv([mod0, sib0], *args, tiles=key_tiles)
     ra1, la1 = along_win(kv_a, 1), along_win(kv_a, -1)
-    mod1, mod3, mod2, ra1, la1, wanted = barrier((mod1, mod3, mod2, ra1, la1, key_tiles))
+    mod1, mod3, mod2, ra1, la1 = barrier((mod1, mod3, mod2, ra1, la1))
     sib1, sib3, sib2 = swap_core(mod1), swap_core(mod3), swap_core(mod2)
-    tiles_next, tiles_prev = along_win(wanted, -1), along_win(wanted, 1)
-    sib1, sib3, sib2, tiles_next, tiles_prev = barrier((sib1, sib3, sib2, tiles_next, tiles_prev))
     kv_b, right_ac, left_ac = project_kv([mod1, sib1, mod3, sib3, mod2, sib2], *args, carry=(ra1, la1))
     rb1, lb1 = along_win(kv_b, 1), along_win(kv_b, -1)
     rac2, lac2 = along_win(right_ac, 1), along_win(left_ac, -1)
@@ -430,6 +469,7 @@
     num, den = attend_hop(2, (0, 1), *hop_args, (lac2, lb2, lac3), (rac2, rb2, rac3), num, den)
     rb3, lb3, rc3, lc3, num, den = barrier((rb3, lb3, rc3, lc3, num, den))
     right, left = (rac3, rb3, rc3), (lac3, lb3, lc3)
+    tiles_prev, tiles_next = (x[TILE : TILE + 1, : 2 * NB].astype(jnp.int32) for x in (ra1, la1))
     last_left, last_right = select_tiles(head, tiles_prev, tiles_next, left, right)
     last_left, last_right = along_win(last_left, -1), along_win(last_right, 1)
     num, den = attend_hop(3, (0, 0), *hop_args, right=right, left=left, num=num, den=den)
@@ -438,7 +478,9 @@
     edge_own = lax.ppermute(edge_a, ("win", "head"), strip_pairs(0))
     edge_sib = lax.ppermute(edge_b, ("win", "head"), strip_pairs(1))
     sib = swap_core(sib)
-    o0, o1, o3, o2 = out_project(head, window, strip_rows, own, sib, edge_own, edge_sib, out_weight, w_sib)
+    part = out_own(head, window, strip_rows, own, out_weight)
+    part, edge_own, edge_sib, sib = barrier((part, edge_own, edge_sib, sib))
+    o0, o1, o3, o2 = out_project(head, window, strip_rows, part, sib, edge_own, edge_sib, out_weight, w_sib)
     total = o0
     for part in (to_y(o1, 1), to_y(o3, -1), to_y(o2, 2)):
         total = total + part.astype(jnp.float32)

time: 147 us -> 139 us (0.946)
  starting transfers between devices: 62.7 us -> 55.2 us
  Pallas kernels: 23.8 us -> 25.9 us
    ppermute x18 -> x16, starting transfers between devices: 53.2 us -> 45.6 us  [along_win(): lax.ppermute(value, 'win', [(i, (i + steps) % WINDOWS) for i in range(WIN...]
    ppermute x1, waiting for transfers between devices: 7.13 us -> 4.71 us  [shards(): edge_own = lax.ppermute(edge_a, ('win', 'head'), strip_pairs(0))]
    ppermute x6, waiting for transfers between devices: 0.02 us -> 2.24 us  [swap_core(): return lax.ppermute(value, 'head', [(h, h ^ 1) for h in range(GROUPS)])]
    pallas_call x1 -> x2, Pallas kernels: 4.3 us -> 5.93 us  [the longest x1 3.55 us: out_project(): pl.pallas_call(out_kernel, grid=(D // NCOL,), in_specs=[SMEM()] * 3 + [ou...]
    unnamed x42 -> x44, local copies, waits for them, and re-layouts: 15.1 us -> 14.2 us
    ppermute x18 -> x16, waiting for transfers between devices: 16 us -> 16.5 us  [along_win(): lax.ppermute(value, 'win', [(i, (i + steps) % WINDOWS) for i in range(WIN...]
  transfers between devices with their start and end apart: 32 -> 30, of which waited for: 11 -> 13; matrix products, arithmetic and copies ran while one was open for 1% -> 1% of each run, Pallas kernels for 9% -> 12%
where the time goes in v3:
time: 139 us
  starting transfers between devices  55.2 us (40%)
  waiting for transfers between devices  40.8 us (29%)
  Pallas kernels  25.9 us (19%)
  local copies, waits for them, and re-layouts  15 us (11%)
    ppermute x16, starting transfers between devices, along_win(): lax.ppermute(value, 'win', [(i, (i + steps) % WINDOWS) for i in range(WIN...  45.6 us
    ppermute x6, waiting for transfers between devices, to_y(): lax.ppermute(value, 'head', [(h, (h // 2 + steps) % 4 * 2 + h % 2) for h...  17.4 us
    ppermute x16, waiting for transfers between devices, along_win(): lax.ppermute(value, 'win', [(i, (i + steps) % WINDOWS) for i in range(WIN...  16.5 us
    unnamed x44, local copies, waits for them, and re-layouts  14.2 us
    pallas_call x3, Pallas kernels, attend_hop(): pl.pallas_call(functools.partial(hop_kernel, 4 * (hop - 1)), grid=(512 //...  8.76 us
    ppermute x6, starting transfers between devices, to_y(): lax.ppermute(value, 'head', [(h, (h // 2 + steps) % 4 * 2 + h % 2) for h...  8.07 us
    pallas_call x3, Pallas kernels, project(): pl.pallas_call(kernel, grid=(count,), in_specs=[whole((ROWS, D))] * parts...  6.76 us
    ppermute x1, waiting for transfers between devices, shards(): edge_own = lax.ppermute(edge_a, ('win', 'head'), strip_pairs(0))  4.71 us
  transfers between devices with their start and end apart: 30, of which 13 were waited for; matrix products, arithmetic and copies ran while one was open for 1% of the time, Pallas kernels for 12%

profile of v3, /device:TPU:24, one launch (start us, length us, event | category | flops | bytes accessed | tf_op | source)
XLA Modules:
  0.0 139.0 jit_solution(9756650368756261900)
XLA Ops:
  3.1 2.5 %collective-permute-start.2 = (bf16[64,3072]{1,0:T(8,128)(2,1)S(1)}, bf16[64,3072]{1,0:T(8,128)(2,1)S(1)}, u32[]{:S(2)}, u32[]{:S(2)}) collective-permute-start(bf16[64,3072]{1,0:T(8,128)(2,1)S(1)} %modulate.1.refs_0_), channel_id=1, source_target_pairs={{0,2},{1,3},{2,4},{3,5},{4,6},{5,7},{6,0},{7,1},{8,10},{9,11},{10,... | collective-permute-start | bytes 1179656 | tf_op jit(solution)/shard_map/ppermute | solution.py:35
  5.8 3.0 %copy-done = bf16[3072,3,384]{2,0,1:T(8,128)(2,1)S(1)} copy-done((bf16[3072,3,384]{2,0,1:T(8,128)(2,1)S(1)}, bf16[3072,3,384]{2,0,1:T(8,128)(2,1)}, u32[]{:S(2)}) %copy-start) | copy-done | bytes 7077912
  14.5 6.2 %collective-permute-start.5 = (bf16[144,768]{1,0:T(8,128)(2,1)S(1)}, bf16[144,768]{1,0:T(8,128)(2,1)S(1)}, u32[]{:S(2)}, u32[]{:S(2)}) collective-permute-start(bf16[144,768]{1,0:T(8,128)(2,1)S(1)} %project.3.a), channel_id=1, source_target_pairs={{0,248},{8,0},{16,8},{24,16},{32,24},{40,32},{48,40},{56,48},{64,5... | collective-permute-start | bytes 663560 | tf_op jit(solution)/shard_map/ppermute | solution.py:31
  23.6 2.5 %collective-permute-done.4.refs_9_.ra = bf16[144,768]{1,0:T(8,128)(2,1)S(1)} collective-permute-done((bf16[144,768]{1,0:T(8,128)(2,1)S(1)}, bf16[144,768]{1,0:T(8,128)(2,1)S(1)}, u32[]{:S(2)}, u32[]{:S(2)}) %collective-permute-start.4) | collective-permute-done | bytes 221216 | tf_op jit(solution)/shard_map/ppermute | solution.py:31
  29.0 3.0 %project.5 = (bf16[256,768]{1,0:T(8,128)(2,1)S(1)}, bf16[256,768]{1,0:T(8,128)(2,1)S(1)}, bf16[256,768]{1,0:T(8,128)(2,1)S(1)}) custom-call(bf16[64,3072]{1,0:T(8,128)(2,1)S(1)} %collective-permute-done.1.refs_2_.refs_0_, bf16[64,3072]{1,0:T(8,128)(2,1)S(1)} %collective-permute-done.6.refs_3_.refs_1_, ...), custom_call_target="tpu_custom_call" | custom-call | flops 1 | bytes 1 | tf_op jit(solution)/shard_map/project/pallas_call | solution.py:136
  32.2 5.5 %collective-permute-start.12 = (bf16[256,768]{1,0:T(8,128)(2,1)S(1)}, bf16[256,768]{1,0:T(8,128)(2,1)}, u32[]{:S(2)}, u32[]{:S(2)}) collective-permute-start(bf16[256,768]{1,0:T(8,128)(2,1)S(1)} %get-tuple-element.59.b), channel_id=1, source_target_pairs={{0,248},{8,0},{16,8},{24,16},{32,24},{40,32},{48,40},{56,48},{64,5... | collective-permute-start | bytes 1179656 | tf_op jit(solution)/shard_map/ppermute | solution.py:31
  37.7 5.3 %collective-permute-start.9 = (bf16[256,768]{1,0:T(8,128)(2,1)S(1)}, bf16[256,768]{1,0:T(8,128)(2,1)}, u32[]{:S(2)}, u32[]{:S(2)}) collective-permute-start(bf16[256,768]{1,0:T(8,128)(2,1)S(1)} %get-tuple-element.57), channel_id=1, source_target_pairs={{0,248},{8,0},{16,8},{24,16},{32,24},{40,32},{48,40},{56,48},{64,5... | collective-permute-start | bytes 1179656 | tf_op jit(solution)/shard_map/ppermute | solution.py:31
  50.0 5.3 %collective-permute-start.15 = (bf16[256,768]{1,0:T(8,128)(2,1)}, bf16[256,768]{1,0:T(8,128)(2,1)}, u32[]{:S(2)}, u32[]{:S(2)}) collective-permute-start(bf16[256,768]{1,0:T(8,128)(2,1)} %collective-permute-done.12.lb), channel_id=1, source_target_pairs={{0,248},{8,0},{16,8},{24,16},{32,24},{40,32},{48,40},{56,48},{64,5... | collective-permute-start | bytes 1179656 | tf_op jit(solution)/shard_map/ppermute | solution.py:31
  56.0 5.3 %collective-permute-start.10 = (bf16[256,768]{1,0:T(8,128)(2,1)}, bf16[256,768]{1,0:T(8,128)(2,1)S(1)}, u32[]{:S(2)}, u32[]{:S(2)}) collective-permute-start(bf16[256,768]{1,0:T(8,128)(2,1)} %collective-permute-done.9.lc.la), channel_id=1, source_target_pairs={{0,248},{8,0},{16,8},{24,16},{32,24},{40,32},{48,40},{56,48},{64,5... | collective-permute-start | bytes 1179656 | tf_op jit(solution)/shard_map/ppermute | solution.py:31
  66.1 3.2 %attend_hop.3 = (f32[512,384]{1,0:T(8,128)S(1)}, f32[512,384]{1,0:T(8,128)S(1)}) custom-call(s32[1]{0:T(128)} %bitcast.1.head, s32[1,16]{1,0:T(1,128)S(1)} %copy-done.19, s32[1]{0:T(128)S(6)} %copy.11.count, bf16[512,384]{1,0:T(8,128)(2,1)S(1)} %project.4.q, bf16[144,768]{1,0:T(8,128)(2,1)S(1)} %copy-done.10, bf16[256,768]{1,0:T(8,128)(2,1)} %collective-permute-done.12.lb, ...), custom_call_target="tpu_custom_call" | custom-call | flops 1 | bytes 1 | tf_op jit(solution)/shard_map/attend_hop/pallas_call | solution.py:286
  69.4 5.3 %collective-permute-start.18 = (bf16[256,768]{1,0:T(8,128)(2,1)}, bf16[256,768]{1,0:T(8,128)(2,1)S(1)}, u32[]{:S(2)}, u32[]{:S(2)}) collective-permute-start(bf16[256,768]{1,0:T(8,128)(2,1)} %collective-permute-done.15.lb), channel_id=1, source_target_pairs={{0,248},{8,0},{16,8},{24,16},{32,24},{40,32},{48,40},{56,48},{64,5... | collective-permute-start | bytes 1179656 | tf_op jit(solution)/shard_map/ppermute | solution.py:31
  74.9 5.4 %collective-permute-start.21 = (bf16[128,768]{1,0:T(8,128)(2,1)S(1)}, bf16[128,768]{1,0:T(8,128)(2,1)S(1)}, u32[]{:S(2)}, u32[]{:S(2)}) collective-permute-start(bf16[128,768]{1,0:T(8,128)(2,1)S(1)} %slice.21), channel_id=1, source_target_pairs={{0,248},{8,0},{16,8},{24,16},{32,24},{40,32},{48,40},{56,48},{64,5... | collective-permute-start | bytes 589832 | tf_op jit(solution)/shard_map/ppermute | solution.py:31
  80.3 3.2 %attend_hop.4 = (f32[512,384]{1,0:T(8,128)S(1)}, f32[512,384]{1,0:T(8,128)S(1)}) custom-call(s32[1]{0:T(128)} %bitcast.1.head, s32[1,16]{1,0:T(1,128)S(1)} %copy-done.19, s32[1]{0:T(128)S(6)} %copy.11.count, bf16[512,384]{1,0:T(8,128)(2,1)S(1)} %project.4.q, bf16[256,768]{1,0:T(8,128)(2,1)} %collective-permute-done.9.lc.la, ...), custom_call_target="tpu_custom_call" | custom-call | flops 1 | bytes 1 | tf_op jit(solution)/shard_map/attend_hop/pallas_call | solution.py:286
  83.5 3.8 %collective-permute-done.20.rc = bf16[128,768]{1,0:T(8,128)(2,1)S(1)} collective-permute-done((bf16[128,768]{1,0:T(8,128)(2,1)S(1)}, bf16[128,768]{1,0:T(8,128)(2,1)S(1)}, u32[]{:S(2)}, u32[]{:S(2)}) %collective-permute-start.20) | collective-permute-done | bytes 196640 | tf_op jit(solution)/shard_map/ppermute | solution.py:31
  88.0 5.1 %collective-permute-start.22 = (bf16[256,768]{1,0:T(8,128)(2,1)S(1)}, bf16[256,768]{1,0:T(8,128)(2,1)S(1)}, u32[]{:S(2)}, u32[]{:S(2)}) collective-permute-start(bf16[256,768]{1,0:T(8,128)(2,1)S(1)} %get-tuple-element.80), channel_id=1, source_target_pairs={{0,248},{8,0},{16,8},{24,16},{32,24},{40,32},{48,40},{56,48},{64,5... | collective-permute-start | bytes 1179656 | tf_op jit(solution)/shard_map/ppermute | solution.py:31
  93.1 2.4 %attend_hop.5 = (f32[512,384]{1,0:T(8,128)S(1)}, f32[512,384]{1,0:T(8,128)S(1)}) custom-call(s32[1]{0:T(128)} %bitcast.1.head, s32[1,16]{1,0:T(1,128)S(1)} %copy-done.19, s32[1]{0:T(128)S(6)} %copy.11.count, bf16[512,384]{1,0:T(8,128)(2,1)S(1)} %project.4.q, bf16[256,768]{1,0:T(8,128)(2,1)S(1)} %collective-permute-done.10.lc.la, ...), custom_call_target="tpu_custom_call" | custom-call | flops 1 | bytes 1 | tf_op jit(solution)/shard_map/attend_hop/pallas_call | solution.py:286
  95.5 4.0 %collective-permute-done.22.left = bf16[256,768]{1,0:T(8,128)(2,1)S(1)} collective-permute-done((bf16[256,768]{1,0:T(8,128)(2,1)S(1)}, bf16[256,768]{1,0:T(8,128)(2,1)S(1)}, u32[]{:S(2)}, u32[]{:S(2)}) %collective-permute-start.22) | collective-permute-done | bytes 393248 | tf_op jit(solution)/shard_map/ppermute | solution.py:31
  99.6 5.5 %collective-permute-done.23.right = bf16[256,768]{1,0:T(8,128)(2,1)S(1)} collective-permute-done((bf16[256,768]{1,0:T(8,128)(2,1)S(1)}, bf16[256,768]{1,0:T(8,128)(2,1)S(1)}, u32[]{:S(2)}, u32[]{:S(2)}) %collective-permute-start.23) | collective-permute-done | bytes 393248 | tf_op jit(solution)/shard_map/ppermute | solution.py:31
  107.4 2.4 %out_own.1.part = f32[256,3072]{1,0:T(8,128)S(1)} custom-call(s32[1]{0:T(128)} %bitcast.1.head, s32[1]{0:T(128)} %bitcast.2.window, s32[32]{0:T(128)S(1)} %copy-done.20, bf16[256,384]{1,0:T(8,128)(2,1)S(1)} %get-tuple-element.86.own, bf16[384,3072]{1,0:T(8,128)(2,1)S(1)} %copy-done.2), custom_call_target="tpu_custom_call" | custom-call | flops 1 | bytes 1 | tf_op jit(solution)/shard_map/out_own/pallas_call | solution.py:397
  109.8 4.7 %collective-permute-done.24.edge_own = bf16[64,384]{1,0:T(8,128)(2,1)S(1)} collective-permute-done((bf16[64,384]{1,0:T(8,128)(2,1)S(1)}, bf16[64,384]{1,0:T(8,128)(2,1)S(1)}, u32[]{:S(2)}, u32[]{:S(2)}) %collective-permute-start.24) | collective-permute-done | bytes 49184 | tf_op jit(solution)/shard_map/ppermute | solution.py:478
  114.5 3.5 %out_project.1 = (f32[64,3072]{1,0:T(8,128)S(1)}, bf16[64,3072]{1,0:T(8,128)(2,1)S(1)}, bf16[64,3072]{1,0:T(8,128)(2,1)S(1)}, bf16[64,3072]{1,0:T(8,128)(2,1)S(1)}) custom-call(s32[1]{0:T(128)} %bitcast.1.head, s32[1]{0:T(128)} %bitcast.2.window, s32[32]{0:T(128)S(1)} %copy-done.20, f32[256,3072]{1,0:T(8,128)S(1)} %out_own.1.part, ...), custom_call_target="tpu_custom_call" | custom-call | flops 1 | bytes 1 | tf_op jit(solution)/shard_map/out_project/pallas_call | solution.py:412
  118.1 3.0 %collective-permute-start.27 = (bf16[64,3072]{1,0:T(8,128)(2,1)S(1)}, bf16[64,3072]{1,0:T(8,128)(2,1)S(1)}, u32[]{:S(2)}, u32[]{:S(2)}) collective-permute-start(bf16[64,3072]{1,0:T(8,128)(2,1)S(1)} %get-tuple-element.96), channel_id=1, source_target_pairs={{0,2},{1,3},{2,4},{3,5},{4,6},{5,7},{6,0},{7,1},{8,10},{9,11},{10,... | collective-permute-start | bytes 1179656 | tf_op jit(solution)/shard_map/ppermute | solution.py:35
  123.5 11.1 %collective-permute-done.27 = bf16[64,3072]{1,0:T(8,128)(2,1)S(1)} collective-permute-done((bf16[64,3072]{1,0:T(8,128)(2,1)S(1)}, bf16[64,3072]{1,0:T(8,128)(2,1)S(1)}, u32[]{:S(2)}, u32[]{:S(2)}) %collective-permute-start.27) | collective-permute-done | bytes 393248 | tf_op jit(solution)/shard_map/ppermute | solution.py:35
  134.6 3.4 %collective-permute-done.28 = bf16[64,3072]{1,0:T(8,128)(2,1)S(1)} collective-permute-done((bf16[64,3072]{1,0:T(8,128)(2,1)S(1)}, bf16[64,3072]{1,0:T(8,128)(2,1)S(1)}, u32[]{:S(2)}, u32[]{:S(2)}) %collective-permute-start.28) | collective-permute-done | bytes 393248 | tf_op jit(solution)/shard_map/ppermute | solution.py:35
  (97 shorter events, 33.2 us)
Async XLA Ops:
  2.3 18.5 %collective-permute-start.1 = (bf16[64,3072]{1,0:T(8,128)(2,1)S(1)}, bf16[64,3072]{1,0:T(8,128)(2,1)S(1)}, u32[]{:S(2)}, u32[]{:S(2)}) collective-permute-start(bf16[64,3072]{1,0:T(8,128)(2,1)S(1)} %modulate.1.refs_0_), channel_id=1, source_target_pairs={{0,6},{1,7},{2,0},{3,1},{4,2},{5,3},{6,4},{7,5},{8,14},{9,15},{10,... | collective-permute-start | bytes 1179656 | tf_op jit(solution)/shard_map/ppermute | solution.py:35
  3.1 19.6 %collective-permute-start.2 = (bf16[64,3072]{1,0:T(8,128)(2,1)S(1)}, bf16[64,3072]{1,0:T(8,128)(2,1)S(1)}, u32[]{:S(2)}, u32[]{:S(2)}) collective-permute-start(bf16[64,3072]{1,0:T(8,128)(2,1)S(1)} %modulate.1.refs_0_), channel_id=1, source_target_pairs={{0,2},{1,3},{2,4},{3,5},{4,6},{5,7},{6,0},{7,1},{8,10},{9,11},{10,... | collective-permute-start | bytes 1179656 | tf_op jit(solution)/shard_map/ppermute | solution.py:35
  5.6 18.0 %collective-permute-start.3 = (bf16[64,3072]{1,0:T(8,128)(2,1)S(1)}, bf16[64,3072]{1,0:T(8,128)(2,1)S(1)}, u32[]{:S(2)}, u32[]{:S(2)}) collective-permute-start(bf16[64,3072]{1,0:T(8,128)(2,1)S(1)} %modulate.1.refs_0_), channel_id=1, source_target_pairs={{0,4},{1,5},{2,6},{3,7},{4,0},{5,1},{6,2},{7,3},{8,12},{9,13},{10,... | collective-permute-start | bytes 1179656 | tf_op jit(solution)/shard_map/ppermute | solution.py:35
  12.6 13.4 %collective-permute-start.4 = (bf16[144,768]{1,0:T(8,128)(2,1)S(1)}, bf16[144,768]{1,0:T(8,128)(2,1)S(1)}, u32[]{:S(2)}, u32[]{:S(2)}) collective-permute-start(bf16[144,768]{1,0:T(8,128)(2,1)S(1)} %project.3.a), channel_id=1, source_target_pairs={{0,8},{8,16},{16,24},{24,32},{32,40},{40,48},{48,56},{56,64},{64,7... | collective-permute-start | bytes 663560 | tf_op jit(solution)/shard_map/ppermute | solution.py:31
  14.5 11.6 %collective-permute-start.5 = (bf16[144,768]{1,0:T(8,128)(2,1)S(1)}, bf16[144,768]{1,0:T(8,128)(2,1)S(1)}, u32[]{:S(2)}, u32[]{:S(2)}) collective-permute-start(bf16[144,768]{1,0:T(8,128)(2,1)S(1)} %project.3.a), channel_id=1, source_target_pairs={{0,248},{8,0},{16,8},{24,16},{32,24},{40,32},{48,40},{56,48},{64,5... | collective-permute-start | bytes 663560 | tf_op jit(solution)/shard_map/ppermute | solution.py:31
  32.0 16.6 %collective-permute-start.13 = (bf16[384,3072]{1,0:T(8,128)(2,1)S(1)}, bf16[384,3072]{1,0:T(8,128)(2,1)S(1)}, u32[]{:S(2)}, u32[]{:S(2)}) collective-permute-start(bf16[384,3072]{1,0:T(8,128)(2,1)S(1)} %copy-done.2), channel_id=1, source_target_pairs={{0,1},{1,0},{2,3},{3,2},{4,5},{5,4},{6,7},{7,6},{8,9},{9,8},{10,11... | collective-permute-start | bytes 7077896 | tf_op jit(solution)/shard_map/ppermute | solution.py:39
  32.2 16.3 %collective-permute-start.11 = (bf16[256,768]{1,0:T(8,128)(2,1)S(1)}, bf16[256,768]{1,0:T(8,128)(2,1)}, u32[]{:S(2)}, u32[]{:S(2)}) collective-permute-start(bf16[256,768]{1,0:T(8,128)(2,1)S(1)} %get-tuple-element.59.b), channel_id=1, source_target_pairs={{0,8},{8,16},{16,24},{24,32},{32,40},{40,48},{48,56},{56,64},{64,7... | collective-permute-start | bytes 1179656 | tf_op jit(solution)/shard_map/ppermute | solution.py:31
  32.2 16.3 %collective-permute-start.12 = (bf16[256,768]{1,0:T(8,128)(2,1)S(1)}, bf16[256,768]{1,0:T(8,128)(2,1)}, u32[]{:S(2)}, u32[]{:S(2)}) collective-permute-start(bf16[256,768]{1,0:T(8,128)(2,1)S(1)} %get-tuple-element.59.b), channel_id=1, source_target_pairs={{0,248},{8,0},{16,8},{24,16},{32,24},{40,32},{48,40},{56,48},{64,5... | collective-permute-start | bytes 1179656 | tf_op jit(solution)/shard_map/ppermute | solution.py:31
  37.7 18.2 %collective-permute-start.16 = (bf16[256,768]{1,0:T(8,128)(2,1)S(1)}, bf16[256,768]{1,0:T(8,128)(2,1)}, u32[]{:S(2)}, u32[]{:S(2)}) collective-permute-start(bf16[256,768]{1,0:T(8,128)(2,1)S(1)} %get-tuple-element.60.c), channel_id=1, source_target_pairs={{0,8},{8,16},{16,24},{24,32},{32,40},{40,48},{48,56},{56,64},{64,7... | collective-permute-start | bytes 1179656 | tf_op jit(solution)/shard_map/ppermute | solution.py:31
  37.7 18.2 %collective-permute-start.9 = (bf16[256,768]{1,0:T(8,128)(2,1)S(1)}, bf16[256,768]{1,0:T(8,128)(2,1)}, u32[]{:S(2)}, u32[]{:S(2)}) collective-permute-start(bf16[256,768]{1,0:T(8,128)(2,1)S(1)} %get-tuple-element.57), channel_id=1, source_target_pairs={{0,248},{8,0},{16,8},{24,16},{32,24},{40,32},{48,40},{56,48},{64,5... | collective-permute-start | bytes 1179656 | tf_op jit(solution)/shard_map/ppermute | solution.py:31
  50.0 19.3 %collective-permute-start.14 = (bf16[256,768]{1,0:T(8,128)(2,1)}, bf16[256,768]{1,0:T(8,128)(2,1)}, u32[]{:S(2)}, u32[]{:S(2)}) collective-permute-start(bf16[256,768]{1,0:T(8,128)(2,1)} %collective-permute-done.11.rb), channel_id=1, source_target_pairs={{0,8},{8,16},{16,24},{24,32},{32,40},{40,48},{48,56},{56,64},{64,7... | collective-permute-start | bytes 1179656 | tf_op jit(solution)/shard_map/ppermute | solution.py:31
  50.0 19.3 %collective-permute-start.15 = (bf16[256,768]{1,0:T(8,128)(2,1)}, bf16[256,768]{1,0:T(8,128)(2,1)}, u32[]{:S(2)}, u32[]{:S(2)}) collective-permute-start(bf16[256,768]{1,0:T(8,128)(2,1)} %collective-permute-done.12.lb), channel_id=1, source_target_pairs={{0,248},{8,0},{16,8},{24,16},{32,24},{40,32},{48,40},{56,48},{64,5... | collective-permute-start | bytes 1179656 | tf_op jit(solution)/shard_map/ppermute | solution.py:31
  56.0 18.8 %collective-permute-start.19 = (bf16[256,768]{1,0:T(8,128)(2,1)}, bf16[256,768]{1,0:T(8,128)(2,1)S(1)}, u32[]{:S(2)}, u32[]{:S(2)}) collective-permute-start(bf16[256,768]{1,0:T(8,128)(2,1)} %collective-permute-done.16.rc.ra), channel_id=1, source_target_pairs={{0,8},{8,16},{16,24},{24,32},{32,40},{40,48},{48,56},{56,64},{64,7... | collective-permute-start | bytes 1179656 | tf_op jit(solution)/shard_map/ppermute | solution.py:31
  56.0 18.9 %collective-permute-start.10 = (bf16[256,768]{1,0:T(8,128)(2,1)}, bf16[256,768]{1,0:T(8,128)(2,1)S(1)}, u32[]{:S(2)}, u32[]{:S(2)}) collective-permute-start(bf16[256,768]{1,0:T(8,128)(2,1)} %collective-permute-done.9.lc.la), channel_id=1, source_target_pairs={{0,248},{8,0},{16,8},{24,16},{32,24},{40,32},{48,40},{56,48},{64,5... | collective-permute-start | bytes 1179656 | tf_op jit(solution)/shard_map/ppermute | solution.py:31
  69.3 18.0 %collective-permute-start.17 = (bf16[256,768]{1,0:T(8,128)(2,1)}, bf16[256,768]{1,0:T(8,128)(2,1)S(1)}, u32[]{:S(2)}, u32[]{:S(2)}) collective-permute-start(bf16[256,768]{1,0:T(8,128)(2,1)} %collective-permute-done.14.rb), channel_id=1, source_target_pairs={{0,8},{8,16},{16,24},{24,32},{32,40},{40,48},{48,56},{56,64},{64,7... | collective-permute-start | bytes 1179656 | tf_op jit(solution)/shard_map/ppermute | solution.py:31
  69.4 17.9 %collective-permute-start.18 = (bf16[256,768]{1,0:T(8,128)(2,1)}, bf16[256,768]{1,0:T(8,128)(2,1)S(1)}, u32[]{:S(2)}, u32[]{:S(2)}) collective-permute-start(bf16[256,768]{1,0:T(8,128)(2,1)} %collective-permute-done.15.lb), channel_id=1, source_target_pairs={{0,248},{8,0},{16,8},{24,16},{32,24},{40,32},{48,40},{56,48},{64,5... | collective-permute-start | bytes 1179656 | tf_op jit(solution)/shard_map/ppermute | solution.py:31
  74.8 12.5 %collective-permute-start.20 = (bf16[128,768]{1,0:T(8,128)(2,1)S(1)}, bf16[128,768]{1,0:T(8,128)(2,1)S(1)}, u32[]{:S(2)}, u32[]{:S(2)}) collective-permute-start(bf16[128,768]{1,0:T(8,128)(2,1)S(1)} %slice.20), channel_id=1, source_target_pairs={{0,8},{8,16},{16,24},{24,32},{32,40},{40,48},{48,56},{56,64},{64,7... | collective-permute-start | bytes 589832 | tf_op jit(solution)/shard_map/ppermute | solution.py:31
  74.9 12.4 %collective-permute-start.21 = (bf16[128,768]{1,0:T(8,128)(2,1)S(1)}, bf16[128,768]{1,0:T(8,128)(2,1)S(1)}, u32[]{:S(2)}, u32[]{:S(2)}) collective-permute-start(bf16[128,768]{1,0:T(8,128)(2,1)S(1)} %slice.21), channel_id=1, source_target_pairs={{0,248},{8,0},{16,8},{24,16},{32,24},{40,32},{48,40},{56,48},{64,5... | collective-permute-start | bytes 589832 | tf_op jit(solution)/shard_map/ppermute | solution.py:31
  88.0 11.6 %collective-permute-start.22 = (bf16[256,768]{1,0:T(8,128)(2,1)S(1)}, bf16[256,768]{1,0:T(8,128)(2,1)S(1)}, u32[]{:S(2)}, u32[]{:S(2)}) collective-permute-start(bf16[256,768]{1,0:T(8,128)(2,1)S(1)} %get-tuple-element.80), channel_id=1, source_target_pairs={{0,248},{8,0},{16,8},{24,16},{32,24},{40,32},{48,40},{56,48},{64,5... | collective-permute-start | bytes 1179656 | tf_op jit(solution)/shard_map/ppermute | solution.py:31
  93.1 12.0 %collective-permute-start.23 = (bf16[256,768]{1,0:T(8,128)(2,1)S(1)}, bf16[256,768]{1,0:T(8,128)(2,1)S(1)}, u32[]{:S(2)}, u32[]{:S(2)}) collective-permute-start(bf16[256,768]{1,0:T(8,128)(2,1)S(1)} %get-tuple-element.81), channel_id=1, source_target_pairs={{0,8},{8,16},{16,24},{24,32},{32,40},{40,48},{48,56},{56,64},{64,7... | collective-permute-start | bytes 1179656 | tf_op jit(solution)/shard_map/ppermute | solution.py:31
  106.9 7.6 %collective-permute-start.26 = (bf16[256,384]{1,0:T(8,128)(2,1)S(1)}, bf16[256,384]{1,0:T(8,128)(2,1)S(1)}, u32[]{:S(2)}, u32[]{:S(2)}) collective-permute-start(bf16[256,384]{1,0:T(8,128)(2,1)S(1)} %get-tuple-element.89), channel_id=1, source_target_pairs={{0,1},{1,0},{2,3},{3,2},{4,5},{5,4},{6,7},{7,6},{8,9},{9,8},{10,11... | collective-permute-start | bytes 589832 | tf_op jit(solution)/shard_map/ppermute | solution.py:39
  118.1 16.5 %collective-permute-start.27 = (bf16[64,3072]{1,0:T(8,128)(2,1)S(1)}, bf16[64,3072]{1,0:T(8,128)(2,1)S(1)}, u32[]{:S(2)}, u32[]{:S(2)}) collective-permute-start(bf16[64,3072]{1,0:T(8,128)(2,1)S(1)} %get-tuple-element.96), channel_id=1, source_target_pairs={{0,2},{1,3},{2,4},{3,5},{4,6},{5,7},{6,0},{7,1},{8,10},{9,11},{10,... | collective-permute-start | bytes 1179656 | tf_op jit(solution)/shard_map/ppermute | solution.py:35
  121.1 16.8 %collective-permute-start.28 = (bf16[64,3072]{1,0:T(8,128)(2,1)S(1)}, bf16[64,3072]{1,0:T(8,128)(2,1)S(1)}, u32[]{:S(2)}, u32[]{:S(2)}) collective-permute-start(bf16[64,3072]{1,0:T(8,128)(2,1)S(1)} %get-tuple-element.97), channel_id=1, source_target_pairs={{0,6},{1,7},{2,0},{3,1},{4,2},{5,3},{6,4},{7,5},{8,14},{9,15},{10,... | collective-permute-start | bytes 1179656 | tf_op jit(solution)/shard_map/ppermute | solution.py:35
  121.1 16.8 %collective-permute-start.29 = (bf16[64,3072]{1,0:T(8,128)(2,1)S(1)}, bf16[64,3072]{1,0:T(8,128)(2,1)S(1)}, u32[]{:S(2)}, u32[]{:S(2)}) collective-permute-start(bf16[64,3072]{1,0:T(8,128)(2,1)S(1)} %get-tuple-element.98), channel_id=1, source_target_pairs={{0,4},{1,5},{2,6},{3,7},{4,0},{5,1},{6,2},{7,3},{8,12},{9,13},{10,... | collective-permute-start | bytes 1179656 | tf_op jit(solution)/shard_map/ppermute | solution.py:35
  (28 other events, 190.5 us)

commit v4 on v3

--- a/solution.py
+++ b/solution.py
@@ -459,9 +459,10 @@
     q = project_q([mod0, sib0, mod1, sib1, mod3, sib3, mod2, sib2], *args)
     hop_args = (head, key_tiles, key_count, q)
     num, den = attend_own(q, (kv_a, kv_b, right_ac))
-    rb1, lb1, num, den, w_sib = barrier((rb1, lb1, num, den, w_sib))
+    rb1, lb1, num, den = barrier((rb1, lb1, num, den))
     rb2, lb2 = along_win(rb1, 1), along_win(lb1, -1)
     rac3, lac3 = along_win(rac2, 1), along_win(lac2, -1)
+    num, den, w_sib = barrier((num, den, w_sib))
     num, den = attend_hop(1, (0, 1), *hop_args, (la1, lb1, lac2), (ra1, rb1, rac2), num, den)
     rb2, lb2, num, den = barrier((rb2, lb2, num, den))
     rb3, lb3 = along_win(rb2, 1), along_win(lb2, -1)

time: 139 us -> 140 us (level)
  local copies, waits for them, and re-layouts: 15 us -> 13.6 us
    unnamed x44 -> x40, local copies, waits for them, and re-layouts: 14.2 us -> 12.8 us
where the time goes in v4:
time: 140 us
  starting transfers between devices  55.1 us (39%)
  waiting for transfers between devices  42 us (30%)
  Pallas kernels  26.9 us (19%)
  local copies, waits for them, and re-layouts  13.6 us (10%)
    ppermute x16, starting transfers between devices, along_win(): lax.ppermute(value, 'win', [(i, (i + steps) % WINDOWS) for i in range(WIN...  45.6 us
    ppermute x16, waiting for transfers between devices, along_win(): lax.ppermute(value, 'win', [(i, (i + steps) % WINDOWS) for i in range(WIN...  17.7 us
    ppermute x6, waiting for transfers between devices, to_y(): lax.ppermute(value, 'head', [(h, (h // 2 + steps) % 4 * 2 + h % 2) for h...  17.4 us
    unnamed x40, local copies, waits for them, and re-layouts  12.8 us
    pallas_call x3, Pallas kernels, attend_hop(): pl.pallas_call(functools.partial(hop_kernel, 4 * (hop - 1)), grid=(512 //...  8.8 us
    ppermute x6, starting transfers between devices, to_y(): lax.ppermute(value, 'head', [(h, (h // 2 + steps) % 4 * 2 + h % 2) for h...  8.02 us
    pallas_call x3, Pallas kernels, project(): pl.pallas_call(kernel, grid=(count,), in_specs=[whole((ROWS, D))] * parts...  6.77 us
    ppermute x1, waiting for transfers between devices, shards(): edge_own = lax.ppermute(edge_a, ('win', 'head'), strip_pairs(0))  4.71 us
  transfers between devices with their start and end apart: 30, of which 13 were waited for; matrix products, arithmetic and copies ran while one was open for 1% of the time, Pallas kernels for 12%

profile of v4, /device:TPU:24, one launch (start us, length us, event | category | flops | bytes accessed | tf_op | source)
XLA Modules:
  0.0 139.7 jit_solution(1330225566242312807)
XLA Ops:
  3.1 2.5 %collective-permute-start.2 = (bf16[64,3072]{1,0:T(8,128)(2,1)S(1)}, bf16[64,3072]{1,0:T(8,128)(2,1)S(1)}, u32[]{:S(2)}, u32[]{:S(2)}) collective-permute-start(bf16[64,3072]{1,0:T(8,128)(2,1)S(1)} %modulate.1.refs_0_), channel_id=1, source_target_pairs={{0,2},{1,3},{2,4},{3,5},{4,6},{5,7},{6,0},{7,1},{8,10},{9,11},{10,... | collective-permute-start | bytes 1179656 | tf_op jit(solution)/shard_map/ppermute | solution.py:35
  5.8 3.0 %copy-done = bf16[3072,3,384]{2,0,1:T(8,128)(2,1)S(1)} copy-done((bf16[3072,3,384]{2,0,1:T(8,128)(2,1)S(1)}, bf16[3072,3,384]{2,0,1:T(8,128)(2,1)}, u32[]{:S(2)}) %copy-start) | copy-done | bytes 7077912
  14.5 6.2 %collective-permute-start.5 = (bf16[144,768]{1,0:T(8,128)(2,1)S(1)}, bf16[144,768]{1,0:T(8,128)(2,1)S(1)}, u32[]{:S(2)}, u32[]{:S(2)}) collective-permute-start(bf16[144,768]{1,0:T(8,128)(2,1)S(1)} %project.3.a), channel_id=1, source_target_pairs={{0,248},{8,0},{16,8},{24,16},{32,24},{40,32},{48,40},{56,48},{64,5... | collective-permute-start | bytes 663560 | tf_op jit(solution)/shard_map/ppermute | solution.py:31
  23.6 2.5 %collective-permute-done.4.refs_9_.ra = bf16[144,768]{1,0:T(8,128)(2,1)S(1)} collective-permute-done((bf16[144,768]{1,0:T(8,128)(2,1)S(1)}, bf16[144,768]{1,0:T(8,128)(2,1)S(1)}, u32[]{:S(2)}, u32[]{:S(2)}) %collective-permute-start.4) | collective-permute-done | bytes 221216 | tf_op jit(solution)/shard_map/ppermute | solution.py:31
  29.0 3.0 %project.5 = (bf16[256,768]{1,0:T(8,128)(2,1)S(1)}, bf16[256,768]{1,0:T(8,128)(2,1)S(1)}, bf16[256,768]{1,0:T(8,128)(2,1)S(1)}) custom-call(bf16[64,3072]{1,0:T(8,128)(2,1)S(1)} %collective-permute-done.1.refs_2_.refs_0_, bf16[64,3072]{1,0:T(8,128)(2,1)S(1)} %collective-permute-done.6.refs_3_.refs_1_, ...), custom_call_target="tpu_custom_call" | custom-call | flops 1 | bytes 1 | tf_op jit(solution)/shard_map/project/pallas_call | solution.py:136
  32.2 5.5 %collective-permute-start.12 = (bf16[256,768]{1,0:T(8,128)(2,1)S(1)}, bf16[256,768]{1,0:T(8,128)(2,1)}, u32[]{:S(2)}, u32[]{:S(2)}) collective-permute-start(bf16[256,768]{1,0:T(8,128)(2,1)S(1)} %get-tuple-element.61.b), channel_id=1, source_target_pairs={{0,248},{8,0},{16,8},{24,16},{32,24},{40,32},{48,40},{56,48},{64,5... | collective-permute-start | bytes 1179656 | tf_op jit(solution)/shard_map/ppermute | solution.py:31
  37.7 5.3 %collective-permute-start.9 = (bf16[256,768]{1,0:T(8,128)(2,1)S(1)}, bf16[256,768]{1,0:T(8,128)(2,1)}, u32[]{:S(2)}, u32[]{:S(2)}) collective-permute-start(bf16[256,768]{1,0:T(8,128)(2,1)S(1)} %get-tuple-element.59), channel_id=1, source_target_pairs={{0,248},{8,0},{16,8},{24,16},{32,24},{40,32},{48,40},{56,48},{64,5... | collective-permute-start | bytes 1179656 | tf_op jit(solution)/shard_map/ppermute | solution.py:31
  48.6 5.3 %collective-permute-start.14 = (bf16[256,768]{1,0:T(8,128)(2,1)}, bf16[256,768]{1,0:T(8,128)(2,1)}, u32[]{:S(2)}, u32[]{:S(2)}) collective-permute-start(bf16[256,768]{1,0:T(8,128)(2,1)} %collective-permute-done.12.lb), channel_id=1, source_target_pairs={{0,248},{8,0},{16,8},{24,16},{32,24},{40,32},{48,40},{56,48},{64,5... | collective-permute-start | bytes 1179656 | tf_op jit(solution)/shard_map/ppermute | solution.py:31
  56.2 5.3 %collective-permute-start.10 = (bf16[256,768]{1,0:T(8,128)(2,1)}, bf16[256,768]{1,0:T(8,128)(2,1)S(1)}, u32[]{:S(2)}, u32[]{:S(2)}) collective-permute-start(bf16[256,768]{1,0:T(8,128)(2,1)} %collective-permute-done.9.lc.la), channel_id=1, source_target_pairs={{0,248},{8,0},{16,8},{24,16},{32,24},{40,32},{48,40},{56,48},{64,5... | collective-permute-start | bytes 1179656 | tf_op jit(solution)/shard_map/ppermute | solution.py:31
  66.3 3.2 %attend_hop.3 = (f32[512,384]{1,0:T(8,128)S(1)}, f32[512,384]{1,0:T(8,128)S(1)}) custom-call(s32[1]{0:T(128)} %bitcast.1.head, s32[1,16]{1,0:T(1,128)S(1)} %copy-done.17, s32[1]{0:T(128)S(6)} %copy.11.count, bf16[512,384]{1,0:T(8,128)(2,1)S(1)} %project.4.q, bf16[144,768]{1,0:T(8,128)(2,1)S(1)} %copy-done.8, bf16[256,768]{1,0:T(8,128)(2,1)} %collective-permute-done.12.lb, ...), custom_call_target="tpu_custom_call" | custom-call | flops 1 | bytes 1 | tf_op jit(solution)/shard_map/attend_hop/pallas_call | solution.py:286
  69.6 5.3 %collective-permute-start.18 = (bf16[256,768]{1,0:T(8,128)(2,1)}, bf16[256,768]{1,0:T(8,128)(2,1)S(1)}, u32[]{:S(2)}, u32[]{:S(2)}) collective-permute-start(bf16[256,768]{1,0:T(8,128)(2,1)} %collective-permute-done.14.lb), channel_id=1, source_target_pairs={{0,248},{8,0},{16,8},{24,16},{32,24},{40,32},{48,40},{56,48},{64,5... | collective-permute-start | bytes 1179656 | tf_op jit(solution)/shard_map/ppermute | solution.py:31
  75.1 5.4 %collective-permute-start.21 = (bf16[128,768]{1,0:T(8,128)(2,1)S(1)}, bf16[128,768]{1,0:T(8,128)(2,1)S(1)}, u32[]{:S(2)}, u32[]{:S(2)}) collective-permute-start(bf16[128,768]{1,0:T(8,128)(2,1)S(1)} %slice.21), channel_id=1, source_target_pairs={{0,248},{8,0},{16,8},{24,16},{32,24},{40,32},{48,40},{56,48},{64,5... | collective-permute-start | bytes 589832 | tf_op jit(solution)/shard_map/ppermute | solution.py:31
  80.5 3.2 %attend_hop.4 = (f32[512,384]{1,0:T(8,128)S(1)}, f32[512,384]{1,0:T(8,128)S(1)}) custom-call(s32[1]{0:T(128)} %bitcast.1.head, s32[1,16]{1,0:T(1,128)S(1)} %copy-done.17, s32[1]{0:T(128)S(6)} %copy.11.count, bf16[512,384]{1,0:T(8,128)(2,1)S(1)} %project.4.q, bf16[256,768]{1,0:T(8,128)(2,1)} %collective-permute-done.9.lc.la, ...), custom_call_target="tpu_custom_call" | custom-call | flops 1 | bytes 1 | tf_op jit(solution)/shard_map/attend_hop/pallas_call | solution.py:286
  83.7 3.6 %collective-permute-done.20.rc = bf16[128,768]{1,0:T(8,128)(2,1)S(1)} collective-permute-done((bf16[128,768]{1,0:T(8,128)(2,1)S(1)}, bf16[128,768]{1,0:T(8,128)(2,1)S(1)}, u32[]{:S(2)}, u32[]{:S(2)}) %collective-permute-start.20) | collective-permute-done | bytes 196640 | tf_op jit(solution)/shard_map/ppermute | solution.py:31
  88.0 5.1 %collective-permute-start.22 = (bf16[256,768]{1,0:T(8,128)(2,1)S(1)}, bf16[256,768]{1,0:T(8,128)(2,1)S(1)}, u32[]{:S(2)}, u32[]{:S(2)}) collective-permute-start(bf16[256,768]{1,0:T(8,128)(2,1)S(1)} %get-tuple-element.84), channel_id=1, source_target_pairs={{0,248},{8,0},{16,8},{24,16},{32,24},{40,32},{48,40},{56,48},{64,5... | collective-permute-start | bytes 1179656 | tf_op jit(solution)/shard_map/ppermute | solution.py:31
  93.2 2.4 %attend_hop.5 = (f32[512,384]{1,0:T(8,128)S(1)}, f32[512,384]{1,0:T(8,128)S(1)}) custom-call(s32[1]{0:T(128)} %bitcast.1.head, s32[1,16]{1,0:T(1,128)S(1)} %copy-done.17, s32[1]{0:T(128)S(6)} %copy.11.count, bf16[512,384]{1,0:T(8,128)(2,1)S(1)} %project.4.q, bf16[256,768]{1,0:T(8,128)(2,1)S(1)} %collective-permute-done.10.lc.la, ...), custom_call_target="tpu_custom_call" | custom-call | flops 1 | bytes 1 | tf_op jit(solution)/shard_map/attend_hop/pallas_call | solution.py:286
  95.6 3.8 %collective-permute-done.22.left = bf16[256,768]{1,0:T(8,128)(2,1)S(1)} collective-permute-done((bf16[256,768]{1,0:T(8,128)(2,1)S(1)}, bf16[256,768]{1,0:T(8,128)(2,1)S(1)}, u32[]{:S(2)}, u32[]{:S(2)}) %collective-permute-start.22) | collective-permute-done | bytes 393248 | tf_op jit(solution)/shard_map/ppermute | solution.py:31
  99.4 5.5 %collective-permute-done.23.right = bf16[256,768]{1,0:T(8,128)(2,1)S(1)} collective-permute-done((bf16[256,768]{1,0:T(8,128)(2,1)S(1)}, bf16[256,768]{1,0:T(8,128)(2,1)S(1)}, u32[]{:S(2)}, u32[]{:S(2)}) %collective-permute-start.23) | collective-permute-done | bytes 393248 | tf_op jit(solution)/shard_map/ppermute | solution.py:31
  107.2 2.4 %out_own.1.part = f32[256,3072]{1,0:T(8,128)S(1)} custom-call(s32[1]{0:T(128)} %bitcast.1.head, s32[1]{0:T(128)} %bitcast.2.window, s32[32]{0:T(128)S(1)} %copy-done.18, bf16[256,384]{1,0:T(8,128)(2,1)S(1)} %get-tuple-element.90.own, bf16[384,3072]{1,0:T(8,128)(2,1)S(1)} %copy-done.2), custom_call_target="tpu_custom_call" | custom-call | flops 1 | bytes 1 | tf_op jit(solution)/shard_map/out_own/pallas_call | solution.py:397
  109.6 4.7 %collective-permute-done.24.edge_own = bf16[64,384]{1,0:T(8,128)(2,1)S(1)} collective-permute-done((bf16[64,384]{1,0:T(8,128)(2,1)S(1)}, bf16[64,384]{1,0:T(8,128)(2,1)S(1)}, u32[]{:S(2)}, u32[]{:S(2)}) %collective-permute-start.24) | collective-permute-done | bytes 49184 | tf_op jit(solution)/shard_map/ppermute | solution.py:479
  114.3 4.4 %out_project.1 = (f32[64,3072]{1,0:T(8,128)S(1)}, bf16[64,3072]{1,0:T(8,128)(2,1)S(1)}, bf16[64,3072]{1,0:T(8,128)(2,1)S(1)}, bf16[64,3072]{1,0:T(8,128)(2,1)S(1)}) custom-call(s32[1]{0:T(128)} %bitcast.1.head, s32[1]{0:T(128)} %bitcast.2.window, s32[32]{0:T(128)S(1)} %copy-done.18, f32[256,3072]{1,0:T(8,128)S(1)} %out_own.1.part, ...), custom_call_target="tpu_custom_call" | custom-call | flops 1 | bytes 1 | tf_op jit(solution)/shard_map/out_project/pallas_call | solution.py:412
  118.8 3.0 %collective-permute-start.27 = (bf16[64,3072]{1,0:T(8,128)(2,1)S(1)}, bf16[64,3072]{1,0:T(8,128)(2,1)S(1)}, u32[]{:S(2)}, u32[]{:S(2)}) collective-permute-start(bf16[64,3072]{1,0:T(8,128)(2,1)S(1)} %get-tuple-element.100), channel_id=1, source_target_pairs={{0,2},{1,3},{2,4},{3,5},{4,6},{5,7},{6,0},{7,1},{8,10},{9,11},{10,... | collective-permute-start | bytes 1179656 | tf_op jit(solution)/shard_map/ppermute | solution.py:35
  124.1 11.1 %collective-permute-done.27 = bf16[64,3072]{1,0:T(8,128)(2,1)S(1)} collective-permute-done((bf16[64,3072]{1,0:T(8,128)(2,1)S(1)}, bf16[64,3072]{1,0:T(8,128)(2,1)S(1)}, u32[]{:S(2)}, u32[]{:S(2)}) %collective-permute-start.27) | collective-permute-done | bytes 393248 | tf_op jit(solution)/shard_map/ppermute | solution.py:35
  135.2 3.4 %collective-permute-done.28 = bf16[64,3072]{1,0:T(8,128)(2,1)S(1)} collective-permute-done((bf16[64,3072]{1,0:T(8,128)(2,1)S(1)}, bf16[64,3072]{1,0:T(8,128)(2,1)S(1)}, u32[]{:S(2)}, u32[]{:S(2)}) %collective-permute-start.28) | collective-permute-done | bytes 393248 | tf_op jit(solution)/shard_map/ppermute | solution.py:35
  (93 shorter events, 33.4 us)
Async XLA Ops:
  2.3 18.5 %collective-permute-start.1 = (bf16[64,3072]{1,0:T(8,128)(2,1)S(1)}, bf16[64,3072]{1,0:T(8,128)(2,1)S(1)}, u32[]{:S(2)}, u32[]{:S(2)}) collective-permute-start(bf16[64,3072]{1,0:T(8,128)(2,1)S(1)} %modulate.1.refs_0_), channel_id=1, source_target_pairs={{0,6},{1,7},{2,0},{3,1},{4,2},{5,3},{6,4},{7,5},{8,14},{9,15},{10,... | collective-permute-start | bytes 1179656 | tf_op jit(solution)/shard_map/ppermute | solution.py:35
  3.1 19.6 %collective-permute-start.2 = (bf16[64,3072]{1,0:T(8,128)(2,1)S(1)}, bf16[64,3072]{1,0:T(8,128)(2,1)S(1)}, u32[]{:S(2)}, u32[]{:S(2)}) collective-permute-start(bf16[64,3072]{1,0:T(8,128)(2,1)S(1)} %modulate.1.refs_0_), channel_id=1, source_target_pairs={{0,2},{1,3},{2,4},{3,5},{4,6},{5,7},{6,0},{7,1},{8,10},{9,11},{10,... | collective-permute-start | bytes 1179656 | tf_op jit(solution)/shard_map/ppermute | solution.py:35
  5.6 18.0 %collective-permute-start.3 = (bf16[64,3072]{1,0:T(8,128)(2,1)S(1)}, bf16[64,3072]{1,0:T(8,128)(2,1)S(1)}, u32[]{:S(2)}, u32[]{:S(2)}) collective-permute-start(bf16[64,3072]{1,0:T(8,128)(2,1)S(1)} %modulate.1.refs_0_), channel_id=1, source_target_pairs={{0,4},{1,5},{2,6},{3,7},{4,0},{5,1},{6,2},{7,3},{8,12},{9,13},{10,... | collective-permute-start | bytes 1179656 | tf_op jit(solution)/shard_map/ppermute | solution.py:35
  12.6 13.4 %collective-permute-start.4 = (bf16[144,768]{1,0:T(8,128)(2,1)S(1)}, bf16[144,768]{1,0:T(8,128)(2,1)S(1)}, u32[]{:S(2)}, u32[]{:S(2)}) collective-permute-start(bf16[144,768]{1,0:T(8,128)(2,1)S(1)} %project.3.a), channel_id=1, source_target_pairs={{0,8},{8,16},{16,24},{24,32},{32,40},{40,48},{48,56},{56,64},{64,7... | collective-permute-start | bytes 663560 | tf_op jit(solution)/shard_map/ppermute | solution.py:31
  14.5 11.6 %collective-permute-start.5 = (bf16[144,768]{1,0:T(8,128)(2,1)S(1)}, bf16[144,768]{1,0:T(8,128)(2,1)S(1)}, u32[]{:S(2)}, u32[]{:S(2)}) collective-permute-start(bf16[144,768]{1,0:T(8,128)(2,1)S(1)} %project.3.a), channel_id=1, source_target_pairs={{0,248},{8,0},{16,8},{24,16},{32,24},{40,32},{48,40},{56,48},{64,5... | collective-permute-start | bytes 663560 | tf_op jit(solution)/shard_map/ppermute | solution.py:31
  32.0 30.2 %collective-permute-start.16 = (bf16[384,3072]{1,0:T(8,128)(2,1)S(1)}, bf16[384,3072]{1,0:T(8,128)(2,1)}, u32[]{:S(2)}, u32[]{:S(2)}) collective-permute-start(bf16[384,3072]{1,0:T(8,128)(2,1)S(1)} %copy-done.2), channel_id=1, source_target_pairs={{0,1},{1,0},{2,3},{3,2},{4,5},{5,4},{6,7},{7,6},{8,9},{9,8},{10,11... | collective-permute-start | bytes 7077896 | tf_op jit(solution)/shard_map/ppermute | solution.py:39
  32.2 16.3 %collective-permute-start.11 = (bf16[256,768]{1,0:T(8,128)(2,1)S(1)}, bf16[256,768]{1,0:T(8,128)(2,1)}, u32[]{:S(2)}, u32[]{:S(2)}) collective-permute-start(bf16[256,768]{1,0:T(8,128)(2,1)S(1)} %get-tuple-element.61.b), channel_id=1, source_target_pairs={{0,8},{8,16},{16,24},{24,32},{32,40},{40,48},{48,56},{56,64},{64,7... | collective-permute-start | bytes 1179656 | tf_op jit(solution)/shard_map/ppermute | solution.py:31
  32.2 16.3 %collective-permute-start.12 = (bf16[256,768]{1,0:T(8,128)(2,1)S(1)}, bf16[256,768]{1,0:T(8,128)(2,1)}, u32[]{:S(2)}, u32[]{:S(2)}) collective-permute-start(bf16[256,768]{1,0:T(8,128)(2,1)S(1)} %get-tuple-element.61.b), channel_id=1, source_target_pairs={{0,248},{8,0},{16,8},{24,16},{32,24},{40,32},{48,40},{56,48},{64,5... | collective-permute-start | bytes 1179656 | tf_op jit(solution)/shard_map/ppermute | solution.py:31
  37.7 18.4 %collective-permute-start.15 = (bf16[256,768]{1,0:T(8,128)(2,1)S(1)}, bf16[256,768]{1,0:T(8,128)(2,1)}, u32[]{:S(2)}, u32[]{:S(2)}) collective-permute-start(bf16[256,768]{1,0:T(8,128)(2,1)S(1)} %get-tuple-element.62.c), channel_id=1, source_target_pairs={{0,8},{8,16},{16,24},{24,32},{32,40},{40,48},{48,56},{56,64},{64,7... | collective-permute-start | bytes 1179656 | tf_op jit(solution)/shard_map/ppermute | solution.py:31
  37.7 18.4 %collective-permute-start.9 = (bf16[256,768]{1,0:T(8,128)(2,1)S(1)}, bf16[256,768]{1,0:T(8,128)(2,1)}, u32[]{:S(2)}, u32[]{:S(2)}) collective-permute-start(bf16[256,768]{1,0:T(8,128)(2,1)S(1)} %get-tuple-element.59), channel_id=1, source_target_pairs={{0,248},{8,0},{16,8},{24,16},{32,24},{40,32},{48,40},{56,48},{64,5... | collective-permute-start | bytes 1179656 | tf_op jit(solution)/shard_map/ppermute | solution.py:31
  48.6 21.0 %collective-permute-start.13 = (bf16[256,768]{1,0:T(8,128)(2,1)}, bf16[256,768]{1,0:T(8,128)(2,1)}, u32[]{:S(2)}, u32[]{:S(2)}) collective-permute-start(bf16[256,768]{1,0:T(8,128)(2,1)} %collective-permute-done.11.rb), channel_id=1, source_target_pairs={{0,8},{8,16},{16,24},{24,32},{32,40},{40,48},{48,56},{56,64},{64,7... | collective-permute-start | bytes 1179656 | tf_op jit(solution)/shard_map/ppermute | solution.py:31
  48.6 21.0 %collective-permute-start.14 = (bf16[256,768]{1,0:T(8,128)(2,1)}, bf16[256,768]{1,0:T(8,128)(2,1)}, u32[]{:S(2)}, u32[]{:S(2)}) collective-permute-start(bf16[256,768]{1,0:T(8,128)(2,1)} %collective-permute-done.12.lb), channel_id=1, source_target_pairs={{0,248},{8,0},{16,8},{24,16},{32,24},{40,32},{48,40},{56,48},{64,5... | collective-permute-start | bytes 1179656 | tf_op jit(solution)/shard_map/ppermute | solution.py:31
  56.2 18.8 %collective-permute-start.19 = (bf16[256,768]{1,0:T(8,128)(2,1)}, bf16[256,768]{1,0:T(8,128)(2,1)S(1)}, u32[]{:S(2)}, u32[]{:S(2)}) collective-permute-start(bf16[256,768]{1,0:T(8,128)(2,1)} %collective-permute-done.15.rc.ra), channel_id=1, source_target_pairs={{0,8},{8,16},{16,24},{24,32},{32,40},{40,48},{48,56},{56,64},{64,7... | collective-permute-start | bytes 1179656 | tf_op jit(solution)/shard_map/ppermute | solution.py:31
  56.2 18.9 %collective-permute-start.10 = (bf16[256,768]{1,0:T(8,128)(2,1)}, bf16[256,768]{1,0:T(8,128)(2,1)S(1)}, u32[]{:S(2)}, u32[]{:S(2)}) collective-permute-start(bf16[256,768]{1,0:T(8,128)(2,1)} %collective-permute-done.9.lc.la), channel_id=1, source_target_pairs={{0,248},{8,0},{16,8},{24,16},{32,24},{40,32},{48,40},{56,48},{64,5... | collective-permute-start | bytes 1179656 | tf_op jit(solution)/shard_map/ppermute | solution.py:31
  69.6 17.8 %collective-permute-start.17 = (bf16[256,768]{1,0:T(8,128)(2,1)}, bf16[256,768]{1,0:T(8,128)(2,1)S(1)}, u32[]{:S(2)}, u32[]{:S(2)}) collective-permute-start(bf16[256,768]{1,0:T(8,128)(2,1)} %collective-permute-done.13.rb), channel_id=1, source_target_pairs={{0,8},{8,16},{16,24},{24,32},{32,40},{40,48},{48,56},{56,64},{64,7... | collective-permute-start | bytes 1179656 | tf_op jit(solution)/shard_map/ppermute | solution.py:31
  69.6 17.7 %collective-permute-start.18 = (bf16[256,768]{1,0:T(8,128)(2,1)}, bf16[256,768]{1,0:T(8,128)(2,1)S(1)}, u32[]{:S(2)}, u32[]{:S(2)}) collective-permute-start(bf16[256,768]{1,0:T(8,128)(2,1)} %collective-permute-done.14.lb), channel_id=1, source_target_pairs={{0,248},{8,0},{16,8},{24,16},{32,24},{40,32},{48,40},{56,48},{64,5... | collective-permute-start | bytes 1179656 | tf_op jit(solution)/shard_map/ppermute | solution.py:31
  75.0 12.3 %collective-permute-start.20 = (bf16[128,768]{1,0:T(8,128)(2,1)S(1)}, bf16[128,768]{1,0:T(8,128)(2,1)S(1)}, u32[]{:S(2)}, u32[]{:S(2)}) collective-permute-start(bf16[128,768]{1,0:T(8,128)(2,1)S(1)} %slice.20), channel_id=1, source_target_pairs={{0,8},{8,16},{16,24},{24,32},{32,40},{40,48},{48,56},{56,64},{64,7... | collective-permute-start | bytes 589832 | tf_op jit(solution)/shard_map/ppermute | solution.py:31
  75.1 12.2 %collective-permute-start.21 = (bf16[128,768]{1,0:T(8,128)(2,1)S(1)}, bf16[128,768]{1,0:T(8,128)(2,1)S(1)}, u32[]{:S(2)}, u32[]{:S(2)}) collective-permute-start(bf16[128,768]{1,0:T(8,128)(2,1)S(1)} %slice.21), channel_id=1, source_target_pairs={{0,248},{8,0},{16,8},{24,16},{32,24},{40,32},{48,40},{56,48},{64,5... | collective-permute-start | bytes 589832 | tf_op jit(solution)/shard_map/ppermute | solution.py:31
  88.0 11.4 %collective-permute-start.22 = (bf16[256,768]{1,0:T(8,128)(2,1)S(1)}, bf16[256,768]{1,0:T(8,128)(2,1)S(1)}, u32[]{:S(2)}, u32[]{:S(2)}) collective-permute-start(bf16[256,768]{1,0:T(8,128)(2,1)S(1)} %get-tuple-element.84), channel_id=1, source_target_pairs={{0,248},{8,0},{16,8},{24,16},{32,24},{40,32},{48,40},{56,48},{64,5... | collective-permute-start | bytes 1179656 | tf_op jit(solution)/shard_map/ppermute | solution.py:31
  93.2 11.8 %collective-permute-start.23 = (bf16[256,768]{1,0:T(8,128)(2,1)S(1)}, bf16[256,768]{1,0:T(8,128)(2,1)S(1)}, u32[]{:S(2)}, u32[]{:S(2)}) collective-permute-start(bf16[256,768]{1,0:T(8,128)(2,1)S(1)} %get-tuple-element.85), channel_id=1, source_target_pairs={{0,8},{8,16},{16,24},{24,32},{32,40},{40,48},{48,56},{56,64},{64,7... | collective-permute-start | bytes 1179656 | tf_op jit(solution)/shard_map/ppermute | solution.py:31
  106.7 7.6 %collective-permute-start.26 = (bf16[256,384]{1,0:T(8,128)(2,1)S(1)}, bf16[256,384]{1,0:T(8,128)(2,1)S(1)}, u32[]{:S(2)}, u32[]{:S(2)}) collective-permute-start(bf16[256,384]{1,0:T(8,128)(2,1)S(1)} %get-tuple-element.93), channel_id=1, source_target_pairs={{0,1},{1,0},{2,3},{3,2},{4,5},{5,4},{6,7},{7,6},{8,9},{9,8},{10,11... | collective-permute-start | bytes 589832 | tf_op jit(solution)/shard_map/ppermute | solution.py:39
  118.8 16.4 %collective-permute-start.27 = (bf16[64,3072]{1,0:T(8,128)(2,1)S(1)}, bf16[64,3072]{1,0:T(8,128)(2,1)S(1)}, u32[]{:S(2)}, u32[]{:S(2)}) collective-permute-start(bf16[64,3072]{1,0:T(8,128)(2,1)S(1)} %get-tuple-element.100), channel_id=1, source_target_pairs={{0,2},{1,3},{2,4},{3,5},{4,6},{5,7},{6,0},{7,1},{8,10},{9,11},{10,... | collective-permute-start | bytes 1179656 | tf_op jit(solution)/shard_map/ppermute | solution.py:35
  121.8 16.9 %collective-permute-start.28 = (bf16[64,3072]{1,0:T(8,128)(2,1)S(1)}, bf16[64,3072]{1,0:T(8,128)(2,1)S(1)}, u32[]{:S(2)}, u32[]{:S(2)}) collective-permute-start(bf16[64,3072]{1,0:T(8,128)(2,1)S(1)} %get-tuple-element.101), channel_id=1, source_target_pairs={{0,6},{1,7},{2,0},{3,1},{4,2},{5,3},{6,4},{7,5},{8,14},{9,15},{10,... | collective-permute-start | bytes 1179656 | tf_op jit(solution)/shard_map/ppermute | solution.py:35
  121.8 16.9 %collective-permute-start.29 = (bf16[64,3072]{1,0:T(8,128)(2,1)S(1)}, bf16[64,3072]{1,0:T(8,128)(2,1)S(1)}, u32[]{:S(2)}, u32[]{:S(2)}) collective-permute-start(bf16[64,3072]{1,0:T(8,128)(2,1)S(1)} %get-tuple-element.102), channel_id=1, source_target_pairs={{0,4},{1,5},{2,6},{3,7},{4,0},{5,1},{6,2},{7,3},{8,12},{9,13},{10,... | collective-permute-start | bytes 1179656 | tf_op jit(solution)/shard_map/ppermute | solution.py:35
  (26 other events, 183.8 us)

commit v5 on v3

--- a/solution.py
+++ b/solution.py
@@ -116,6 +116,73 @@
     def _():
         raw = jnp.dot(mod_ref[...], weight[0], preferred_element_type=jnp.float32)
         store((raw + bias[2:3, :]).astype(jnp.bfloat16), slice(LW, 2 * LW))
+
+
+def kv_both(step, rows, weight, bias, gain, store):
+    @pl.when(step == 0)
+    def _():
+        raw = jnp.dot(rows[...], weight[0], preferred_element_type=jnp.float32)
+        for h, part in enumerate(normed_heads(raw + bias[1:2, :], gain[1:2, :])):
+            store(part, slice(h * HD, (h + 1) * HD))
+
+    @pl.when(step == 1)
+    def _():
+        raw = jnp.dot(rows[...], weight[0], preferred_element_type=jnp.float32)
+        store((raw + bias[2:3, :]).astype(jnp.bfloat16), slice(LW, 2 * LW))
+
+
+def join_rows(dst, parts):
+    for i, part in enumerate(parts):
+        dst[i * ROWS : (i + 1) * ROWS, :] = part[...]
+
+
+def kv_half_kernel(m1, m3, m2, weight, bias, gain, out, rows):
+    step = pl.program_id(0)
+
+    @pl.when(step == 0)
+    def _():
+        join_rows(rows, (m1, m3, m2))
+
+    def store(part, cols):
+        out[:, cols] = part
+
+    kv_both(step, rows, weight, bias, gain, store)
+
+
+def kv_rest_kernel(m1, m3, m2, weight, bias, gain, half, ra, la, kv_b, right, left, rows):
+    step = pl.program_id(0)
+
+    def place(values, at, cols):
+        kv_b[at : at + ROWS, cols] = values[0:ROWS]
+        kv_b[TILE + at : TILE + at + ROWS, cols] = values[ROWS : 2 * ROWS]
+        for out in (right, left):
+            out[TILE + at : TILE + at + ROWS, cols] = values[2 * ROWS :]
+
+    @pl.when(step == 0)
+    def _():
+        join_rows(rows, (m1, m3, m2))
+        right[0:TILE, :] = ra[...]
+        left[0:TILE, :] = la[...]
+        place(half[...], 0, slice(0, 2 * LW))
+
+    kv_both(step, rows, weight, bias, gain, lambda part, cols: place(part, ROWS, cols))
+
+
+def project_others(kernel, mod, weight, bias, gain, more, out_rows):
+    whole = lambda shape: pl.BlockSpec(shape, lambda c: (0,) * len(shape))
+    return pl.pallas_call(
+        kernel,
+        grid=(2,),
+        in_specs=[whole((ROWS, D))] * 3
+        + [pl.BlockSpec((1, D, LW), lambda c: (1 + c, 0, 0)), whole((3, LW)), whole((2, HD))]
+        + [whole((n, 2 * LW)) for n, _ in more],
+        out_specs=[whole((n, 2 * LW)) for n in out_rows],
+        out_shape=[jax.ShapeDtypeStruct((n, 2 * LW), jnp.bfloat16) for n in out_rows],
+        scratch_shapes=[pltpu.VMEM((3 * ROWS, D), jnp.bfloat16)],
+        compiler_params=pltpu.CompilerParams(vmem_limit_bytes=BIG * MIB),
+        cost_estimate=COST,
+        name="project_others",
+    )(*mod, weight, bias, gain, *(array for _, array in more))
 
 
 def q_kernel(parts, *refs):
@@ -451,7 +518,10 @@
     ra1, la1 = along_win(kv_a, 1), along_win(kv_a, -1)
     mod1, mod3, mod2, ra1, la1 = barrier((mod1, mod3, mod2, ra1, la1))
     sib1, sib3, sib2 = swap_core(mod1), swap_core(mod3), swap_core(mod2)
-    kv_b, right_ac, left_ac = project_kv([mod1, sib1, mod3, sib3, mod2, sib2], *args, carry=(ra1, la1))
+    (half,) = project_others(kv_half_kernel, (mod1, mod3, mod2), *args, (), (3 * ROWS,))
+    half, sib1, sib3, sib2 = barrier((half, sib1, sib3, sib2))
+    more = ((3 * ROWS, half), (TILE, ra1), (TILE, la1))
+    kv_b, right_ac, left_ac = project_others(kv_rest_kernel, (sib1, sib3, sib2), *args, more, (2 * TILE,) * 3)
     rb1, lb1 = along_win(kv_b, 1), along_win(kv_b, -1)
     rac2, lac2 = along_win(right_ac, 1), along_win(left_ac, -1)
     kv_b, w_sent = barrier((kv_b, out_weight))

time: 139 us -> 139 us (level)
  waiting for transfers between devices: 40.8 us -> 38.9 us
    pallas_call x0 -> x2, Pallas kernels: none -> 3.46 us  [project_others(): pl.pallas_call(kernel, grid=(2,), in_specs=[whole((ROWS, D))] * 3 + [pl.B...]
    pallas_call x3 -> x2, Pallas kernels: 6.76 us -> 3.79 us  [project(): pl.pallas_call(kernel, grid=(count,), in_specs=[whole((ROWS, D))] * parts...]
    ppermute x6, waiting for transfers between devices: 2.24 us -> 0.5 us  [swap_core(): return lax.ppermute(value, 'head', [(h, h ^ 1) for h in range(GROUPS)])]
  transfers between devices with their start and end apart: 30 -> 30, of which waited for: 13 -> 11; matrix products, arithmetic and copies ran while one was open for 1% -> 1% of each run, Pallas kernels for 12% -> 13%
where the time goes in v5:
time: 139 us; the launch traced here: 138 us
  starting transfers between devices  55.6 us (40%)
  waiting for transfers between devices  38.9 us (28%)
  Pallas kernels  26.4 us (19%)
  local copies, waits for them, and re-layouts  15 us (11%)
    ppermute x16, starting transfers between devices, along_win(): lax.ppermute(value, 'win', [(i, (i + steps) % WINDOWS) for i in range(WIN...  46 us
    ppermute x6, waiting for transfers between devices, to_y(): lax.ppermute(value, 'head', [(h, (h // 2 + steps) % 4 * 2 + h % 2) for h...  17.4 us
    ppermute x16, waiting for transfers between devices, along_win(): lax.ppermute(value, 'win', [(i, (i + steps) % WINDOWS) for i in range(WIN...  16.3 us
    unnamed x44, local copies, waits for them, and re-layouts  14.2 us
    pallas_call x3, Pallas kernels, attend_hop(): pl.pallas_call(functools.partial(hop_kernel, 4 * (hop - 1)), grid=(512 //...  8.77 us
    ppermute x6, starting transfers between devices, to_y(): lax.ppermute(value, 'head', [(h, (h // 2 + steps) % 4 * 2 + h % 2) for h...  8.09 us
    ppermute x1, waiting for transfers between devices, shards(): edge_own = lax.ppermute(edge_a, ('win', 'head'), strip_pairs(0))  4.7 us
    pallas_call x2, Pallas kernels, project(): pl.pallas_call(kernel, grid=(count,), in_specs=[whole((ROWS, D))] * parts...  3.79 us
  transfers between devices with their start and end apart: 30, of which 11 were waited for; matrix products, arithmetic and copies ran while one was open for 1% of the time, Pallas kernels for 13%

profile of v5, /device:TPU:24, one launch (start us, length us, event | category | flops | bytes accessed | tf_op | source)
XLA Modules:
  0.0 138.0 jit_solution(14747469815584910959)
XLA Ops:
  3.1 2.5 %collective-permute-start.2 = (bf16[64,3072]{1,0:T(8,128)(2,1)S(1)}, bf16[64,3072]{1,0:T(8,128)(2,1)S(1)}, u32[]{:S(2)}, u32[]{:S(2)}) collective-permute-start(bf16[64,3072]{1,0:T(8,128)(2,1)S(1)} %modulate.1.refs_0_), channel_id=1, source_target_pairs={{0,2},{1,3},{2,4},{3,5},{4,6},{5,7},{6,0},{7,1},{8,10},{9,11},{10,... | collective-permute-start | bytes 1179656 | tf_op jit(solution)/shard_map/ppermute | solution.py:35
  5.8 3.0 %copy-done = bf16[3072,3,384]{2,0,1:T(8,128)(2,1)S(1)} copy-done((bf16[3072,3,384]{2,0,1:T(8,128)(2,1)S(1)}, bf16[3072,3,384]{2,0,1:T(8,128)(2,1)}, u32[]{:S(2)}) %copy-start) | copy-done | bytes 7077912
  14.5 6.2 %collective-permute-start.5 = (bf16[144,768]{1,0:T(8,128)(2,1)S(1)}, bf16[144,768]{1,0:T(8,128)(2,1)S(1)}, u32[]{:S(2)}, u32[]{:S(2)}) collective-permute-start(bf16[144,768]{1,0:T(8,128)(2,1)S(1)} %project.2.a), channel_id=1, source_target_pairs={{0,248},{8,0},{16,8},{24,16},{32,24},{40,32},{48,40},{56,48},{64,5... | collective-permute-start | bytes 663560 | tf_op jit(solution)/shard_map/ppermute | solution.py:31
  20.7 2.0 %collective-permute-done.2.m3.refs_4_ = bf16[64,3072]{1,0:T(8,128)(2,1)S(1)} collective-permute-done((bf16[64,3072]{1,0:T(8,128)(2,1)S(1)}, bf16[64,3072]{1,0:T(8,128)(2,1)S(1)}, u32[]{:S(2)}, u32[]{:S(2)}) %collective-permute-start.2) | collective-permute-done | bytes 393248 | tf_op jit(solution)/shard_map/ppermute | solution.py:35
  23.6 2.4 %collective-permute-done.4.ra = bf16[144,768]{1,0:T(8,128)(2,1)S(1)} collective-permute-done((bf16[144,768]{1,0:T(8,128)(2,1)S(1)}, bf16[144,768]{1,0:T(8,128)(2,1)S(1)}, u32[]{:S(2)}, u32[]{:S(2)}) %collective-permute-start.4) | collective-permute-done | bytes 221216 | tf_op jit(solution)/shard_map/ppermute | solution.py:31
  31.0 5.7 %collective-permute-start.12 = (bf16[256,768]{1,0:T(8,128)(2,1)S(1)}, bf16[256,768]{1,0:T(8,128)(2,1)}, u32[]{:S(2)}, u32[]{:S(2)}) collective-permute-start(bf16[256,768]{1,0:T(8,128)(2,1)S(1)} %get-tuple-element.67.b), channel_id=1, source_target_pairs={{0,248},{8,0},{16,8},{24,16},{32,24},{40,32},{48,40},{56,48},{64,5... | collective-permute-start | bytes 1179656 | tf_op jit(solution)/shard_map/ppermute | solution.py:31
  36.7 5.3 %collective-permute-start.9 = (bf16[256,768]{1,0:T(8,128)(2,1)S(1)}, bf16[256,768]{1,0:T(8,128)(2,1)}, u32[]{:S(2)}, u32[]{:S(2)}) collective-permute-start(bf16[256,768]{1,0:T(8,128)(2,1)S(1)} %get-tuple-element.65), channel_id=1, source_target_pairs={{0,248},{8,0},{16,8},{24,16},{32,24},{40,32},{48,40},{56,48},{64,5... | collective-permute-start | bytes 1179656 | tf_op jit(solution)/shard_map/ppermute | solution.py:31
  48.9 5.3 %collective-permute-start.15 = (bf16[256,768]{1,0:T(8,128)(2,1)}, bf16[256,768]{1,0:T(8,128)(2,1)}, u32[]{:S(2)}, u32[]{:S(2)}) collective-permute-start(bf16[256,768]{1,0:T(8,128)(2,1)} %collective-permute-done.12.lb), channel_id=1, source_target_pairs={{0,248},{8,0},{16,8},{24,16},{32,24},{40,32},{48,40},{56,48},{64,5... | collective-permute-start | bytes 1179656 | tf_op jit(solution)/shard_map/ppermute | solution.py:31
  54.7 5.3 %collective-permute-start.10 = (bf16[256,768]{1,0:T(8,128)(2,1)}, bf16[256,768]{1,0:T(8,128)(2,1)S(1)}, u32[]{:S(2)}, u32[]{:S(2)}) collective-permute-start(bf16[256,768]{1,0:T(8,128)(2,1)} %collective-permute-done.9.lc.la), channel_id=1, source_target_pairs={{0,248},{8,0},{16,8},{24,16},{32,24},{40,32},{48,40},{56,48},{64,5... | collective-permute-start | bytes 1179656 | tf_op jit(solution)/shard_map/ppermute | solution.py:31
  64.9 3.2 %attend_hop.3 = (f32[512,384]{1,0:T(8,128)S(1)}, f32[512,384]{1,0:T(8,128)S(1)}) custom-call(s32[1]{0:T(128)} %bitcast.1.head, s32[1,16]{1,0:T(1,128)S(1)} %copy-done.19, s32[1]{0:T(128)S(6)} %copy.11.count, bf16[512,384]{1,0:T(8,128)(2,1)S(1)} %project.3.q, bf16[144,768]{1,0:T(8,128)(2,1)S(1)} %copy-done.10, bf16[256,768]{1,0:T(8,128)(2,1)} %collective-permute-done.12.lb, ...), custom_call_target="tpu_custom_call" | custom-call | flops 1 | bytes 1 | tf_op jit(solution)/shard_map/attend_hop/pallas_call | solution.py:353
  68.2 5.3 %collective-permute-start.18 = (bf16[256,768]{1,0:T(8,128)(2,1)}, bf16[256,768]{1,0:T(8,128)(2,1)S(1)}, u32[]{:S(2)}, u32[]{:S(2)}) collective-permute-start(bf16[256,768]{1,0:T(8,128)(2,1)} %collective-permute-done.15.lb), channel_id=1, source_target_pairs={{0,248},{8,0},{16,8},{24,16},{32,24},{40,32},{48,40},{56,48},{64,5... | collective-permute-start | bytes 1179656 | tf_op jit(solution)/shard_map/ppermute | solution.py:31
  73.7 5.4 %collective-permute-start.21 = (bf16[128,768]{1,0:T(8,128)(2,1)S(1)}, bf16[128,768]{1,0:T(8,128)(2,1)S(1)}, u32[]{:S(2)}, u32[]{:S(2)}) collective-permute-start(bf16[128,768]{1,0:T(8,128)(2,1)S(1)} %slice.21), channel_id=1, source_target_pairs={{0,248},{8,0},{16,8},{24,16},{32,24},{40,32},{48,40},{56,48},{64,5... | collective-permute-start | bytes 589832 | tf_op jit(solution)/shard_map/ppermute | solution.py:31
  79.1 3.2 %attend_hop.4 = (f32[512,384]{1,0:T(8,128)S(1)}, f32[512,384]{1,0:T(8,128)S(1)}) custom-call(s32[1]{0:T(128)} %bitcast.1.head, s32[1,16]{1,0:T(1,128)S(1)} %copy-done.19, s32[1]{0:T(128)S(6)} %copy.11.count, bf16[512,384]{1,0:T(8,128)(2,1)S(1)} %project.3.q, bf16[256,768]{1,0:T(8,128)(2,1)} %collective-permute-done.9.lc.la, ...), custom_call_target="tpu_custom_call" | custom-call | flops 1 | bytes 1 | tf_op jit(solution)/shard_map/attend_hop/pallas_call | solution.py:353
  82.3 3.8 %collective-permute-done.20.rc = bf16[128,768]{1,0:T(8,128)(2,1)S(1)} collective-permute-done((bf16[128,768]{1,0:T(8,128)(2,1)S(1)}, bf16[128,768]{1,0:T(8,128)(2,1)S(1)}, u32[]{:S(2)}, u32[]{:S(2)}) %collective-permute-start.20) | collective-permute-done | bytes 196640 | tf_op jit(solution)/shard_map/ppermute | solution.py:31
  86.8 5.4 %collective-permute-start.22 = (bf16[256,768]{1,0:T(8,128)(2,1)S(1)}, bf16[256,768]{1,0:T(8,128)(2,1)S(1)}, u32[]{:S(2)}, u32[]{:S(2)}) collective-permute-start(bf16[256,768]{1,0:T(8,128)(2,1)S(1)} %get-tuple-element.88), channel_id=1, source_target_pairs={{0,248},{8,0},{16,8},{24,16},{32,24},{40,32},{48,40},{56,48},{64,5... | collective-permute-start | bytes 1179656 | tf_op jit(solution)/shard_map/ppermute | solution.py:31
  92.1 2.4 %attend_hop.5 = (f32[512,384]{1,0:T(8,128)S(1)}, f32[512,384]{1,0:T(8,128)S(1)}) custom-call(s32[1]{0:T(128)} %bitcast.1.head, s32[1,16]{1,0:T(1,128)S(1)} %copy-done.19, s32[1]{0:T(128)S(6)} %copy.11.count, bf16[512,384]{1,0:T(8,128)(2,1)S(1)} %project.3.q, bf16[256,768]{1,0:T(8,128)(2,1)S(1)} %collective-permute-done.10.lc.la, ...), custom_call_target="tpu_custom_call" | custom-call | flops 1 | bytes 1 | tf_op jit(solution)/shard_map/attend_hop/pallas_call | solution.py:353
  94.5 4.0 %collective-permute-done.22.left = bf16[256,768]{1,0:T(8,128)(2,1)S(1)} collective-permute-done((bf16[256,768]{1,0:T(8,128)(2,1)S(1)}, bf16[256,768]{1,0:T(8,128)(2,1)S(1)}, u32[]{:S(2)}, u32[]{:S(2)}) %collective-permute-start.22) | collective-permute-done | bytes 393248 | tf_op jit(solution)/shard_map/ppermute | solution.py:31
  98.6 5.5 %collective-permute-done.23.right = bf16[256,768]{1,0:T(8,128)(2,1)S(1)} collective-permute-done((bf16[256,768]{1,0:T(8,128)(2,1)S(1)}, bf16[256,768]{1,0:T(8,128)(2,1)S(1)}, u32[]{:S(2)}, u32[]{:S(2)}) %collective-permute-start.23) | collective-permute-done | bytes 393248 | tf_op jit(solution)/shard_map/ppermute | solution.py:31
  106.4 2.4 %out_own.1.part = f32[256,3072]{1,0:T(8,128)S(1)} custom-call(s32[1]{0:T(128)} %bitcast.1.head, s32[1]{0:T(128)} %bitcast.2.window, s32[32]{0:T(128)S(1)} %copy-done.20, bf16[256,384]{1,0:T(8,128)(2,1)S(1)} %get-tuple-element.94.own, bf16[384,3072]{1,0:T(8,128)(2,1)S(1)} %copy-done.2), custom_call_target="tpu_custom_call" | custom-call | flops 1 | bytes 1 | tf_op jit(solution)/shard_map/out_own/pallas_call | solution.py:464
  108.8 4.7 %collective-permute-done.24.edge_own = bf16[64,384]{1,0:T(8,128)(2,1)S(1)} collective-permute-done((bf16[64,384]{1,0:T(8,128)(2,1)S(1)}, bf16[64,384]{1,0:T(8,128)(2,1)S(1)}, u32[]{:S(2)}, u32[]{:S(2)}) %collective-permute-start.24) | collective-permute-done | bytes 49184 | tf_op jit(solution)/shard_map/ppermute | solution.py:548
  113.5 3.6 %out_project.1 = (f32[64,3072]{1,0:T(8,128)S(1)}, bf16[64,3072]{1,0:T(8,128)(2,1)S(1)}, bf16[64,3072]{1,0:T(8,128)(2,1)S(1)}, bf16[64,3072]{1,0:T(8,128)(2,1)S(1)}) custom-call(s32[1]{0:T(128)} %bitcast.1.head, s32[1]{0:T(128)} %bitcast.2.window, s32[32]{0:T(128)S(1)} %copy-done.20, f32[256,3072]{1,0:T(8,128)S(1)} %out_own.1.part, ...), custom_call_target="tpu_custom_call" | custom-call | flops 1 | bytes 1 | tf_op jit(solution)/shard_map/out_project/pallas_call | solution.py:479
  117.1 3.0 %collective-permute-start.27 = (bf16[64,3072]{1,0:T(8,128)(2,1)S(1)}, bf16[64,3072]{1,0:T(8,128)(2,1)S(1)}, u32[]{:S(2)}, u32[]{:S(2)}) collective-permute-start(bf16[64,3072]{1,0:T(8,128)(2,1)S(1)} %get-tuple-element.104), channel_id=1, source_target_pairs={{0,2},{1,3},{2,4},{3,5},{4,6},{5,7},{6,0},{7,1},{8,10},{9,11},{10,... | collective-permute-start | bytes 1179656 | tf_op jit(solution)/shard_map/ppermute | solution.py:35
  122.5 11.1 %collective-permute-done.27 = bf16[64,3072]{1,0:T(8,128)(2,1)S(1)} collective-permute-done((bf16[64,3072]{1,0:T(8,128)(2,1)S(1)}, bf16[64,3072]{1,0:T(8,128)(2,1)S(1)}, u32[]{:S(2)}, u32[]{:S(2)}) %collective-permute-start.27) | collective-permute-done | bytes 393248 | tf_op jit(solution)/shard_map/ppermute | solution.py:35
  133.6 3.4 %collective-permute-done.28 = bf16[64,3072]{1,0:T(8,128)(2,1)S(1)} collective-permute-done((bf16[64,3072]{1,0:T(8,128)(2,1)S(1)}, bf16[64,3072]{1,0:T(8,128)(2,1)S(1)}, u32[]{:S(2)}, u32[]{:S(2)}) %collective-permute-start.28) | collective-permute-done | bytes 393248 | tf_op jit(solution)/shard_map/ppermute | solution.py:35
  (98 shorter events, 32.7 us)
Async XLA Ops:
  2.3 18.4 %collective-permute-start.1 = (bf16[64,3072]{1,0:T(8,128)(2,1)S(1)}, bf16[64,3072]{1,0:T(8,128)(2,1)S(1)}, u32[]{:S(2)}, u32[]{:S(2)}) collective-permute-start(bf16[64,3072]{1,0:T(8,128)(2,1)S(1)} %modulate.1.refs_0_), channel_id=1, source_target_pairs={{0,6},{1,7},{2,0},{3,1},{4,2},{5,3},{6,4},{7,5},{8,14},{9,15},{10,... | collective-permute-start | bytes 1179656 | tf_op jit(solution)/shard_map/ppermute | solution.py:35
  3.1 19.6 %collective-permute-start.2 = (bf16[64,3072]{1,0:T(8,128)(2,1)S(1)}, bf16[64,3072]{1,0:T(8,128)(2,1)S(1)}, u32[]{:S(2)}, u32[]{:S(2)}) collective-permute-start(bf16[64,3072]{1,0:T(8,128)(2,1)S(1)} %modulate.1.refs_0_), channel_id=1, source_target_pairs={{0,2},{1,3},{2,4},{3,5},{4,6},{5,7},{6,0},{7,1},{8,10},{9,11},{10,... | collective-permute-start | bytes 1179656 | tf_op jit(solution)/shard_map/ppermute | solution.py:35
  5.6 18.0 %collective-permute-start.3 = (bf16[64,3072]{1,0:T(8,128)(2,1)S(1)}, bf16[64,3072]{1,0:T(8,128)(2,1)S(1)}, u32[]{:S(2)}, u32[]{:S(2)}) collective-permute-start(bf16[64,3072]{1,0:T(8,128)(2,1)S(1)} %modulate.1.refs_0_), channel_id=1, source_target_pairs={{0,4},{1,5},{2,6},{3,7},{4,0},{5,1},{6,2},{7,3},{8,12},{9,13},{10,... | collective-permute-start | bytes 1179656 | tf_op jit(solution)/shard_map/ppermute | solution.py:35
  12.6 13.4 %collective-permute-start.4 = (bf16[144,768]{1,0:T(8,128)(2,1)S(1)}, bf16[144,768]{1,0:T(8,128)(2,1)S(1)}, u32[]{:S(2)}, u32[]{:S(2)}) collective-permute-start(bf16[144,768]{1,0:T(8,128)(2,1)S(1)} %project.2.a), channel_id=1, source_target_pairs={{0,8},{8,16},{16,24},{24,32},{32,40},{40,48},{48,56},{56,64},{64,7... | collective-permute-start | bytes 663560 | tf_op jit(solution)/shard_map/ppermute | solution.py:31
  14.5 11.6 %collective-permute-start.5 = (bf16[144,768]{1,0:T(8,128)(2,1)S(1)}, bf16[144,768]{1,0:T(8,128)(2,1)S(1)}, u32[]{:S(2)}, u32[]{:S(2)}) collective-permute-start(bf16[144,768]{1,0:T(8,128)(2,1)S(1)} %project.2.a), channel_id=1, source_target_pairs={{0,248},{8,0},{16,8},{24,16},{32,24},{40,32},{48,40},{56,48},{64,5... | collective-permute-start | bytes 663560 | tf_op jit(solution)/shard_map/ppermute | solution.py:31
  30.8 16.7 %collective-permute-start.13 = (bf16[384,3072]{1,0:T(8,128)(2,1)S(1)}, bf16[384,3072]{1,0:T(8,128)(2,1)S(1)}, u32[]{:S(2)}, u32[]{:S(2)}) collective-permute-start(bf16[384,3072]{1,0:T(8,128)(2,1)S(1)} %copy-done.2), channel_id=1, source_target_pairs={{0,1},{1,0},{2,3},{3,2},{4,5},{5,4},{6,7},{7,6},{8,9},{9,8},{10,11... | collective-permute-start | bytes 7077896 | tf_op jit(solution)/shard_map/ppermute | solution.py:39
  31.0 16.5 %collective-permute-start.11 = (bf16[256,768]{1,0:T(8,128)(2,1)S(1)}, bf16[256,768]{1,0:T(8,128)(2,1)}, u32[]{:S(2)}, u32[]{:S(2)}) collective-permute-start(bf16[256,768]{1,0:T(8,128)(2,1)S(1)} %get-tuple-element.67.b), channel_id=1, source_target_pairs={{0,8},{8,16},{16,24},{24,32},{32,40},{40,48},{48,56},{56,64},{64,7... | collective-permute-start | bytes 1179656 | tf_op jit(solution)/shard_map/ppermute | solution.py:31
  31.0 16.5 %collective-permute-start.12 = (bf16[256,768]{1,0:T(8,128)(2,1)S(1)}, bf16[256,768]{1,0:T(8,128)(2,1)}, u32[]{:S(2)}, u32[]{:S(2)}) collective-permute-start(bf16[256,768]{1,0:T(8,128)(2,1)S(1)} %get-tuple-element.67.b), channel_id=1, source_target_pairs={{0,248},{8,0},{16,8},{24,16},{32,24},{40,32},{48,40},{56,48},{64,5... | collective-permute-start | bytes 1179656 | tf_op jit(solution)/shard_map/ppermute | solution.py:31
  36.7 18.1 %collective-permute-start.16 = (bf16[256,768]{1,0:T(8,128)(2,1)S(1)}, bf16[256,768]{1,0:T(8,128)(2,1)}, u32[]{:S(2)}, u32[]{:S(2)}) collective-permute-start(bf16[256,768]{1,0:T(8,128)(2,1)S(1)} %get-tuple-element.68.c), channel_id=1, source_target_pairs={{0,8},{8,16},{16,24},{24,32},{32,40},{40,48},{48,56},{56,64},{64,7... | collective-permute-start | bytes 1179656 | tf_op jit(solution)/shard_map/ppermute | solution.py:31
  36.7 18.1 %collective-permute-start.9 = (bf16[256,768]{1,0:T(8,128)(2,1)S(1)}, bf16[256,768]{1,0:T(8,128)(2,1)}, u32[]{:S(2)}, u32[]{:S(2)}) collective-permute-start(bf16[256,768]{1,0:T(8,128)(2,1)S(1)} %get-tuple-element.65), channel_id=1, source_target_pairs={{0,248},{8,0},{16,8},{24,16},{32,24},{40,32},{48,40},{56,48},{64,5... | collective-permute-start | bytes 1179656 | tf_op jit(solution)/shard_map/ppermute | solution.py:31
  48.9 19.2 %collective-permute-start.14 = (bf16[256,768]{1,0:T(8,128)(2,1)}, bf16[256,768]{1,0:T(8,128)(2,1)}, u32[]{:S(2)}, u32[]{:S(2)}) collective-permute-start(bf16[256,768]{1,0:T(8,128)(2,1)} %collective-permute-done.11.rb), channel_id=1, source_target_pairs={{0,8},{8,16},{16,24},{24,32},{32,40},{40,48},{48,56},{56,64},{64,7... | collective-permute-start | bytes 1179656 | tf_op jit(solution)/shard_map/ppermute | solution.py:31
  48.9 19.2 %collective-permute-start.15 = (bf16[256,768]{1,0:T(8,128)(2,1)}, bf16[256,768]{1,0:T(8,128)(2,1)}, u32[]{:S(2)}, u32[]{:S(2)}) collective-permute-start(bf16[256,768]{1,0:T(8,128)(2,1)} %collective-permute-done.12.lb), channel_id=1, source_target_pairs={{0,248},{8,0},{16,8},{24,16},{32,24},{40,32},{48,40},{56,48},{64,5... | collective-permute-start | bytes 1179656 | tf_op jit(solution)/shard_map/ppermute | solution.py:31
  54.7 18.8 %collective-permute-start.19 = (bf16[256,768]{1,0:T(8,128)(2,1)}, bf16[256,768]{1,0:T(8,128)(2,1)S(1)}, u32[]{:S(2)}, u32[]{:S(2)}) collective-permute-start(bf16[256,768]{1,0:T(8,128)(2,1)} %collective-permute-done.16.rc.ra), channel_id=1, source_target_pairs={{0,8},{8,16},{16,24},{24,32},{32,40},{40,48},{48,56},{56,64},{64,7... | collective-permute-start | bytes 1179656 | tf_op jit(solution)/shard_map/ppermute | solution.py:31
  54.7 18.9 %collective-permute-start.10 = (bf16[256,768]{1,0:T(8,128)(2,1)}, bf16[256,768]{1,0:T(8,128)(2,1)S(1)}, u32[]{:S(2)}, u32[]{:S(2)}) collective-permute-start(bf16[256,768]{1,0:T(8,128)(2,1)} %collective-permute-done.9.lc.la), channel_id=1, source_target_pairs={{0,248},{8,0},{16,8},{24,16},{32,24},{40,32},{48,40},{56,48},{64,5... | collective-permute-start | bytes 1179656 | tf_op jit(solution)/shard_map/ppermute | solution.py:31
  68.1 18.0 %collective-permute-start.17 = (bf16[256,768]{1,0:T(8,128)(2,1)}, bf16[256,768]{1,0:T(8,128)(2,1)S(1)}, u32[]{:S(2)}, u32[]{:S(2)}) collective-permute-start(bf16[256,768]{1,0:T(8,128)(2,1)} %collective-permute-done.14.rb), channel_id=1, source_target_pairs={{0,8},{8,16},{16,24},{24,32},{32,40},{40,48},{48,56},{56,64},{64,7... | collective-permute-start | bytes 1179656 | tf_op jit(solution)/shard_map/ppermute | solution.py:31
  68.2 17.9 %collective-permute-start.18 = (bf16[256,768]{1,0:T(8,128)(2,1)}, bf16[256,768]{1,0:T(8,128)(2,1)S(1)}, u32[]{:S(2)}, u32[]{:S(2)}) collective-permute-start(bf16[256,768]{1,0:T(8,128)(2,1)} %collective-permute-done.15.lb), channel_id=1, source_target_pairs={{0,248},{8,0},{16,8},{24,16},{32,24},{40,32},{48,40},{56,48},{64,5... | collective-permute-start | bytes 1179656 | tf_op jit(solution)/shard_map/ppermute | solution.py:31
  73.5 12.5 %collective-permute-start.20 = (bf16[128,768]{1,0:T(8,128)(2,1)S(1)}, bf16[128,768]{1,0:T(8,128)(2,1)S(1)}, u32[]{:S(2)}, u32[]{:S(2)}) collective-permute-start(bf16[128,768]{1,0:T(8,128)(2,1)S(1)} %slice.20), channel_id=1, source_target_pairs={{0,8},{8,16},{16,24},{24,32},{32,40},{40,48},{48,56},{56,64},{64,7... | collective-permute-start | bytes 589832 | tf_op jit(solution)/shard_map/ppermute | solution.py:31
  73.7 12.4 %collective-permute-start.21 = (bf16[128,768]{1,0:T(8,128)(2,1)S(1)}, bf16[128,768]{1,0:T(8,128)(2,1)S(1)}, u32[]{:S(2)}, u32[]{:S(2)}) collective-permute-start(bf16[128,768]{1,0:T(8,128)(2,1)S(1)} %slice.21), channel_id=1, source_target_pairs={{0,248},{8,0},{16,8},{24,16},{32,24},{40,32},{48,40},{56,48},{64,5... | collective-permute-start | bytes 589832 | tf_op jit(solution)/shard_map/ppermute | solution.py:31
  86.8 11.8 %collective-permute-start.22 = (bf16[256,768]{1,0:T(8,128)(2,1)S(1)}, bf16[256,768]{1,0:T(8,128)(2,1)S(1)}, u32[]{:S(2)}, u32[]{:S(2)}) collective-permute-start(bf16[256,768]{1,0:T(8,128)(2,1)S(1)} %get-tuple-element.88), channel_id=1, source_target_pairs={{0,248},{8,0},{16,8},{24,16},{32,24},{40,32},{48,40},{56,48},{64,5... | collective-permute-start | bytes 1179656 | tf_op jit(solution)/shard_map/ppermute | solution.py:31
  92.1 12.0 %collective-permute-start.23 = (bf16[256,768]{1,0:T(8,128)(2,1)S(1)}, bf16[256,768]{1,0:T(8,128)(2,1)S(1)}, u32[]{:S(2)}, u32[]{:S(2)}) collective-permute-start(bf16[256,768]{1,0:T(8,128)(2,1)S(1)} %get-tuple-element.89), channel_id=1, source_target_pairs={{0,8},{8,16},{16,24},{24,32},{32,40},{40,48},{48,56},{56,64},{64,7... | collective-permute-start | bytes 1179656 | tf_op jit(solution)/shard_map/ppermute | solution.py:31
  105.9 7.6 %collective-permute-start.26 = (bf16[256,384]{1,0:T(8,128)(2,1)S(1)}, bf16[256,384]{1,0:T(8,128)(2,1)S(1)}, u32[]{:S(2)}, u32[]{:S(2)}) collective-permute-start(bf16[256,384]{1,0:T(8,128)(2,1)S(1)} %get-tuple-element.97), channel_id=1, source_target_pairs={{0,1},{1,0},{2,3},{3,2},{4,5},{5,4},{6,7},{7,6},{8,9},{9,8},{10,11... | collective-permute-start | bytes 589832 | tf_op jit(solution)/shard_map/ppermute | solution.py:39
  117.1 16.5 %collective-permute-start.27 = (bf16[64,3072]{1,0:T(8,128)(2,1)S(1)}, bf16[64,3072]{1,0:T(8,128)(2,1)S(1)}, u32[]{:S(2)}, u32[]{:S(2)}) collective-permute-start(bf16[64,3072]{1,0:T(8,128)(2,1)S(1)} %get-tuple-element.104), channel_id=1, source_target_pairs={{0,2},{1,3},{2,4},{3,5},{4,6},{5,7},{6,0},{7,1},{8,10},{9,11},{10,... | collective-permute-start | bytes 1179656 | tf_op jit(solution)/shard_map/ppermute | solution.py:35
  120.1 16.8 %collective-permute-start.28 = (bf16[64,3072]{1,0:T(8,128)(2,1)S(1)}, bf16[64,3072]{1,0:T(8,128)(2,1)S(1)}, u32[]{:S(2)}, u32[]{:S(2)}) collective-permute-start(bf16[64,3072]{1,0:T(8,128)(2,1)S(1)} %get-tuple-element.105), channel_id=1, source_target_pairs={{0,6},{1,7},{2,0},{3,1},{4,2},{5,3},{6,4},{7,5},{8,14},{9,15},{10,... | collective-permute-start | bytes 1179656 | tf_op jit(solution)/shard_map/ppermute | solution.py:35
  120.1 16.8 %collective-permute-start.29 = (bf16[64,3072]{1,0:T(8,128)(2,1)S(1)}, bf16[64,3072]{1,0:T(8,128)(2,1)S(1)}, u32[]{:S(2)}, u32[]{:S(2)}) collective-permute-start(bf16[64,3072]{1,0:T(8,128)(2,1)S(1)} %get-tuple-element.106), channel_id=1, source_target_pairs={{0,4},{1,5},{2,6},{3,7},{4,0},{5,1},{6,2},{7,3},{8,12},{9,13},{10,... | collective-permute-start | bytes 1179656 | tf_op jit(solution)/shard_map/ppermute | solution.py:35
  (28 other events, 165.8 us)

commit v6 on v5

--- a/solution.py
+++ b/solution.py
@@ -529,7 +529,7 @@
     q = project_q([mod0, sib0, mod1, sib1, mod3, sib3, mod2, sib2], *args)
     hop_args = (head, key_tiles, key_count, q)
     num, den = attend_own(q, (kv_a, kv_b, right_ac))
-    rb1, lb1, num, den, w_sib = barrier((rb1, lb1, num, den, w_sib))
+    rb1, lb1, num, den = barrier((rb1, lb1, num, den))
     rb2, lb2 = along_win(rb1, 1), along_win(lb1, -1)
     rac3, lac3 = along_win(rac2, 1), along_win(lac2, -1)
     num, den = attend_hop(1, (0, 1), *hop_args, (la1, lb1, lac2), (ra1, rb1, rac2), num, den)

time: 139 us -> 139 us (level)
  local copies, waits for them, and re-layouts: 15 us -> 13.6 us
    unnamed x44 -> x40, local copies, waits for them, and re-layouts: 14.2 us -> 12.8 us
  transfers between devices with their start and end apart: 30 -> 30, of which waited for: 11 -> 11; matrix products, arithmetic and copies ran while one was open for 1% -> 1% of each run, Pallas kernels for 13% -> 15%
where the time goes in v6:
time: 139 us; the launch traced here: 138 us
  starting transfers between devices  55.8 us (40%)
  waiting for transfers between devices  39.8 us (29%)
  Pallas kernels  27.3 us (20%)
  local copies, waits for them, and re-layouts  13.6 us (10%)
    ppermute x16, starting transfers between devices, along_win(): lax.ppermute(value, 'win', [(i, (i + steps) % WINDOWS) for i in range(WIN...  46.2 us
    ppermute x6, waiting for transfers between devices, to_y(): lax.ppermute(value, 'head', [(h, (h // 2 + steps) % 4 * 2 + h % 2) for h...  17.4 us
    ppermute x16, waiting for transfers between devices, along_win(): lax.ppermute(value, 'win', [(i, (i + steps) % WINDOWS) for i in range(WIN...  17.1 us
    unnamed x40, local copies, waits for them, and re-layouts  12.8 us
    pallas_call x3, Pallas kernels, attend_hop(): pl.pallas_call(functools.partial(hop_kernel, 4 * (hop - 1)), grid=(512 //...  8.78 us
    ppermute x6, starting transfers between devices, to_y(): lax.ppermute(value, 'head', [(h, (h // 2 + steps) % 4 * 2 + h % 2) for h...  8.04 us
    ppermute x1, waiting for transfers between devices, shards(): edge_own = lax.ppermute(edge_a, ('win', 'head'), strip_pairs(0))  4.71 us
    pallas_call x1, Pallas kernels, out_project(): pl.pallas_call(out_kernel, grid=(D // NCOL,), in_specs=[SMEM()] * 3 + [ou...  4.46 us
  transfers between devices with their start and end apart: 30, of which 11 were waited for; matrix products, arithmetic and copies ran while one was open for 1% of the time, Pallas kernels for 15%

profile of v6, /device:TPU:24, one launch (start us, length us, event | category | flops | bytes accessed | tf_op | source)
XLA Modules:
  0.0 138.5 jit_solution(15444440605081106163)
XLA Ops:
  3.1 2.5 %collective-permute-start.2 = (bf16[64,3072]{1,0:T(8,128)(2,1)S(1)}, bf16[64,3072]{1,0:T(8,128)(2,1)S(1)}, u32[]{:S(2)}, u32[]{:S(2)}) collective-permute-start(bf16[64,3072]{1,0:T(8,128)(2,1)S(1)} %modulate.1.refs_0_), channel_id=1, source_target_pairs={{0,2},{1,3},{2,4},{3,5},{4,6},{5,7},{6,0},{7,1},{8,10},{9,11},{10,... | collective-permute-start | bytes 1179656 | tf_op jit(solution)/shard_map/ppermute | solution.py:35
  5.8 3.0 %copy-done = bf16[3072,3,384]{2,0,1:T(8,128)(2,1)S(1)} copy-done((bf16[3072,3,384]{2,0,1:T(8,128)(2,1)S(1)}, bf16[3072,3,384]{2,0,1:T(8,128)(2,1)}, u32[]{:S(2)}) %copy-start) | copy-done | bytes 7077912
  14.5 6.2 %collective-permute-start.5 = (bf16[144,768]{1,0:T(8,128)(2,1)S(1)}, bf16[144,768]{1,0:T(8,128)(2,1)S(1)}, u32[]{:S(2)}, u32[]{:S(2)}) collective-permute-start(bf16[144,768]{1,0:T(8,128)(2,1)S(1)} %project.2.a), channel_id=1, source_target_pairs={{0,248},{8,0},{16,8},{24,16},{32,24},{40,32},{48,40},{56,48},{64,5... | collective-permute-start | bytes 663560 | tf_op jit(solution)/shard_map/ppermute | solution.py:31
  23.6 2.4 %collective-permute-done.4.ra = bf16[144,768]{1,0:T(8,128)(2,1)S(1)} collective-permute-done((bf16[144,768]{1,0:T(8,128)(2,1)S(1)}, bf16[144,768]{1,0:T(8,128)(2,1)S(1)}, u32[]{:S(2)}, u32[]{:S(2)}) %collective-permute-start.4) | collective-permute-done | bytes 221216 | tf_op jit(solution)/shard_map/ppermute | solution.py:31
  31.0 5.7 %collective-permute-start.12 = (bf16[256,768]{1,0:T(8,128)(2,1)S(1)}, bf16[256,768]{1,0:T(8,128)(2,1)}, u32[]{:S(2)}, u32[]{:S(2)}) collective-permute-start(bf16[256,768]{1,0:T(8,128)(2,1)S(1)} %get-tuple-element.66.b), channel_id=1, source_target_pairs={{0,248},{8,0},{16,8},{24,16},{32,24},{40,32},{48,40},{56,48},{64,5... | collective-permute-start | bytes 1179656 | tf_op jit(solution)/shard_map/ppermute | solution.py:31
  36.7 5.3 %collective-permute-start.9 = (bf16[256,768]{1,0:T(8,128)(2,1)S(1)}, bf16[256,768]{1,0:T(8,128)(2,1)}, u32[]{:S(2)}, u32[]{:S(2)}) collective-permute-start(bf16[256,768]{1,0:T(8,128)(2,1)S(1)} %get-tuple-element.64), channel_id=1, source_target_pairs={{0,248},{8,0},{16,8},{24,16},{32,24},{40,32},{48,40},{56,48},{64,5... | collective-permute-start | bytes 1179656 | tf_op jit(solution)/shard_map/ppermute | solution.py:31
  47.5 5.3 %collective-permute-start.14 = (bf16[256,768]{1,0:T(8,128)(2,1)}, bf16[256,768]{1,0:T(8,128)(2,1)}, u32[]{:S(2)}, u32[]{:S(2)}) collective-permute-start(bf16[256,768]{1,0:T(8,128)(2,1)} %collective-permute-done.12.lb), channel_id=1, source_target_pairs={{0,248},{8,0},{16,8},{24,16},{32,24},{40,32},{48,40},{56,48},{64,5... | collective-permute-start | bytes 1179656 | tf_op jit(solution)/shard_map/ppermute | solution.py:31
  52.9 2.1 %collective-permute-done.15.rc.ra = bf16[256,768]{1,0:T(8,128)(2,1)} collective-permute-done((bf16[256,768]{1,0:T(8,128)(2,1)S(1)}, bf16[256,768]{1,0:T(8,128)(2,1)}, u32[]{:S(2)}, u32[]{:S(2)}) %collective-permute-start.15) | collective-permute-done | bytes 393248 | tf_op jit(solution)/shard_map/ppermute | solution.py:31
  55.0 5.5 %collective-permute-start.10 = (bf16[256,768]{1,0:T(8,128)(2,1)}, bf16[256,768]{1,0:T(8,128)(2,1)S(1)}, u32[]{:S(2)}, u32[]{:S(2)}) collective-permute-start(bf16[256,768]{1,0:T(8,128)(2,1)} %collective-permute-done.9.lc.la), channel_id=1, source_target_pairs={{0,248},{8,0},{16,8},{24,16},{32,24},{40,32},{48,40},{56,48},{64,5... | collective-permute-start | bytes 1179656 | tf_op jit(solution)/shard_map/ppermute | solution.py:31
  65.3 3.2 %attend_hop.3 = (f32[512,384]{1,0:T(8,128)S(1)}, f32[512,384]{1,0:T(8,128)S(1)}) custom-call(s32[1]{0:T(128)} %bitcast.1.head, s32[1,16]{1,0:T(1,128)S(1)} %copy-done.17, s32[1]{0:T(128)S(6)} %copy.11.count, bf16[512,384]{1,0:T(8,128)(2,1)S(1)} %project.3.q, bf16[144,768]{1,0:T(8,128)(2,1)S(1)} %copy-done.8, bf16[256,768]{1,0:T(8,128)(2,1)} %collective-permute-done.12.lb, ...), custom_call_target="tpu_custom_call" | custom-call | flops 1 | bytes 1 | tf_op jit(solution)/shard_map/attend_hop/pallas_call | solution.py:353
  68.6 5.3 %collective-permute-start.17 = (bf16[256,768]{1,0:T(8,128)(2,1)}, bf16[256,768]{1,0:T(8,128)(2,1)S(1)}, u32[]{:S(2)}, u32[]{:S(2)}) collective-permute-start(bf16[256,768]{1,0:T(8,128)(2,1)} %collective-permute-done.14.lb), channel_id=1, source_target_pairs={{0,248},{8,0},{16,8},{24,16},{32,24},{40,32},{48,40},{56,48},{64,5... | collective-permute-start | bytes 1179656 | tf_op jit(solution)/shard_map/ppermute | solution.py:31
  74.1 5.4 %collective-permute-start.20 = (bf16[128,768]{1,0:T(8,128)(2,1)S(1)}, bf16[128,768]{1,0:T(8,128)(2,1)S(1)}, u32[]{:S(2)}, u32[]{:S(2)}) collective-permute-start(bf16[128,768]{1,0:T(8,128)(2,1)S(1)} %slice.21), channel_id=1, source_target_pairs={{0,248},{8,0},{16,8},{24,16},{32,24},{40,32},{48,40},{56,48},{64,5... | collective-permute-start | bytes 589832 | tf_op jit(solution)/shard_map/ppermute | solution.py:31
  79.5 3.2 %attend_hop.4 = (f32[512,384]{1,0:T(8,128)S(1)}, f32[512,384]{1,0:T(8,128)S(1)}) custom-call(s32[1]{0:T(128)} %bitcast.1.head, s32[1,16]{1,0:T(1,128)S(1)} %copy-done.17, s32[1]{0:T(128)S(6)} %copy.11.count, bf16[512,384]{1,0:T(8,128)(2,1)S(1)} %project.3.q, bf16[256,768]{1,0:T(8,128)(2,1)} %collective-permute-done.9.lc.la, ...), custom_call_target="tpu_custom_call" | custom-call | flops 1 | bytes 1 | tf_op jit(solution)/shard_map/attend_hop/pallas_call | solution.py:353
  82.7 3.4 %collective-permute-done.19.rc = bf16[128,768]{1,0:T(8,128)(2,1)S(1)} collective-permute-done((bf16[128,768]{1,0:T(8,128)(2,1)S(1)}, bf16[128,768]{1,0:T(8,128)(2,1)S(1)}, u32[]{:S(2)}, u32[]{:S(2)}) %collective-permute-start.19) | collective-permute-done | bytes 196640 | tf_op jit(solution)/shard_map/ppermute | solution.py:31
  86.8 5.4 %collective-permute-start.21 = (bf16[256,768]{1,0:T(8,128)(2,1)S(1)}, bf16[256,768]{1,0:T(8,128)(2,1)S(1)}, u32[]{:S(2)}, u32[]{:S(2)}) collective-permute-start(bf16[256,768]{1,0:T(8,128)(2,1)S(1)} %get-tuple-element.86), channel_id=1, source_target_pairs={{0,248},{8,0},{16,8},{24,16},{32,24},{40,32},{48,40},{56,48},{64,5... | collective-permute-start | bytes 1179656 | tf_op jit(solution)/shard_map/ppermute | solution.py:31
  92.1 2.4 %attend_hop.5 = (f32[512,384]{1,0:T(8,128)S(1)}, f32[512,384]{1,0:T(8,128)S(1)}) custom-call(s32[1]{0:T(128)} %bitcast.1.head, s32[1,16]{1,0:T(1,128)S(1)} %copy-done.17, s32[1]{0:T(128)S(6)} %copy.11.count, bf16[512,384]{1,0:T(8,128)(2,1)S(1)} %project.3.q, bf16[256,768]{1,0:T(8,128)(2,1)S(1)} %collective-permute-done.10.lc.la, ...), custom_call_target="tpu_custom_call" | custom-call | flops 1 | bytes 1 | tf_op jit(solution)/shard_map/attend_hop/pallas_call | solution.py:353
  94.6 3.6 %collective-permute-done.21.left = bf16[256,768]{1,0:T(8,128)(2,1)S(1)} collective-permute-done((bf16[256,768]{1,0:T(8,128)(2,1)S(1)}, bf16[256,768]{1,0:T(8,128)(2,1)S(1)}, u32[]{:S(2)}, u32[]{:S(2)}) %collective-permute-start.21) | collective-permute-done | bytes 393248 | tf_op jit(solution)/shard_map/ppermute | solution.py:31
  98.2 5.5 %collective-permute-done.22.right = bf16[256,768]{1,0:T(8,128)(2,1)S(1)} collective-permute-done((bf16[256,768]{1,0:T(8,128)(2,1)S(1)}, bf16[256,768]{1,0:T(8,128)(2,1)S(1)}, u32[]{:S(2)}, u32[]{:S(2)}) %collective-permute-start.22) | collective-permute-done | bytes 393248 | tf_op jit(solution)/shard_map/ppermute | solution.py:31
  106.0 2.4 %out_own.1.part = f32[256,3072]{1,0:T(8,128)S(1)} custom-call(s32[1]{0:T(128)} %bitcast.1.head, s32[1]{0:T(128)} %bitcast.2.window, s32[32]{0:T(128)S(1)} %copy-done.18, bf16[256,384]{1,0:T(8,128)(2,1)S(1)} %get-tuple-element.92.own, bf16[384,3072]{1,0:T(8,128)(2,1)S(1)} %copy-done.2), custom_call_target="tpu_custom_call" | custom-call | flops 1 | bytes 1 | tf_op jit(solution)/shard_map/out_own/pallas_call | solution.py:464
  108.4 4.7 %collective-permute-done.23.edge_own = bf16[64,384]{1,0:T(8,128)(2,1)S(1)} collective-permute-done((bf16[64,384]{1,0:T(8,128)(2,1)S(1)}, bf16[64,384]{1,0:T(8,128)(2,1)S(1)}, u32[]{:S(2)}, u32[]{:S(2)}) %collective-permute-start.23) | collective-permute-done | bytes 49184 | tf_op jit(solution)/shard_map/ppermute | solution.py:548
  113.1 4.5 %out_project.1 = (f32[64,3072]{1,0:T(8,128)S(1)}, bf16[64,3072]{1,0:T(8,128)(2,1)S(1)}, bf16[64,3072]{1,0:T(8,128)(2,1)S(1)}, bf16[64,3072]{1,0:T(8,128)(2,1)S(1)}) custom-call(s32[1]{0:T(128)} %bitcast.1.head, s32[1]{0:T(128)} %bitcast.2.window, s32[32]{0:T(128)S(1)} %copy-done.18, f32[256,3072]{1,0:T(8,128)S(1)} %out_own.1.part, ...), custom_call_target="tpu_custom_call" | custom-call | flops 1 | bytes 1 | tf_op jit(solution)/shard_map/out_project/pallas_call | solution.py:479
  117.6 3.0 %collective-permute-start.27 = (bf16[64,3072]{1,0:T(8,128)(2,1)S(1)}, bf16[64,3072]{1,0:T(8,128)(2,1)S(1)}, u32[]{:S(2)}, u32[]{:S(2)}) collective-permute-start(bf16[64,3072]{1,0:T(8,128)(2,1)S(1)} %get-tuple-element.102), channel_id=1, source_target_pairs={{0,2},{1,3},{2,4},{3,5},{4,6},{5,7},{6,0},{7,1},{8,10},{9,11},{10,... | collective-permute-start | bytes 1179656 | tf_op jit(solution)/shard_map/ppermute | solution.py:35
  123.0 11.1 %collective-permute-done.27 = bf16[64,3072]{1,0:T(8,128)(2,1)S(1)} collective-permute-done((bf16[64,3072]{1,0:T(8,128)(2,1)S(1)}, bf16[64,3072]{1,0:T(8,128)(2,1)S(1)}, u32[]{:S(2)}, u32[]{:S(2)}) %collective-permute-start.27) | collective-permute-done | bytes 393248 | tf_op jit(solution)/shard_map/ppermute | solution.py:35
  134.1 3.4 %collective-permute-done.28 = bf16[64,3072]{1,0:T(8,128)(2,1)S(1)} collective-permute-done((bf16[64,3072]{1,0:T(8,128)(2,1)S(1)}, bf16[64,3072]{1,0:T(8,128)(2,1)S(1)}, u32[]{:S(2)}, u32[]{:S(2)}) %collective-permute-start.28) | collective-permute-done | bytes 393248 | tf_op jit(solution)/shard_map/ppermute | solution.py:35
  (94 shorter events, 32.9 us)
Async XLA Ops:
  2.3 18.4 %collective-permute-start.1 = (bf16[64,3072]{1,0:T(8,128)(2,1)S(1)}, bf16[64,3072]{1,0:T(8,128)(2,1)S(1)}, u32[]{:S(2)}, u32[]{:S(2)}) collective-permute-start(bf16[64,3072]{1,0:T(8,128)(2,1)S(1)} %modulate.1.refs_0_), channel_id=1, source_target_pairs={{0,6},{1,7},{2,0},{3,1},{4,2},{5,3},{6,4},{7,5},{8,14},{9,15},{10,... | collective-permute-start | bytes 1179656 | tf_op jit(solution)/shard_map/ppermute | solution.py:35
  3.1 19.6 %collective-permute-start.2 = (bf16[64,3072]{1,0:T(8,128)(2,1)S(1)}, bf16[64,3072]{1,0:T(8,128)(2,1)S(1)}, u32[]{:S(2)}, u32[]{:S(2)}) collective-permute-start(bf16[64,3072]{1,0:T(8,128)(2,1)S(1)} %modulate.1.refs_0_), channel_id=1, source_target_pairs={{0,2},{1,3},{2,4},{3,5},{4,6},{5,7},{6,0},{7,1},{8,10},{9,11},{10,... | collective-permute-start | bytes 1179656 | tf_op jit(solution)/shard_map/ppermute | solution.py:35
  5.6 18.0 %collective-permute-start.3 = (bf16[64,3072]{1,0:T(8,128)(2,1)S(1)}, bf16[64,3072]{1,0:T(8,128)(2,1)S(1)}, u32[]{:S(2)}, u32[]{:S(2)}) collective-permute-start(bf16[64,3072]{1,0:T(8,128)(2,1)S(1)} %modulate.1.refs_0_), channel_id=1, source_target_pairs={{0,4},{1,5},{2,6},{3,7},{4,0},{5,1},{6,2},{7,3},{8,12},{9,13},{10,... | collective-permute-start | bytes 1179656 | tf_op jit(solution)/shard_map/ppermute | solution.py:35
  12.6 13.4 %collective-permute-start.4 = (bf16[144,768]{1,0:T(8,128)(2,1)S(1)}, bf16[144,768]{1,0:T(8,128)(2,1)S(1)}, u32[]{:S(2)}, u32[]{:S(2)}) collective-permute-start(bf16[144,768]{1,0:T(8,128)(2,1)S(1)} %project.2.a), channel_id=1, source_target_pairs={{0,8},{8,16},{16,24},{24,32},{32,40},{40,48},{48,56},{56,64},{64,7... | collective-permute-start | bytes 663560 | tf_op jit(solution)/shard_map/ppermute | solution.py:31
  14.5 11.6 %collective-permute-start.5 = (bf16[144,768]{1,0:T(8,128)(2,1)S(1)}, bf16[144,768]{1,0:T(8,128)(2,1)S(1)}, u32[]{:S(2)}, u32[]{:S(2)}) collective-permute-start(bf16[144,768]{1,0:T(8,128)(2,1)S(1)} %project.2.a), channel_id=1, source_target_pairs={{0,248},{8,0},{16,8},{24,16},{32,24},{40,32},{48,40},{56,48},{64,5... | collective-permute-start | bytes 663560 | tf_op jit(solution)/shard_map/ppermute | solution.py:31
  30.8 82.4 %collective-permute-start.26 = (bf16[384,3072]{1,0:T(8,128)(2,1)S(1)}, bf16[384,3072]{1,0:T(8,128)(2,1)}, u32[]{:S(2)}, u32[]{:S(2)}) collective-permute-start(bf16[384,3072]{1,0:T(8,128)(2,1)S(1)} %copy-done.2), channel_id=1, source_target_pairs={{0,1},{1,0},{2,3},{3,2},{4,5},{5,4},{6,7},{7,6},{8,9},{9,8},{10,11... | collective-permute-start | bytes 7077896 | tf_op jit(solution)/shard_map/ppermute | solution.py:39
  31.0 16.5 %collective-permute-start.11 = (bf16[256,768]{1,0:T(8,128)(2,1)S(1)}, bf16[256,768]{1,0:T(8,128)(2,1)}, u32[]{:S(2)}, u32[]{:S(2)}) collective-permute-start(bf16[256,768]{1,0:T(8,128)(2,1)S(1)} %get-tuple-element.66.b), channel_id=1, source_target_pairs={{0,8},{8,16},{16,24},{24,32},{32,40},{40,48},{48,56},{56,64},{64,7... | collective-permute-start | bytes 1179656 | tf_op jit(solution)/shard_map/ppermute | solution.py:31
  31.0 16.5 %collective-permute-start.12 = (bf16[256,768]{1,0:T(8,128)(2,1)S(1)}, bf16[256,768]{1,0:T(8,128)(2,1)}, u32[]{:S(2)}, u32[]{:S(2)}) collective-permute-start(bf16[256,768]{1,0:T(8,128)(2,1)S(1)} %get-tuple-element.66.b), channel_id=1, source_target_pairs={{0,248},{8,0},{16,8},{24,16},{32,24},{40,32},{48,40},{56,48},{64,5... | collective-permute-start | bytes 1179656 | tf_op jit(solution)/shard_map/ppermute | solution.py:31
  36.7 18.3 %collective-permute-start.15 = (bf16[256,768]{1,0:T(8,128)(2,1)S(1)}, bf16[256,768]{1,0:T(8,128)(2,1)}, u32[]{:S(2)}, u32[]{:S(2)}) collective-permute-start(bf16[256,768]{1,0:T(8,128)(2,1)S(1)} %get-tuple-element.67.c), channel_id=1, source_target_pairs={{0,8},{8,16},{16,24},{24,32},{32,40},{40,48},{48,56},{56,64},{64,7... | collective-permute-start | bytes 1179656 | tf_op jit(solution)/shard_map/ppermute | solution.py:31
  36.7 18.3 %collective-permute-start.9 = (bf16[256,768]{1,0:T(8,128)(2,1)S(1)}, bf16[256,768]{1,0:T(8,128)(2,1)}, u32[]{:S(2)}, u32[]{:S(2)}) collective-permute-start(bf16[256,768]{1,0:T(8,128)(2,1)S(1)} %get-tuple-element.64), channel_id=1, source_target_pairs={{0,248},{8,0},{16,8},{24,16},{32,24},{40,32},{48,40},{56,48},{64,5... | collective-permute-start | bytes 1179656 | tf_op jit(solution)/shard_map/ppermute | solution.py:31
  47.5 21.0 %collective-permute-start.13 = (bf16[256,768]{1,0:T(8,128)(2,1)}, bf16[256,768]{1,0:T(8,128)(2,1)}, u32[]{:S(2)}, u32[]{:S(2)}) collective-permute-start(bf16[256,768]{1,0:T(8,128)(2,1)} %collective-permute-done.11.rb), channel_id=1, source_target_pairs={{0,8},{8,16},{16,24},{24,32},{32,40},{40,48},{48,56},{56,64},{64,7... | collective-permute-start | bytes 1179656 | tf_op jit(solution)/shard_map/ppermute | solution.py:31
  47.5 21.0 %collective-permute-start.14 = (bf16[256,768]{1,0:T(8,128)(2,1)}, bf16[256,768]{1,0:T(8,128)(2,1)}, u32[]{:S(2)}, u32[]{:S(2)}) collective-permute-start(bf16[256,768]{1,0:T(8,128)(2,1)} %collective-permute-done.12.lb), channel_id=1, source_target_pairs={{0,248},{8,0},{16,8},{24,16},{32,24},{40,32},{48,40},{56,48},{64,5... | collective-permute-start | bytes 1179656 | tf_op jit(solution)/shard_map/ppermute | solution.py:31
  54.9 19.0 %collective-permute-start.18 = (bf16[256,768]{1,0:T(8,128)(2,1)}, bf16[256,768]{1,0:T(8,128)(2,1)S(1)}, u32[]{:S(2)}, u32[]{:S(2)}) collective-permute-start(bf16[256,768]{1,0:T(8,128)(2,1)} %collective-permute-done.15.rc.ra), channel_id=1, source_target_pairs={{0,8},{8,16},{16,24},{24,32},{32,40},{40,48},{48,56},{56,64},{64,7... | collective-permute-start | bytes 1179656 | tf_op jit(solution)/shard_map/ppermute | solution.py:31
  55.0 19.1 %collective-permute-start.10 = (bf16[256,768]{1,0:T(8,128)(2,1)}, bf16[256,768]{1,0:T(8,128)(2,1)S(1)}, u32[]{:S(2)}, u32[]{:S(2)}) collective-permute-start(bf16[256,768]{1,0:T(8,128)(2,1)} %collective-permute-done.9.lc.la), channel_id=1, source_target_pairs={{0,248},{8,0},{16,8},{24,16},{32,24},{40,32},{48,40},{56,48},{64,5... | collective-permute-start | bytes 1179656 | tf_op jit(solution)/shard_map/ppermute | solution.py:31
  68.5 17.6 %collective-permute-start.16 = (bf16[256,768]{1,0:T(8,128)(2,1)}, bf16[256,768]{1,0:T(8,128)(2,1)S(1)}, u32[]{:S(2)}, u32[]{:S(2)}) collective-permute-start(bf16[256,768]{1,0:T(8,128)(2,1)} %collective-permute-done.13.rb), channel_id=1, source_target_pairs={{0,8},{8,16},{16,24},{24,32},{32,40},{40,48},{48,56},{56,64},{64,7... | collective-permute-start | bytes 1179656 | tf_op jit(solution)/shard_map/ppermute | solution.py:31
  68.6 17.5 %collective-permute-start.17 = (bf16[256,768]{1,0:T(8,128)(2,1)}, bf16[256,768]{1,0:T(8,128)(2,1)S(1)}, u32[]{:S(2)}, u32[]{:S(2)}) collective-permute-start(bf16[256,768]{1,0:T(8,128)(2,1)} %collective-permute-done.14.lb), channel_id=1, source_target_pairs={{0,248},{8,0},{16,8},{24,16},{32,24},{40,32},{48,40},{56,48},{64,5... | collective-permute-start | bytes 1179656 | tf_op jit(solution)/shard_map/ppermute | solution.py:31
  73.9 12.1 %collective-permute-start.19 = (bf16[128,768]{1,0:T(8,128)(2,1)S(1)}, bf16[128,768]{1,0:T(8,128)(2,1)S(1)}, u32[]{:S(2)}, u32[]{:S(2)}) collective-permute-start(bf16[128,768]{1,0:T(8,128)(2,1)S(1)} %slice.20), channel_id=1, source_target_pairs={{0,8},{8,16},{16,24},{24,32},{32,40},{40,48},{48,56},{56,64},{64,7... | collective-permute-start | bytes 589832 | tf_op jit(solution)/shard_map/ppermute | solution.py:31
  74.1 12.0 %collective-permute-start.20 = (bf16[128,768]{1,0:T(8,128)(2,1)S(1)}, bf16[128,768]{1,0:T(8,128)(2,1)S(1)}, u32[]{:S(2)}, u32[]{:S(2)}) collective-permute-start(bf16[128,768]{1,0:T(8,128)(2,1)S(1)} %slice.21), channel_id=1, source_target_pairs={{0,248},{8,0},{16,8},{24,16},{32,24},{40,32},{48,40},{56,48},{64,5... | collective-permute-start | bytes 589832 | tf_op jit(solution)/shard_map/ppermute | solution.py:31
  86.8 11.4 %collective-permute-start.21 = (bf16[256,768]{1,0:T(8,128)(2,1)S(1)}, bf16[256,768]{1,0:T(8,128)(2,1)S(1)}, u32[]{:S(2)}, u32[]{:S(2)}) collective-permute-start(bf16[256,768]{1,0:T(8,128)(2,1)S(1)} %get-tuple-element.86), channel_id=1, source_target_pairs={{0,248},{8,0},{16,8},{24,16},{32,24},{40,32},{48,40},{56,48},{64,5... | collective-permute-start | bytes 1179656 | tf_op jit(solution)/shard_map/ppermute | solution.py:31
  92.1 11.6 %collective-permute-start.22 = (bf16[256,768]{1,0:T(8,128)(2,1)S(1)}, bf16[256,768]{1,0:T(8,128)(2,1)S(1)}, u32[]{:S(2)}, u32[]{:S(2)}) collective-permute-start(bf16[256,768]{1,0:T(8,128)(2,1)S(1)} %get-tuple-element.87), channel_id=1, source_target_pairs={{0,8},{8,16},{16,24},{24,32},{32,40},{40,48},{48,56},{56,64},{64,7... | collective-permute-start | bytes 1179656 | tf_op jit(solution)/shard_map/ppermute | solution.py:31
  105.5 7.6 %collective-permute-start.25 = (bf16[256,384]{1,0:T(8,128)(2,1)S(1)}, bf16[256,384]{1,0:T(8,128)(2,1)S(1)}, u32[]{:S(2)}, u32[]{:S(2)}) collective-permute-start(bf16[256,384]{1,0:T(8,128)(2,1)S(1)} %get-tuple-element.95), channel_id=1, source_target_pairs={{0,1},{1,0},{2,3},{3,2},{4,5},{5,4},{6,7},{7,6},{8,9},{9,8},{10,11... | collective-permute-start | bytes 589832 | tf_op jit(solution)/shard_map/ppermute | solution.py:39
  117.6 16.5 %collective-permute-start.27 = (bf16[64,3072]{1,0:T(8,128)(2,1)S(1)}, bf16[64,3072]{1,0:T(8,128)(2,1)S(1)}, u32[]{:S(2)}, u32[]{:S(2)}) collective-permute-start(bf16[64,3072]{1,0:T(8,128)(2,1)S(1)} %get-tuple-element.102), channel_id=1, source_target_pairs={{0,2},{1,3},{2,4},{3,5},{4,6},{5,7},{6,0},{7,1},{8,10},{9,11},{10,... | collective-permute-start | bytes 1179656 | tf_op jit(solution)/shard_map/ppermute | solution.py:35
  120.6 16.9 %collective-permute-start.28 = (bf16[64,3072]{1,0:T(8,128)(2,1)S(1)}, bf16[64,3072]{1,0:T(8,128)(2,1)S(1)}, u32[]{:S(2)}, u32[]{:S(2)}) collective-permute-start(bf16[64,3072]{1,0:T(8,128)(2,1)S(1)} %get-tuple-element.103), channel_id=1, source_target_pairs={{0,6},{1,7},{2,0},{3,1},{4,2},{5,3},{6,4},{7,5},{8,14},{9,15},{10,... | collective-permute-start | bytes 1179656 | tf_op jit(solution)/shard_map/ppermute | solution.py:35
  120.6 16.9 %collective-permute-start.29 = (bf16[64,3072]{1,0:T(8,128)(2,1)S(1)}, bf16[64,3072]{1,0:T(8,128)(2,1)S(1)}, u32[]{:S(2)}, u32[]{:S(2)}) collective-permute-start(bf16[64,3072]{1,0:T(8,128)(2,1)S(1)} %get-tuple-element.104), channel_id=1, source_target_pairs={{0,4},{1,5},{2,6},{3,7},{4,0},{5,1},{6,2},{7,3},{8,12},{9,13},{10,... | collective-permute-start | bytes 1179656 | tf_op jit(solution)/shard_map/ppermute | solution.py:35
  (26 other events, 159.1 us)

commit v7 on v5

--- a/solution.py
+++ b/solution.py
@@ -532,9 +532,10 @@
     rb1, lb1, num, den, w_sib = barrier((rb1, lb1, num, den, w_sib))
     rb2, lb2 = along_win(rb1, 1), along_win(lb1, -1)
     rac3, lac3 = along_win(rac2, 1), along_win(lac2, -1)
-    num, den = attend_hop(1, (0, 1), *hop_args, (la1, lb1, lac2), (ra1, rb1, rac2), num, den)
     rb2, lb2, num, den = barrier((rb2, lb2, num, den))
     rb3, lb3 = along_win(rb2, 1), along_win(lb2, -1)
+    num, den = attend_hop(1, (0, 1), *hop_args, (la1, lb1, lac2), (ra1, rb1, rac2), num, den)
+    rac3, lac3, num, den = barrier((rac3, lac3, num, den))
     rc3, lc3 = along_win(rac3[TILE:], 1), along_win(lac3[TILE:], -1)
     num, den = attend_hop(2, (0, 1), *hop_args, (lac2, lb2, lac3), (rac2, rb2, rac3), num, den)
     rb3, lb3, rc3, lc3, num, den = barrier((rb3, lb3, rc3, lc3, num, den))

time: 139 us -> 142 us (1.022)
  local copies, waits for them, and re-layouts: 15 us -> 18.5 us
  waiting for transfers between devices: 38.9 us -> 36.7 us
    unnamed x44 -> x52, local copies, waits for them, and re-layouts: 14.2 us -> 17.7 us
    ppermute x16, waiting for transfers between devices: 16.3 us -> 14.4 us  [along_win(): lax.ppermute(value, 'win', [(i, (i + steps) % WINDOWS) for i in range(WIN...]
  transfers between devices with their start and end apart: 30 -> 30, of which waited for: 11 -> 12; matrix products, arithmetic and copies ran while one was open for 1% -> 1% of each run, Pallas kernels for 13% -> 13%
where the time goes in v7:
time: 142 us; the launch traced here: 141 us
  starting transfers between devices  56.7 us (40%)
  waiting for transfers between devices  36.7 us (26%)
  Pallas kernels  27.4 us (19%)
  local copies, waits for them, and re-layouts  18.5 us (13%)
    ppermute x16, starting transfers between devices, along_win(): lax.ppermute(value, 'win', [(i, (i + steps) % WINDOWS) for i in range(WIN...  46.9 us
    unnamed x52, local copies, waits for them, and re-layouts  17.7 us
    ppermute x6, waiting for transfers between devices, to_y(): lax.ppermute(value, 'head', [(h, (h // 2 + steps) % 4 * 2 + h % 2) for h...  16.9 us
    ppermute x16, waiting for transfers between devices, along_win(): lax.ppermute(value, 'win', [(i, (i + steps) % WINDOWS) for i in range(WIN...  14.4 us
    pallas_call x3, Pallas kernels, attend_hop(): pl.pallas_call(functools.partial(hop_kernel, 4 * (hop - 1)), grid=(512 //...  9.12 us
    ppermute x6, starting transfers between devices, to_y(): lax.ppermute(value, 'head', [(h, (h // 2 + steps) % 4 * 2 + h % 2) for h...  8.51 us
    ppermute x1, waiting for transfers between devices, shards(): edge_own = lax.ppermute(edge_a, ('win', 'head'), strip_pairs(0))  4.89 us
    pallas_call x2, Pallas kernels, project(): pl.pallas_call(kernel, grid=(count,), in_specs=[whole((ROWS, D))] * parts...  3.79 us
  transfers between devices with their start and end apart: 30, of which 12 were waited for; matrix products, arithmetic and copies ran while one was open for 1% of the time, Pallas kernels for 13%

profile of v7, /device:TPU:24, one launch (start us, length us, event | category | flops | bytes accessed | tf_op | source)
XLA Modules:
  0.0 141.3 jit_solution(14904991589481202918)
XLA Ops:
  3.1 2.5 %collective-permute-start.2 = (bf16[64,3072]{1,0:T(8,128)(2,1)S(1)}, bf16[64,3072]{1,0:T(8,128)(2,1)S(1)}, u32[]{:S(2)}, u32[]{:S(2)}) collective-permute-start(bf16[64,3072]{1,0:T(8,128)(2,1)S(1)} %modulate.1.refs_0_), channel_id=1, source_target_pairs={{0,2},{1,3},{2,4},{3,5},{4,6},{5,7},{6,0},{7,1},{8,10},{9,11},{10,... | collective-permute-start | bytes 1179656 | tf_op jit(solution)/shard_map/ppermute | solution.py:35
  5.8 3.0 %copy-done = bf16[3072,3,384]{2,0,1:T(8,128)(2,1)S(1)} copy-done((bf16[3072,3,384]{2,0,1:T(8,128)(2,1)S(1)}, bf16[3072,3,384]{2,0,1:T(8,128)(2,1)}, u32[]{:S(2)}) %copy-start) | copy-done | bytes 7077912
  14.5 6.2 %collective-permute-start.5 = (bf16[144,768]{1,0:T(8,128)(2,1)S(1)}, bf16[144,768]{1,0:T(8,128)(2,1)S(1)}, u32[]{:S(2)}, u32[]{:S(2)}) collective-permute-start(bf16[144,768]{1,0:T(8,128)(2,1)S(1)} %project.2.a), channel_id=1, source_target_pairs={{0,248},{8,0},{16,8},{24,16},{32,24},{40,32},{48,40},{56,48},{64,5... | collective-permute-start | bytes 663560 | tf_op jit(solution)/shard_map/ppermute | solution.py:31
  20.7 2.0 %collective-permute-done.2.m3.refs_4_ = bf16[64,3072]{1,0:T(8,128)(2,1)S(1)} collective-permute-done((bf16[64,3072]{1,0:T(8,128)(2,1)S(1)}, bf16[64,3072]{1,0:T(8,128)(2,1)S(1)}, u32[]{:S(2)}, u32[]{:S(2)}) %collective-permute-start.2) | collective-permute-done | bytes 393248 | tf_op jit(solution)/shard_map/ppermute | solution.py:35
  23.6 2.4 %collective-permute-done.4.ra = bf16[144,768]{1,0:T(8,128)(2,1)S(1)} collective-permute-done((bf16[144,768]{1,0:T(8,128)(2,1)S(1)}, bf16[144,768]{1,0:T(8,128)(2,1)S(1)}, u32[]{:S(2)}, u32[]{:S(2)}) %collective-permute-start.4) | collective-permute-done | bytes 221216 | tf_op jit(solution)/shard_map/ppermute | solution.py:31
  31.0 5.7 %collective-permute-start.14 = (bf16[256,768]{1,0:T(8,128)(2,1)S(1)}, bf16[256,768]{1,0:T(8,128)(2,1)S(1)}, u32[]{:S(2)}, u32[]{:S(2)}) collective-permute-start(bf16[256,768]{1,0:T(8,128)(2,1)S(1)} %get-tuple-element.72.b), channel_id=1, source_target_pairs={{0,248},{8,0},{16,8},{24,16},{32,24},{40,32},{48,40},{56,48},{64,5... | collective-permute-start | bytes 1179656 | tf_op jit(solution)/shard_map/ppermute | solution.py:31
  36.7 5.3 %collective-permute-start.11 = (bf16[256,768]{1,0:T(8,128)(2,1)S(1)}, bf16[256,768]{1,0:T(8,128)(2,1)}, u32[]{:S(2)}, u32[]{:S(2)}) collective-permute-start(bf16[256,768]{1,0:T(8,128)(2,1)S(1)} %get-tuple-element.70), channel_id=1, source_target_pairs={{0,248},{8,0},{16,8},{24,16},{32,24},{40,32},{48,40},{56,48},{64,5... | collective-permute-start | bytes 1179656 | tf_op jit(solution)/shard_map/ppermute | solution.py:31
  49.7 5.3 %collective-permute-start.17 = (bf16[256,768]{1,0:T(8,128)(2,1)S(1)}, bf16[256,768]{1,0:T(8,128)(2,1)}, u32[]{:S(2)}, u32[]{:S(2)}) collective-permute-start(bf16[256,768]{1,0:T(8,128)(2,1)S(1)} %collective-permute-done.14.lb), channel_id=1, source_target_pairs={{0,248},{8,0},{16,8},{24,16},{32,24},{40,32},{48,40},{56,48},{64,5... | collective-permute-start | bytes 1179656 | tf_op jit(solution)/shard_map/ppermute | solution.py:31
  55.8 5.3 %collective-permute-start.12 = (bf16[256,768]{1,0:T(8,128)(2,1)}, bf16[256,768]{1,0:T(8,128)(2,1)S(1)}, u32[]{:S(2)}, u32[]{:S(2)}) collective-permute-start(bf16[256,768]{1,0:T(8,128)(2,1)} %collective-permute-done.11.lc.la), channel_id=1, source_target_pairs={{0,248},{8,0},{16,8},{24,16},{32,24},{40,32},{48,40},{56,48},{64,5... | collective-permute-start | bytes 1179656 | tf_op jit(solution)/shard_map/ppermute | solution.py:31
  61.1 3.3 %collective-permute-done.16.rb = bf16[256,768]{1,0:T(8,128)(2,1)} collective-permute-done((bf16[256,768]{1,0:T(8,128)(2,1)S(1)}, bf16[256,768]{1,0:T(8,128)(2,1)}, u32[]{:S(2)}, u32[]{:S(2)}) %collective-permute-start.16) | collective-permute-done | bytes 393248 | tf_op jit(solution)/shard_map/ppermute | solution.py:31
  64.6 5.9 %collective-permute-start.19 = (bf16[256,768]{1,0:T(8,128)(2,1)}, bf16[256,768]{1,0:T(8,128)(2,1)}, u32[]{:S(2)}, u32[]{:S(2)}) collective-permute-start(bf16[256,768]{1,0:T(8,128)(2,1)} %collective-permute-done.17.lb), channel_id=1, source_target_pairs={{0,248},{8,0},{16,8},{24,16},{32,24},{40,32},{48,40},{56,48},{64,5... | collective-permute-start | bytes 1179656 | tf_op jit(solution)/shard_map/ppermute | solution.py:31
  77.3 2.9 %attend_hop.3 = (f32[512,384]{1,0:T(8,128)S(1)}, f32[512,384]{1,0:T(8,128)S(1)}) custom-call(s32[1]{0:T(128)} %bitcast.1.head, s32[1,16]{1,0:T(1,128)S(1)} %copy-done.23, s32[1]{0:T(128)S(6)} %copy.11.count, bf16[512,384]{1,0:T(8,128)(2,1)S(1)} %project.3.q, bf16[144,768]{1,0:T(8,128)(2,1)S(1)} %copy-done.10, bf16[256,768]{1,0:T(8,128)(2,1)S(1)} %copy-done.18, ...), custom_call_target="tpu_custom_call" | custom-call | flops 1 | bytes 1 | tf_op jit(solution)/shard_map/attend_hop/pallas_call | solution.py:353
  80.4 5.4 %collective-permute-start.21 = (bf16[128,768]{1,0:T(8,128)(2,1)S(1)}, bf16[128,768]{1,0:T(8,128)(2,1)S(1)}, u32[]{:S(2)}, u32[]{:S(2)}) collective-permute-start(bf16[128,768]{1,0:T(8,128)(2,1)S(1)} %slice.19), channel_id=1, source_target_pairs={{0,248},{8,0},{16,8},{24,16},{32,24},{40,32},{48,40},{56,48},{64,5... | collective-permute-start | bytes 589832 | tf_op jit(solution)/shard_map/ppermute | solution.py:31
  85.8 3.2 %attend_hop.4 = (f32[512,384]{1,0:T(8,128)S(1)}, f32[512,384]{1,0:T(8,128)S(1)}) custom-call(s32[1]{0:T(128)} %bitcast.1.head, s32[1,16]{1,0:T(1,128)S(1)} %copy-done.23, s32[1]{0:T(128)S(6)} %copy.11.count, bf16[512,384]{1,0:T(8,128)(2,1)S(1)} %project.3.q, bf16[256,768]{1,0:T(8,128)(2,1)} %collective-permute-done.11.lc.la, ...), custom_call_target="tpu_custom_call" | custom-call | flops 1 | bytes 1 | tf_op jit(solution)/shard_map/attend_hop/pallas_call | solution.py:353
  90.6 5.7 %collective-permute-start.22 = (bf16[256,768]{1,0:T(8,128)(2,1)S(1)}, bf16[256,768]{1,0:T(8,128)(2,1)S(1)}, u32[]{:S(2)}, u32[]{:S(2)}) collective-permute-start(bf16[256,768]{1,0:T(8,128)(2,1)S(1)} %get-tuple-element.96), channel_id=1, source_target_pairs={{0,248},{8,0},{16,8},{24,16},{32,24},{40,32},{48,40},{56,48},{64,5... | collective-permute-start | bytes 1179656 | tf_op jit(solution)/shard_map/ppermute | solution.py:31
  96.4 3.0 %attend_hop.5 = (f32[512,384]{1,0:T(8,128)S(1)}, f32[512,384]{1,0:T(8,128)S(1)}) custom-call(s32[1]{0:T(128)} %bitcast.1.head, s32[1,16]{1,0:T(1,128)S(1)} %copy-done.23, s32[1]{0:T(128)S(6)} %copy.11.count, bf16[512,384]{1,0:T(8,128)(2,1)S(1)} %project.3.q, bf16[256,768]{1,0:T(8,128)(2,1)S(1)} %collective-permute-done.12.lc.la, ...), custom_call_target="tpu_custom_call" | custom-call | flops 1 | bytes 1 | tf_op jit(solution)/shard_map/attend_hop/pallas_call | solution.py:353
  99.4 2.3 %collective-permute-done.22.left = bf16[256,768]{1,0:T(8,128)(2,1)S(1)} collective-permute-done((bf16[256,768]{1,0:T(8,128)(2,1)S(1)}, bf16[256,768]{1,0:T(8,128)(2,1)S(1)}, u32[]{:S(2)}, u32[]{:S(2)}) %collective-permute-start.22) | collective-permute-done | bytes 393248 | tf_op jit(solution)/shard_map/ppermute | solution.py:31
  101.7 5.8 %collective-permute-done.23.right = bf16[256,768]{1,0:T(8,128)(2,1)S(1)} collective-permute-done((bf16[256,768]{1,0:T(8,128)(2,1)S(1)}, bf16[256,768]{1,0:T(8,128)(2,1)S(1)}, u32[]{:S(2)}, u32[]{:S(2)}) %collective-permute-start.23) | collective-permute-done | bytes 393248 | tf_op jit(solution)/shard_map/ppermute | solution.py:31
  109.5 2.4 %out_own.1.part = f32[256,3072]{1,0:T(8,128)S(1)} custom-call(s32[1]{0:T(128)} %bitcast.1.head, s32[1]{0:T(128)} %bitcast.2.window, s32[32]{0:T(128)S(1)} %copy-done.24, bf16[256,384]{1,0:T(8,128)(2,1)S(1)} %get-tuple-element.102.own, bf16[384,3072]{1,0:T(8,128)(2,1)S(1)} %copy-done.2), custom_call_target="tpu_custom_call" | custom-call | flops 1 | bytes 1 | tf_op jit(solution)/shard_map/out_own/pallas_call | solution.py:464
  112.0 4.9 %collective-permute-done.24.edge_own = bf16[64,384]{1,0:T(8,128)(2,1)S(1)} collective-permute-done((bf16[64,384]{1,0:T(8,128)(2,1)S(1)}, bf16[64,384]{1,0:T(8,128)(2,1)S(1)}, u32[]{:S(2)}, u32[]{:S(2)}) %collective-permute-start.24) | collective-permute-done | bytes 49184 | tf_op jit(solution)/shard_map/ppermute | solution.py:549
  116.9 3.6 %out_project.1 = (f32[64,3072]{1,0:T(8,128)S(1)}, bf16[64,3072]{1,0:T(8,128)(2,1)S(1)}, bf16[64,3072]{1,0:T(8,128)(2,1)S(1)}, bf16[64,3072]{1,0:T(8,128)(2,1)S(1)}) custom-call(s32[1]{0:T(128)} %bitcast.1.head, s32[1]{0:T(128)} %bitcast.2.window, s32[32]{0:T(128)S(1)} %copy-done.24, f32[256,3072]{1,0:T(8,128)S(1)} %out_own.1.part, ...), custom_call_target="tpu_custom_call" | custom-call | flops 1 | bytes 1 | tf_op jit(solution)/shard_map/out_project/pallas_call | solution.py:479
  120.4 3.0 %collective-permute-start.27 = (bf16[64,3072]{1,0:T(8,128)(2,1)S(1)}, bf16[64,3072]{1,0:T(8,128)(2,1)S(1)}, u32[]{:S(2)}, u32[]{:S(2)}) collective-permute-start(bf16[64,3072]{1,0:T(8,128)(2,1)S(1)} %get-tuple-element.112), channel_id=1, source_target_pairs={{0,2},{1,3},{2,4},{3,5},{4,6},{5,7},{6,0},{7,1},{8,10},{9,11},{10,... | collective-permute-start | bytes 1179656 | tf_op jit(solution)/shard_map/ppermute | solution.py:35
  126.3 10.6 %collective-permute-done.27 = bf16[64,3072]{1,0:T(8,128)(2,1)S(1)} collective-permute-done((bf16[64,3072]{1,0:T(8,128)(2,1)S(1)}, bf16[64,3072]{1,0:T(8,128)(2,1)S(1)}, u32[]{:S(2)}, u32[]{:S(2)}) %collective-permute-start.27) | collective-permute-done | bytes 393248 | tf_op jit(solution)/shard_map/ppermute | solution.py:35
  136.9 3.4 %collective-permute-done.28 = bf16[64,3072]{1,0:T(8,128)(2,1)S(1)} collective-permute-done((bf16[64,3072]{1,0:T(8,128)(2,1)S(1)}, bf16[64,3072]{1,0:T(8,128)(2,1)S(1)}, u32[]{:S(2)}, u32[]{:S(2)}) %collective-permute-start.28) | collective-permute-done | bytes 393248 | tf_op jit(solution)/shard_map/ppermute | solution.py:35
  (106 shorter events, 37.0 us)
Async XLA Ops:
  2.3 18.4 %collective-permute-start.1 = (bf16[64,3072]{1,0:T(8,128)(2,1)S(1)}, bf16[64,3072]{1,0:T(8,128)(2,1)S(1)}, u32[]{:S(2)}, u32[]{:S(2)}) collective-permute-start(bf16[64,3072]{1,0:T(8,128)(2,1)S(1)} %modulate.1.refs_0_), channel_id=1, source_target_pairs={{0,6},{1,7},{2,0},{3,1},{4,2},{5,3},{6,4},{7,5},{8,14},{9,15},{10,... | collective-permute-start | bytes 1179656 | tf_op jit(solution)/shard_map/ppermute | solution.py:35
  3.1 19.6 %collective-permute-start.2 = (bf16[64,3072]{1,0:T(8,128)(2,1)S(1)}, bf16[64,3072]{1,0:T(8,128)(2,1)S(1)}, u32[]{:S(2)}, u32[]{:S(2)}) collective-permute-start(bf16[64,3072]{1,0:T(8,128)(2,1)S(1)} %modulate.1.refs_0_), channel_id=1, source_target_pairs={{0,2},{1,3},{2,4},{3,5},{4,6},{5,7},{6,0},{7,1},{8,10},{9,11},{10,... | collective-permute-start | bytes 1179656 | tf_op jit(solution)/shard_map/ppermute | solution.py:35
  5.6 18.0 %collective-permute-start.3 = (bf16[64,3072]{1,0:T(8,128)(2,1)S(1)}, bf16[64,3072]{1,0:T(8,128)(2,1)S(1)}, u32[]{:S(2)}, u32[]{:S(2)}) collective-permute-start(bf16[64,3072]{1,0:T(8,128)(2,1)S(1)} %modulate.1.refs_0_), channel_id=1, source_target_pairs={{0,4},{1,5},{2,6},{3,7},{4,0},{5,1},{6,2},{7,3},{8,12},{9,13},{10,... | collective-permute-start | bytes 1179656 | tf_op jit(solution)/shard_map/ppermute | solution.py:35
  12.6 13.4 %collective-permute-start.4 = (bf16[144,768]{1,0:T(8,128)(2,1)S(1)}, bf16[144,768]{1,0:T(8,128)(2,1)S(1)}, u32[]{:S(2)}, u32[]{:S(2)}) collective-permute-start(bf16[144,768]{1,0:T(8,128)(2,1)S(1)} %project.2.a), channel_id=1, source_target_pairs={{0,8},{8,16},{16,24},{24,32},{32,40},{40,48},{48,56},{56,64},{64,7... | collective-permute-start | bytes 663560 | tf_op jit(solution)/shard_map/ppermute | solution.py:31
  14.5 11.6 %collective-permute-start.5 = (bf16[144,768]{1,0:T(8,128)(2,1)S(1)}, bf16[144,768]{1,0:T(8,128)(2,1)S(1)}, u32[]{:S(2)}, u32[]{:S(2)}) collective-permute-start(bf16[144,768]{1,0:T(8,128)(2,1)S(1)} %project.2.a), channel_id=1, source_target_pairs={{0,248},{8,0},{16,8},{24,16},{32,24},{40,32},{48,40},{56,48},{64,5... | collective-permute-start | bytes 663560 | tf_op jit(solution)/shard_map/ppermute | solution.py:31
  30.8 16.8 %collective-permute-start.15 = (bf16[384,3072]{1,0:T(8,128)(2,1)S(1)}, bf16[384,3072]{1,0:T(8,128)(2,1)S(1)}, u32[]{:S(2)}, u32[]{:S(2)}) collective-permute-start(bf16[384,3072]{1,0:T(8,128)(2,1)S(1)} %copy-done.2), channel_id=1, source_target_pairs={{0,1},{1,0},{2,3},{3,2},{4,5},{5,4},{6,7},{7,6},{8,9},{9,8},{10,11... | collective-permute-start | bytes 7077896 | tf_op jit(solution)/shard_map/ppermute | solution.py:39
  31.0 16.5 %collective-permute-start.13 = (bf16[256,768]{1,0:T(8,128)(2,1)S(1)}, bf16[256,768]{1,0:T(8,128)(2,1)S(1)}, u32[]{:S(2)}, u32[]{:S(2)}) collective-permute-start(bf16[256,768]{1,0:T(8,128)(2,1)S(1)} %get-tuple-element.72.b), channel_id=1, source_target_pairs={{0,8},{8,16},{16,24},{24,32},{32,40},{40,48},{48,56},{56,64},{64,7... | collective-permute-start | bytes 1179656 | tf_op jit(solution)/shard_map/ppermute | solution.py:31
  31.0 16.5 %collective-permute-start.14 = (bf16[256,768]{1,0:T(8,128)(2,1)S(1)}, bf16[256,768]{1,0:T(8,128)(2,1)S(1)}, u32[]{:S(2)}, u32[]{:S(2)}) collective-permute-start(bf16[256,768]{1,0:T(8,128)(2,1)S(1)} %get-tuple-element.72.b), channel_id=1, source_target_pairs={{0,248},{8,0},{16,8},{24,16},{32,24},{40,32},{48,40},{56,48},{64,5... | collective-permute-start | bytes 1179656 | tf_op jit(solution)/shard_map/ppermute | solution.py:31
  36.7 19.1 %collective-permute-start.9 = (bf16[256,768]{1,0:T(8,128)(2,1)S(1)}, bf16[256,768]{1,0:T(8,128)(2,1)}, u32[]{:S(2)}, u32[]{:S(2)}) collective-permute-start(bf16[256,768]{1,0:T(8,128)(2,1)S(1)} %get-tuple-element.69.c), channel_id=1, source_target_pairs={{0,8},{8,16},{16,24},{24,32},{32,40},{40,48},{48,56},{56,64},{64,7... | collective-permute-start | bytes 1179656 | tf_op jit(solution)/shard_map/ppermute | solution.py:31
  36.7 19.1 %collective-permute-start.11 = (bf16[256,768]{1,0:T(8,128)(2,1)S(1)}, bf16[256,768]{1,0:T(8,128)(2,1)}, u32[]{:S(2)}, u32[]{:S(2)}) collective-permute-start(bf16[256,768]{1,0:T(8,128)(2,1)S(1)} %get-tuple-element.70), channel_id=1, source_target_pairs={{0,248},{8,0},{16,8},{24,16},{32,24},{40,32},{48,40},{56,48},{64,5... | collective-permute-start | bytes 1179656 | tf_op jit(solution)/shard_map/ppermute | solution.py:31
  49.0 15.5 %collective-permute-start.16 = (bf16[256,768]{1,0:T(8,128)(2,1)S(1)}, bf16[256,768]{1,0:T(8,128)(2,1)}, u32[]{:S(2)}, u32[]{:S(2)}) collective-permute-start(bf16[256,768]{1,0:T(8,128)(2,1)S(1)} %collective-permute-done.13.rb), channel_id=1, source_target_pairs={{0,8},{8,16},{16,24},{24,32},{32,40},{40,48},{48,56},{56,64},{64,7... | collective-permute-start | bytes 1179656 | tf_op jit(solution)/shard_map/ppermute | solution.py:31
  49.7 14.9 %collective-permute-start.17 = (bf16[256,768]{1,0:T(8,128)(2,1)S(1)}, bf16[256,768]{1,0:T(8,128)(2,1)}, u32[]{:S(2)}, u32[]{:S(2)}) collective-permute-start(bf16[256,768]{1,0:T(8,128)(2,1)S(1)} %collective-permute-done.14.lb), channel_id=1, source_target_pairs={{0,248},{8,0},{16,8},{24,16},{32,24},{40,32},{48,40},{56,48},{64,5... | collective-permute-start | bytes 1179656 | tf_op jit(solution)/shard_map/ppermute | solution.py:31
  55.8 24.5 %collective-permute-start.10 = (bf16[256,768]{1,0:T(8,128)(2,1)}, bf16[256,768]{1,0:T(8,128)(2,1)S(1)}, u32[]{:S(2)}, u32[]{:S(2)}) collective-permute-start(bf16[256,768]{1,0:T(8,128)(2,1)} %collective-permute-done.9.rc.ra), channel_id=1, source_target_pairs={{0,8},{8,16},{16,24},{24,32},{32,40},{40,48},{48,56},{56,64},{64,7... | collective-permute-start | bytes 1179656 | tf_op jit(solution)/shard_map/ppermute | solution.py:31
  55.8 24.5 %collective-permute-start.12 = (bf16[256,768]{1,0:T(8,128)(2,1)}, bf16[256,768]{1,0:T(8,128)(2,1)S(1)}, u32[]{:S(2)}, u32[]{:S(2)}) collective-permute-start(bf16[256,768]{1,0:T(8,128)(2,1)} %collective-permute-done.11.lc.la), channel_id=1, source_target_pairs={{0,248},{8,0},{16,8},{24,16},{32,24},{40,32},{48,40},{56,48},{64,5... | collective-permute-start | bytes 1179656 | tf_op jit(solution)/shard_map/ppermute | solution.py:31
  64.6 24.8 %collective-permute-start.18 = (bf16[256,768]{1,0:T(8,128)(2,1)}, bf16[256,768]{1,0:T(8,128)(2,1)}, u32[]{:S(2)}, u32[]{:S(2)}) collective-permute-start(bf16[256,768]{1,0:T(8,128)(2,1)} %collective-permute-done.16.rb), channel_id=1, source_target_pairs={{0,8},{8,16},{16,24},{24,32},{32,40},{40,48},{48,56},{56,64},{64,7... | collective-permute-start | bytes 1179656 | tf_op jit(solution)/shard_map/ppermute | solution.py:31
  64.6 24.8 %collective-permute-start.19 = (bf16[256,768]{1,0:T(8,128)(2,1)}, bf16[256,768]{1,0:T(8,128)(2,1)}, u32[]{:S(2)}, u32[]{:S(2)}) collective-permute-start(bf16[256,768]{1,0:T(8,128)(2,1)} %collective-permute-done.17.lb), channel_id=1, source_target_pairs={{0,248},{8,0},{16,8},{24,16},{32,24},{40,32},{48,40},{56,48},{64,5... | collective-permute-start | bytes 1179656 | tf_op jit(solution)/shard_map/ppermute | solution.py:31
  80.3 9.1 %collective-permute-start.20 = (bf16[128,768]{1,0:T(8,128)(2,1)S(1)}, bf16[128,768]{1,0:T(8,128)(2,1)S(1)}, u32[]{:S(2)}, u32[]{:S(2)}) collective-permute-start(bf16[128,768]{1,0:T(8,128)(2,1)S(1)} %slice.18), channel_id=1, source_target_pairs={{0,8},{8,16},{16,24},{24,32},{32,40},{40,48},{48,56},{56,64},{64,7... | collective-permute-start | bytes 589832 | tf_op jit(solution)/shard_map/ppermute | solution.py:31
  80.4 9.0 %collective-permute-start.21 = (bf16[128,768]{1,0:T(8,128)(2,1)S(1)}, bf16[128,768]{1,0:T(8,128)(2,1)S(1)}, u32[]{:S(2)}, u32[]{:S(2)}) collective-permute-start(bf16[128,768]{1,0:T(8,128)(2,1)S(1)} %slice.19), channel_id=1, source_target_pairs={{0,248},{8,0},{16,8},{24,16},{32,24},{40,32},{48,40},{56,48},{64,5... | collective-permute-start | bytes 589832 | tf_op jit(solution)/shard_map/ppermute | solution.py:31
  90.6 11.0 %collective-permute-start.22 = (bf16[256,768]{1,0:T(8,128)(2,1)S(1)}, bf16[256,768]{1,0:T(8,128)(2,1)S(1)}, u32[]{:S(2)}, u32[]{:S(2)}) collective-permute-start(bf16[256,768]{1,0:T(8,128)(2,1)S(1)} %get-tuple-element.96), channel_id=1, source_target_pairs={{0,248},{8,0},{16,8},{24,16},{32,24},{40,32},{48,40},{56,48},{64,5... | collective-permute-start | bytes 1179656 | tf_op jit(solution)/shard_map/ppermute | solution.py:31
  96.4 11.1 %collective-permute-start.23 = (bf16[256,768]{1,0:T(8,128)(2,1)S(1)}, bf16[256,768]{1,0:T(8,128)(2,1)S(1)}, u32[]{:S(2)}, u32[]{:S(2)}) collective-permute-start(bf16[256,768]{1,0:T(8,128)(2,1)S(1)} %get-tuple-element.97), channel_id=1, source_target_pairs={{0,8},{8,16},{16,24},{24,32},{32,40},{40,48},{48,56},{56,64},{64,7... | collective-permute-start | bytes 1179656 | tf_op jit(solution)/shard_map/ppermute | solution.py:31
  109.2 7.6 %collective-permute-start.26 = (bf16[256,384]{1,0:T(8,128)(2,1)S(1)}, bf16[256,384]{1,0:T(8,128)(2,1)S(1)}, u32[]{:S(2)}, u32[]{:S(2)}) collective-permute-start(bf16[256,384]{1,0:T(8,128)(2,1)S(1)} %get-tuple-element.105), channel_id=1, source_target_pairs={{0,1},{1,0},{2,3},{3,2},{4,5},{5,4},{6,7},{7,6},{8,9},{9,8},{10,11... | collective-permute-start | bytes 589832 | tf_op jit(solution)/shard_map/ppermute | solution.py:39
  120.4 16.5 %collective-permute-start.27 = (bf16[64,3072]{1,0:T(8,128)(2,1)S(1)}, bf16[64,3072]{1,0:T(8,128)(2,1)S(1)}, u32[]{:S(2)}, u32[]{:S(2)}) collective-permute-start(bf16[64,3072]{1,0:T(8,128)(2,1)S(1)} %get-tuple-element.112), channel_id=1, source_target_pairs={{0,2},{1,3},{2,4},{3,5},{4,6},{5,7},{6,0},{7,1},{8,10},{9,11},{10,... | collective-permute-start | bytes 1179656 | tf_op jit(solution)/shard_map/ppermute | solution.py:35
  123.4 16.9 %collective-permute-start.28 = (bf16[64,3072]{1,0:T(8,128)(2,1)S(1)}, bf16[64,3072]{1,0:T(8,128)(2,1)S(1)}, u32[]{:S(2)}, u32[]{:S(2)}) collective-permute-start(bf16[64,3072]{1,0:T(8,128)(2,1)S(1)} %get-tuple-element.113), channel_id=1, source_target_pairs={{0,6},{1,7},{2,0},{3,1},{4,2},{5,3},{6,4},{7,5},{8,14},{9,15},{10,... | collective-permute-start | bytes 1179656 | tf_op jit(solution)/shard_map/ppermute | solution.py:35
  123.4 16.9 %collective-permute-start.29 = (bf16[64,3072]{1,0:T(8,128)(2,1)S(1)}, bf16[64,3072]{1,0:T(8,128)(2,1)S(1)}, u32[]{:S(2)}, u32[]{:S(2)}) collective-permute-start(bf16[64,3072]{1,0:T(8,128)(2,1)S(1)} %get-tuple-element.114), channel_id=1, source_target_pairs={{0,4},{1,5},{2,6},{3,7},{4,0},{5,1},{6,2},{7,3},{8,12},{9,13},{10,... | collective-permute-start | bytes 1179656 | tf_op jit(solution)/shard_map/ppermute | solution.py:35
  (32 other events, 179.2 us)

commit v8 on v6

--- a/solution.py
+++ b/solution.py
@@ -529,7 +529,7 @@
     q = project_q([mod0, sib0, mod1, sib1, mod3, sib3, mod2, sib2], *args)
     hop_args = (head, key_tiles, key_count, q)
     num, den = attend_own(q, (kv_a, kv_b, right_ac))
-    rb1, lb1, num, den = barrier((rb1, lb1, num, den))
+    rac2, lac2, num, den, w_sib = barrier((rac2, lac2, num, den, w_sib))
     rb2, lb2 = along_win(rb1, 1), along_win(lb1, -1)
     rac3, lac3 = along_win(rac2, 1), along_win(lac2, -1)
     num, den = attend_hop(1, (0, 1), *hop_args, (la1, lb1, lac2), (ra1, rb1, rac2), num, den)

time: 139 us -> 141 us (1.014)
  waiting for transfers between devices: 39.8 us -> 44.3 us
  starting transfers between devices: 55.8 us -> 52.6 us
    ppermute x16, waiting for transfers between devices: 17.1 us -> 21.8 us  [along_win(): lax.ppermute(value, 'win', [(i, (i + steps) % WINDOWS) for i in range(WIN...]
    ppermute x16, starting transfers between devices: 46.2 us -> 42.9 us  [along_win(): lax.ppermute(value, 'win', [(i, (i + steps) % WINDOWS) for i in range(WIN...]
    unnamed x40 -> x44, local copies, waits for them, and re-layouts: 12.8 us -> 14.2 us
  transfers between devices with their start and end apart: 30 -> 30, of which waited for: 11 -> 12; matrix products, arithmetic and copies ran while one was open for 1% -> 1% of each run, Pallas kernels for 15% -> 13%
where the time goes in v8:
time: 141 us; the launch traced here: 140 us
  starting transfers between devices  52.6 us (37%)
  waiting for transfers between devices  44.3 us (31%)
  Pallas kernels  26.4 us (19%)
  local copies, waits for them, and re-layouts  15 us (11%)
    ppermute x16, starting transfers between devices, along_win(): lax.ppermute(value, 'win', [(i, (i + steps) % WINDOWS) for i in range(WIN...  42.9 us
    ppermute x16, waiting for transfers between devices, along_win(): lax.ppermute(value, 'win', [(i, (i + steps) % WINDOWS) for i in range(WIN...  21.8 us
    ppermute x6, waiting for transfers between devices, to_y(): lax.ppermute(value, 'head', [(h, (h // 2 + steps) % 4 * 2 + h % 2) for h...  17.3 us
    unnamed x44, local copies, waits for them, and re-layouts  14.2 us
    pallas_call x3, Pallas kernels, attend_hop(): pl.pallas_call(functools.partial(hop_kernel, 4 * (hop - 1)), grid=(512 //...  8.78 us
    ppermute x6, starting transfers between devices, to_y(): lax.ppermute(value, 'head', [(h, (h // 2 + steps) % 4 * 2 + h % 2) for h...  8.23 us
    ppermute x1, waiting for transfers between devices, shards(): edge_own = lax.ppermute(edge_a, ('win', 'head'), strip_pairs(0))  4.78 us
    pallas_call x2, Pallas kernels, project(): pl.pallas_call(kernel, grid=(count,), in_specs=[whole((ROWS, D))] * parts...  3.79 us
  transfers between devices with their start and end apart: 30, of which 12 were waited for; matrix products, arithmetic and copies ran while one was open for 1% of the time, Pallas kernels for 13%

profile of v8, /device:TPU:24, one launch (start us, length us, event | category | flops | bytes accessed | tf_op | source)
XLA Modules:
  0.0 140.3 jit_solution(1734014695394585755)
XLA Ops:
  3.1 2.5 %collective-permute-start.2 = (bf16[64,3072]{1,0:T(8,128)(2,1)S(1)}, bf16[64,3072]{1,0:T(8,128)(2,1)S(1)}, u32[]{:S(2)}, u32[]{:S(2)}) collective-permute-start(bf16[64,3072]{1,0:T(8,128)(2,1)S(1)} %modulate.1.refs_0_), channel_id=1, source_target_pairs={{0,2},{1,3},{2,4},{3,5},{4,6},{5,7},{6,0},{7,1},{8,10},{9,11},{10,... | collective-permute-start | bytes 1179656 | tf_op jit(solution)/shard_map/ppermute | solution.py:35
  5.8 3.0 %copy-done = bf16[3072,3,384]{2,0,1:T(8,128)(2,1)S(1)} copy-done((bf16[3072,3,384]{2,0,1:T(8,128)(2,1)S(1)}, bf16[3072,3,384]{2,0,1:T(8,128)(2,1)}, u32[]{:S(2)}) %copy-start) | copy-done | bytes 7077912
  14.5 6.2 %collective-permute-start.5 = (bf16[144,768]{1,0:T(8,128)(2,1)S(1)}, bf16[144,768]{1,0:T(8,128)(2,1)S(1)}, u32[]{:S(2)}, u32[]{:S(2)}) collective-permute-start(bf16[144,768]{1,0:T(8,128)(2,1)S(1)} %project.2.a), channel_id=1, source_target_pairs={{0,248},{8,0},{16,8},{24,16},{32,24},{40,32},{48,40},{56,48},{64,5... | collective-permute-start | bytes 663560 | tf_op jit(solution)/shard_map/ppermute | solution.py:31
  20.7 2.0 %collective-permute-done.2.m3.refs_4_ = bf16[64,3072]{1,0:T(8,128)(2,1)S(1)} collective-permute-done((bf16[64,3072]{1,0:T(8,128)(2,1)S(1)}, bf16[64,3072]{1,0:T(8,128)(2,1)S(1)}, u32[]{:S(2)}, u32[]{:S(2)}) %collective-permute-start.2) | collective-permute-done | bytes 393248 | tf_op jit(solution)/shard_map/ppermute | solution.py:35
  23.6 2.4 %collective-permute-done.4.ra = bf16[144,768]{1,0:T(8,128)(2,1)S(1)} collective-permute-done((bf16[144,768]{1,0:T(8,128)(2,1)S(1)}, bf16[144,768]{1,0:T(8,128)(2,1)S(1)}, u32[]{:S(2)}, u32[]{:S(2)}) %collective-permute-start.4) | collective-permute-done | bytes 221216 | tf_op jit(solution)/shard_map/ppermute | solution.py:31
  31.0 5.7 %collective-permute-start.15 = (bf16[256,768]{1,0:T(8,128)(2,1)S(1)}, bf16[256,768]{1,0:T(8,128)(2,1)}, u32[]{:S(2)}, u32[]{:S(2)}) collective-permute-start(bf16[256,768]{1,0:T(8,128)(2,1)S(1)} %get-tuple-element.68.b), channel_id=1, source_target_pairs={{0,248},{8,0},{16,8},{24,16},{32,24},{40,32},{48,40},{56,48},{64,5... | collective-permute-start | bytes 1179656 | tf_op jit(solution)/shard_map/ppermute | solution.py:31
  38.7 7.8 %collective-permute-done.13.rb = bf16[256,768]{1,0:T(8,128)(2,1)} collective-permute-done((bf16[256,768]{1,0:T(8,128)(2,1)S(1)}, bf16[256,768]{1,0:T(8,128)(2,1)}, u32[]{:S(2)}, u32[]{:S(2)}) %collective-permute-start.13) | collective-permute-done | bytes 393248 | tf_op jit(solution)/shard_map/ppermute | solution.py:31
  46.5 5.5 %collective-permute-start.16 = (bf16[256,768]{1,0:T(8,128)(2,1)}, bf16[256,768]{1,0:T(8,128)(2,1)}, u32[]{:S(2)}, u32[]{:S(2)}) collective-permute-start(bf16[256,768]{1,0:T(8,128)(2,1)} %collective-permute-done.15.lb), channel_id=1, source_target_pairs={{0,248},{8,0},{16,8},{24,16},{32,24},{40,32},{48,40},{56,48},{64,5... | collective-permute-start | bytes 1179656 | tf_op jit(solution)/shard_map/ppermute | solution.py:31
  59.0 5.3 %collective-permute-start.12 = (bf16[256,768]{1,0:T(8,128)(2,1)}, bf16[256,768]{1,0:T(8,128)(2,1)S(1)}, u32[]{:S(2)}, u32[]{:S(2)}) collective-permute-start(bf16[256,768]{1,0:T(8,128)(2,1)} %collective-permute-done.10.lc.la), channel_id=1, source_target_pairs={{0,248},{8,0},{16,8},{24,16},{32,24},{40,32},{48,40},{56,48},{64,5... | collective-permute-start | bytes 1179656 | tf_op jit(solution)/shard_map/ppermute | solution.py:31
  69.1 3.2 %attend_hop.3 = (f32[512,384]{1,0:T(8,128)S(1)}, f32[512,384]{1,0:T(8,128)S(1)}) custom-call(s32[1]{0:T(128)} %bitcast.1.head, s32[1,16]{1,0:T(1,128)S(1)} %copy-done.19, s32[1]{0:T(128)S(6)} %copy.11.count, bf16[512,384]{1,0:T(8,128)(2,1)S(1)} %project.3.q, bf16[144,768]{1,0:T(8,128)(2,1)S(1)} %copy-done.10, bf16[256,768]{1,0:T(8,128)(2,1)} %collective-permute-done.15.lb, ...), custom_call_target="tpu_custom_call" | custom-call | flops 1 | bytes 1 | tf_op jit(solution)/shard_map/attend_hop/pallas_call | solution.py:353
  72.4 5.3 %collective-permute-start.18 = (bf16[256,768]{1,0:T(8,128)(2,1)}, bf16[256,768]{1,0:T(8,128)(2,1)S(1)}, u32[]{:S(2)}, u32[]{:S(2)}) collective-permute-start(bf16[256,768]{1,0:T(8,128)(2,1)} %collective-permute-done.16.lb), channel_id=1, source_target_pairs={{0,248},{8,0},{16,8},{24,16},{32,24},{40,32},{48,40},{56,48},{64,5... | collective-permute-start | bytes 1179656 | tf_op jit(solution)/shard_map/ppermute | solution.py:31
  77.9 5.4 %collective-permute-start.21 = (bf16[128,768]{1,0:T(8,128)(2,1)S(1)}, bf16[128,768]{1,0:T(8,128)(2,1)S(1)}, u32[]{:S(2)}, u32[]{:S(2)}) collective-permute-start(bf16[128,768]{1,0:T(8,128)(2,1)S(1)} %slice.21), channel_id=1, source_target_pairs={{0,248},{8,0},{16,8},{24,16},{32,24},{40,32},{48,40},{56,48},{64,5... | collective-permute-start | bytes 589832 | tf_op jit(solution)/shard_map/ppermute | solution.py:31
  83.3 3.2 %attend_hop.4 = (f32[512,384]{1,0:T(8,128)S(1)}, f32[512,384]{1,0:T(8,128)S(1)}) custom-call(s32[1]{0:T(128)} %bitcast.1.head, s32[1,16]{1,0:T(1,128)S(1)} %copy-done.19, s32[1]{0:T(128)S(6)} %copy.11.count, bf16[512,384]{1,0:T(8,128)(2,1)S(1)} %project.3.q, bf16[256,768]{1,0:T(8,128)(2,1)} %collective-permute-done.10.lc.la, ...), custom_call_target="tpu_custom_call" | custom-call | flops 1 | bytes 1 | tf_op jit(solution)/shard_map/attend_hop/pallas_call | solution.py:353
  87.2 2.1 %collective-permute-done.20.rc = bf16[128,768]{1,0:T(8,128)(2,1)S(1)} collective-permute-done((bf16[128,768]{1,0:T(8,128)(2,1)S(1)}, bf16[128,768]{1,0:T(8,128)(2,1)S(1)}, u32[]{:S(2)}, u32[]{:S(2)}) %collective-permute-start.20) | collective-permute-done | bytes 196640 | tf_op jit(solution)/shard_map/ppermute | solution.py:31
  90.0 5.4 %collective-permute-start.22 = (bf16[256,768]{1,0:T(8,128)(2,1)S(1)}, bf16[256,768]{1,0:T(8,128)(2,1)S(1)}, u32[]{:S(2)}, u32[]{:S(2)}) collective-permute-start(bf16[256,768]{1,0:T(8,128)(2,1)S(1)} %get-tuple-element.88), channel_id=1, source_target_pairs={{0,248},{8,0},{16,8},{24,16},{32,24},{40,32},{48,40},{56,48},{64,5... | collective-permute-start | bytes 1179656 | tf_op jit(solution)/shard_map/ppermute | solution.py:31
  95.3 2.4 %attend_hop.5 = (f32[512,384]{1,0:T(8,128)S(1)}, f32[512,384]{1,0:T(8,128)S(1)}) custom-call(s32[1]{0:T(128)} %bitcast.1.head, s32[1,16]{1,0:T(1,128)S(1)} %copy-done.19, s32[1]{0:T(128)S(6)} %copy.11.count, bf16[512,384]{1,0:T(8,128)(2,1)S(1)} %project.3.q, bf16[256,768]{1,0:T(8,128)(2,1)S(1)} %collective-permute-done.12.lc.la, ...), custom_call_target="tpu_custom_call" | custom-call | flops 1 | bytes 1 | tf_op jit(solution)/shard_map/attend_hop/pallas_call | solution.py:353
  97.8 3.1 %collective-permute-done.22.left = bf16[256,768]{1,0:T(8,128)(2,1)S(1)} collective-permute-done((bf16[256,768]{1,0:T(8,128)(2,1)S(1)}, bf16[256,768]{1,0:T(8,128)(2,1)S(1)}, u32[]{:S(2)}, u32[]{:S(2)}) %collective-permute-start.22) | collective-permute-done | bytes 393248 | tf_op jit(solution)/shard_map/ppermute | solution.py:31
  100.8 5.6 %collective-permute-done.23.right = bf16[256,768]{1,0:T(8,128)(2,1)S(1)} collective-permute-done((bf16[256,768]{1,0:T(8,128)(2,1)S(1)}, bf16[256,768]{1,0:T(8,128)(2,1)S(1)}, u32[]{:S(2)}, u32[]{:S(2)}) %collective-permute-start.23) | collective-permute-done | bytes 393248 | tf_op jit(solution)/shard_map/ppermute | solution.py:31
  108.6 2.4 %out_own.1.part = f32[256,3072]{1,0:T(8,128)S(1)} custom-call(s32[1]{0:T(128)} %bitcast.1.head, s32[1]{0:T(128)} %bitcast.2.window, s32[32]{0:T(128)S(1)} %copy-done.20, bf16[256,384]{1,0:T(8,128)(2,1)S(1)} %get-tuple-element.94.own, bf16[384,3072]{1,0:T(8,128)(2,1)S(1)} %copy-done.2), custom_call_target="tpu_custom_call" | custom-call | flops 1 | bytes 1 | tf_op jit(solution)/shard_map/out_own/pallas_call | solution.py:464
  111.0 4.8 %collective-permute-done.24.edge_own = bf16[64,384]{1,0:T(8,128)(2,1)S(1)} collective-permute-done((bf16[64,384]{1,0:T(8,128)(2,1)S(1)}, bf16[64,384]{1,0:T(8,128)(2,1)S(1)}, u32[]{:S(2)}, u32[]{:S(2)}) %collective-permute-start.24) | collective-permute-done | bytes 49184 | tf_op jit(solution)/shard_map/ppermute | solution.py:548
  115.8 3.5 %out_project.1 = (f32[64,3072]{1,0:T(8,128)S(1)}, bf16[64,3072]{1,0:T(8,128)(2,1)S(1)}, bf16[64,3072]{1,0:T(8,128)(2,1)S(1)}, bf16[64,3072]{1,0:T(8,128)(2,1)S(1)}) custom-call(s32[1]{0:T(128)} %bitcast.1.head, s32[1]{0:T(128)} %bitcast.2.window, s32[32]{0:T(128)S(1)} %copy-done.20, f32[256,3072]{1,0:T(8,128)S(1)} %out_own.1.part, ...), custom_call_target="tpu_custom_call" | custom-call | flops 1 | bytes 1 | tf_op jit(solution)/shard_map/out_project/pallas_call | solution.py:479
  119.4 3.0 %collective-permute-start.27 = (bf16[64,3072]{1,0:T(8,128)(2,1)S(1)}, bf16[64,3072]{1,0:T(8,128)(2,1)S(1)}, u32[]{:S(2)}, u32[]{:S(2)}) collective-permute-start(bf16[64,3072]{1,0:T(8,128)(2,1)S(1)} %get-tuple-element.104), channel_id=1, source_target_pairs={{0,2},{1,3},{2,4},{3,5},{4,6},{5,7},{6,0},{7,1},{8,10},{9,11},{10,... | collective-permute-start | bytes 1179656 | tf_op jit(solution)/shard_map/ppermute | solution.py:35
  124.9 11.0 %collective-permute-done.27 = bf16[64,3072]{1,0:T(8,128)(2,1)S(1)} collective-permute-done((bf16[64,3072]{1,0:T(8,128)(2,1)S(1)}, bf16[64,3072]{1,0:T(8,128)(2,1)S(1)}, u32[]{:S(2)}, u32[]{:S(2)}) %collective-permute-start.27) | collective-permute-done | bytes 393248 | tf_op jit(solution)/shard_map/ppermute | solution.py:35
  135.9 3.4 %collective-permute-done.28 = bf16[64,3072]{1,0:T(8,128)(2,1)S(1)} collective-permute-done((bf16[64,3072]{1,0:T(8,128)(2,1)S(1)}, bf16[64,3072]{1,0:T(8,128)(2,1)S(1)}, u32[]{:S(2)}, u32[]{:S(2)}) %collective-permute-start.28) | collective-permute-done | bytes 393248 | tf_op jit(solution)/shard_map/ppermute | solution.py:35
  (98 shorter events, 35.1 us)
Async XLA Ops:
  2.3 18.4 %collective-permute-start.1 = (bf16[64,3072]{1,0:T(8,128)(2,1)S(1)}, bf16[64,3072]{1,0:T(8,128)(2,1)S(1)}, u32[]{:S(2)}, u32[]{:S(2)}) collective-permute-start(bf16[64,3072]{1,0:T(8,128)(2,1)S(1)} %modulate.1.refs_0_), channel_id=1, source_target_pairs={{0,6},{1,7},{2,0},{3,1},{4,2},{5,3},{6,4},{7,5},{8,14},{9,15},{10,... | collective-permute-start | bytes 1179656 | tf_op jit(solution)/shard_map/ppermute | solution.py:35
  3.1 19.6 %collective-permute-start.2 = (bf16[64,3072]{1,0:T(8,128)(2,1)S(1)}, bf16[64,3072]{1,0:T(8,128)(2,1)S(1)}, u32[]{:S(2)}, u32[]{:S(2)}) collective-permute-start(bf16[64,3072]{1,0:T(8,128)(2,1)S(1)} %modulate.1.refs_0_), channel_id=1, source_target_pairs={{0,2},{1,3},{2,4},{3,5},{4,6},{5,7},{6,0},{7,1},{8,10},{9,11},{10,... | collective-permute-start | bytes 1179656 | tf_op jit(solution)/shard_map/ppermute | solution.py:35
  5.6 18.0 %collective-permute-start.3 = (bf16[64,3072]{1,0:T(8,128)(2,1)S(1)}, bf16[64,3072]{1,0:T(8,128)(2,1)S(1)}, u32[]{:S(2)}, u32[]{:S(2)}) collective-permute-start(bf16[64,3072]{1,0:T(8,128)(2,1)S(1)} %modulate.1.refs_0_), channel_id=1, source_target_pairs={{0,4},{1,5},{2,6},{3,7},{4,0},{5,1},{6,2},{7,3},{8,12},{9,13},{10,... | collective-permute-start | bytes 1179656 | tf_op jit(solution)/shard_map/ppermute | solution.py:35
  12.6 13.4 %collective-permute-start.4 = (bf16[144,768]{1,0:T(8,128)(2,1)S(1)}, bf16[144,768]{1,0:T(8,128)(2,1)S(1)}, u32[]{:S(2)}, u32[]{:S(2)}) collective-permute-start(bf16[144,768]{1,0:T(8,128)(2,1)S(1)} %project.2.a), channel_id=1, source_target_pairs={{0,8},{8,16},{16,24},{24,32},{32,40},{40,48},{48,56},{56,64},{64,7... | collective-permute-start | bytes 663560 | tf_op jit(solution)/shard_map/ppermute | solution.py:31
  14.5 11.6 %collective-permute-start.5 = (bf16[144,768]{1,0:T(8,128)(2,1)S(1)}, bf16[144,768]{1,0:T(8,128)(2,1)S(1)}, u32[]{:S(2)}, u32[]{:S(2)}) collective-permute-start(bf16[144,768]{1,0:T(8,128)(2,1)S(1)} %project.2.a), channel_id=1, source_target_pairs={{0,248},{8,0},{16,8},{24,16},{32,24},{40,32},{48,40},{56,48},{64,5... | collective-permute-start | bytes 663560 | tf_op jit(solution)/shard_map/ppermute | solution.py:31
  30.8 26.8 %collective-permute-start.11 = (bf16[384,3072]{1,0:T(8,128)(2,1)S(1)}, bf16[384,3072]{1,0:T(8,128)(2,1)S(1)}, u32[]{:S(2)}, u32[]{:S(2)}) collective-permute-start(bf16[384,3072]{1,0:T(8,128)(2,1)S(1)} %copy-done.2), channel_id=1, source_target_pairs={{0,1},{1,0},{2,3},{3,2},{4,5},{5,4},{6,7},{7,6},{8,9},{9,8},{10,11... | collective-permute-start | bytes 7077896 | tf_op jit(solution)/shard_map/ppermute | solution.py:39
  31.0 15.5 %collective-permute-start.13 = (bf16[256,768]{1,0:T(8,128)(2,1)S(1)}, bf16[256,768]{1,0:T(8,128)(2,1)}, u32[]{:S(2)}, u32[]{:S(2)}) collective-permute-start(bf16[256,768]{1,0:T(8,128)(2,1)S(1)} %get-tuple-element.68.b), channel_id=1, source_target_pairs={{0,8},{8,16},{16,24},{24,32},{32,40},{40,48},{48,56},{56,64},{64,7... | collective-permute-start | bytes 1179656 | tf_op jit(solution)/shard_map/ppermute | solution.py:31
  31.0 15.5 %collective-permute-start.15 = (bf16[256,768]{1,0:T(8,128)(2,1)S(1)}, bf16[256,768]{1,0:T(8,128)(2,1)}, u32[]{:S(2)}, u32[]{:S(2)}) collective-permute-start(bf16[256,768]{1,0:T(8,128)(2,1)S(1)} %get-tuple-element.68.b), channel_id=1, source_target_pairs={{0,248},{8,0},{16,8},{24,16},{32,24},{40,32},{48,40},{56,48},{64,5... | collective-permute-start | bytes 1179656 | tf_op jit(solution)/shard_map/ppermute | solution.py:31
  36.7 20.9 %collective-permute-start.10 = (bf16[256,768]{1,0:T(8,128)(2,1)S(1)}, bf16[256,768]{1,0:T(8,128)(2,1)}, u32[]{:S(2)}, u32[]{:S(2)}) collective-permute-start(bf16[256,768]{1,0:T(8,128)(2,1)S(1)} %get-tuple-element.66), channel_id=1, source_target_pairs={{0,248},{8,0},{16,8},{24,16},{32,24},{40,32},{48,40},{56,48},{64,5... | collective-permute-start | bytes 1179656 | tf_op jit(solution)/shard_map/ppermute | solution.py:31
  38.5 19.1 %collective-permute-start.9 = (bf16[256,768]{1,0:T(8,128)(2,1)S(1)}, bf16[256,768]{1,0:T(8,128)(2,1)}, u32[]{:S(2)}, u32[]{:S(2)}) collective-permute-start(bf16[256,768]{1,0:T(8,128)(2,1)S(1)} %get-tuple-element.65.c), channel_id=1, source_target_pairs={{0,8},{8,16},{16,24},{24,32},{32,40},{40,48},{48,56},{56,64},{64,7... | collective-permute-start | bytes 1179656 | tf_op jit(solution)/shard_map/ppermute | solution.py:31
  46.5 25.8 %collective-permute-start.14 = (bf16[256,768]{1,0:T(8,128)(2,1)}, bf16[256,768]{1,0:T(8,128)(2,1)}, u32[]{:S(2)}, u32[]{:S(2)}) collective-permute-start(bf16[256,768]{1,0:T(8,128)(2,1)} %collective-permute-done.13.rb), channel_id=1, source_target_pairs={{0,8},{8,16},{16,24},{24,32},{32,40},{40,48},{48,56},{56,64},{64,7... | collective-permute-start | bytes 1179656 | tf_op jit(solution)/shard_map/ppermute | solution.py:31
  46.5 25.8 %collective-permute-start.16 = (bf16[256,768]{1,0:T(8,128)(2,1)}, bf16[256,768]{1,0:T(8,128)(2,1)}, u32[]{:S(2)}, u32[]{:S(2)}) collective-permute-start(bf16[256,768]{1,0:T(8,128)(2,1)} %collective-permute-done.15.lb), channel_id=1, source_target_pairs={{0,248},{8,0},{16,8},{24,16},{32,24},{40,32},{48,40},{56,48},{64,5... | collective-permute-start | bytes 1179656 | tf_op jit(solution)/shard_map/ppermute | solution.py:31
  59.0 18.8 %collective-permute-start.19 = (bf16[256,768]{1,0:T(8,128)(2,1)}, bf16[256,768]{1,0:T(8,128)(2,1)S(1)}, u32[]{:S(2)}, u32[]{:S(2)}) collective-permute-start(bf16[256,768]{1,0:T(8,128)(2,1)} %collective-permute-done.9.rc.ra), channel_id=1, source_target_pairs={{0,8},{8,16},{16,24},{24,32},{32,40},{40,48},{48,56},{56,64},{64,7... | collective-permute-start | bytes 1179656 | tf_op jit(solution)/shard_map/ppermute | solution.py:31
  59.0 18.9 %collective-permute-start.12 = (bf16[256,768]{1,0:T(8,128)(2,1)}, bf16[256,768]{1,0:T(8,128)(2,1)S(1)}, u32[]{:S(2)}, u32[]{:S(2)}) collective-permute-start(bf16[256,768]{1,0:T(8,128)(2,1)} %collective-permute-done.10.lc.la), channel_id=1, source_target_pairs={{0,248},{8,0},{16,8},{24,16},{32,24},{40,32},{48,40},{56,48},{64,5... | collective-permute-start | bytes 1179656 | tf_op jit(solution)/shard_map/ppermute | solution.py:31
  72.3 14.9 %collective-permute-start.17 = (bf16[256,768]{1,0:T(8,128)(2,1)}, bf16[256,768]{1,0:T(8,128)(2,1)S(1)}, u32[]{:S(2)}, u32[]{:S(2)}) collective-permute-start(bf16[256,768]{1,0:T(8,128)(2,1)} %collective-permute-done.14.rb), channel_id=1, source_target_pairs={{0,8},{8,16},{16,24},{24,32},{32,40},{40,48},{48,56},{56,64},{64,7... | collective-permute-start | bytes 1179656 | tf_op jit(solution)/shard_map/ppermute | solution.py:31
  72.4 14.8 %collective-permute-start.18 = (bf16[256,768]{1,0:T(8,128)(2,1)}, bf16[256,768]{1,0:T(8,128)(2,1)S(1)}, u32[]{:S(2)}, u32[]{:S(2)}) collective-permute-start(bf16[256,768]{1,0:T(8,128)(2,1)} %collective-permute-done.16.lb), channel_id=1, source_target_pairs={{0,248},{8,0},{16,8},{24,16},{32,24},{40,32},{48,40},{56,48},{64,5... | collective-permute-start | bytes 1179656 | tf_op jit(solution)/shard_map/ppermute | solution.py:31
  77.7 11.6 %collective-permute-start.20 = (bf16[128,768]{1,0:T(8,128)(2,1)S(1)}, bf16[128,768]{1,0:T(8,128)(2,1)S(1)}, u32[]{:S(2)}, u32[]{:S(2)}) collective-permute-start(bf16[128,768]{1,0:T(8,128)(2,1)S(1)} %slice.20), channel_id=1, source_target_pairs={{0,8},{8,16},{16,24},{24,32},{32,40},{40,48},{48,56},{56,64},{64,7... | collective-permute-start | bytes 589832 | tf_op jit(solution)/shard_map/ppermute | solution.py:31
  77.9 11.4 %collective-permute-start.21 = (bf16[128,768]{1,0:T(8,128)(2,1)S(1)}, bf16[128,768]{1,0:T(8,128)(2,1)S(1)}, u32[]{:S(2)}, u32[]{:S(2)}) collective-permute-start(bf16[128,768]{1,0:T(8,128)(2,1)S(1)} %slice.21), channel_id=1, source_target_pairs={{0,248},{8,0},{16,8},{24,16},{32,24},{40,32},{48,40},{56,48},{64,5... | collective-permute-start | bytes 589832 | tf_op jit(solution)/shard_map/ppermute | solution.py:31
  90.0 10.9 %collective-permute-start.22 = (bf16[256,768]{1,0:T(8,128)(2,1)S(1)}, bf16[256,768]{1,0:T(8,128)(2,1)S(1)}, u32[]{:S(2)}, u32[]{:S(2)}) collective-permute-start(bf16[256,768]{1,0:T(8,128)(2,1)S(1)} %get-tuple-element.88), channel_id=1, source_target_pairs={{0,248},{8,0},{16,8},{24,16},{32,24},{40,32},{48,40},{56,48},{64,5... | collective-permute-start | bytes 1179656 | tf_op jit(solution)/shard_map/ppermute | solution.py:31
  95.3 11.1 %collective-permute-start.23 = (bf16[256,768]{1,0:T(8,128)(2,1)S(1)}, bf16[256,768]{1,0:T(8,128)(2,1)S(1)}, u32[]{:S(2)}, u32[]{:S(2)}) collective-permute-start(bf16[256,768]{1,0:T(8,128)(2,1)S(1)} %get-tuple-element.89), channel_id=1, source_target_pairs={{0,8},{8,16},{16,24},{24,32},{32,40},{40,48},{48,56},{56,64},{64,7... | collective-permute-start | bytes 1179656 | tf_op jit(solution)/shard_map/ppermute | solution.py:31
  108.2 7.6 %collective-permute-start.26 = (bf16[256,384]{1,0:T(8,128)(2,1)S(1)}, bf16[256,384]{1,0:T(8,128)(2,1)S(1)}, u32[]{:S(2)}, u32[]{:S(2)}) collective-permute-start(bf16[256,384]{1,0:T(8,128)(2,1)S(1)} %get-tuple-element.97), channel_id=1, source_target_pairs={{0,1},{1,0},{2,3},{3,2},{4,5},{5,4},{6,7},{7,6},{8,9},{9,8},{10,11... | collective-permute-start | bytes 589832 | tf_op jit(solution)/shard_map/ppermute | solution.py:39
  119.4 16.5 %collective-permute-start.27 = (bf16[64,3072]{1,0:T(8,128)(2,1)S(1)}, bf16[64,3072]{1,0:T(8,128)(2,1)S(1)}, u32[]{:S(2)}, u32[]{:S(2)}) collective-permute-start(bf16[64,3072]{1,0:T(8,128)(2,1)S(1)} %get-tuple-element.104), channel_id=1, source_target_pairs={{0,2},{1,3},{2,4},{3,5},{4,6},{5,7},{6,0},{7,1},{8,10},{9,11},{10,... | collective-permute-start | bytes 1179656 | tf_op jit(solution)/shard_map/ppermute | solution.py:35
  122.4 16.8 %collective-permute-start.28 = (bf16[64,3072]{1,0:T(8,128)(2,1)S(1)}, bf16[64,3072]{1,0:T(8,128)(2,1)S(1)}, u32[]{:S(2)}, u32[]{:S(2)}) collective-permute-start(bf16[64,3072]{1,0:T(8,128)(2,1)S(1)} %get-tuple-element.105), channel_id=1, source_target_pairs={{0,6},{1,7},{2,0},{3,1},{4,2},{5,3},{6,4},{7,5},{8,14},{9,15},{10,... | collective-permute-start | bytes 1179656 | tf_op jit(solution)/shard_map/ppermute | solution.py:35
  122.4 16.8 %collective-permute-start.29 = (bf16[64,3072]{1,0:T(8,128)(2,1)S(1)}, bf16[64,3072]{1,0:T(8,128)(2,1)S(1)}, u32[]{:S(2)}, u32[]{:S(2)}) collective-permute-start(bf16[64,3072]{1,0:T(8,128)(2,1)S(1)} %get-tuple-element.106), channel_id=1, source_target_pairs={{0,4},{1,5},{2,6},{3,7},{4,0},{5,1},{6,2},{7,3},{8,12},{9,13},{10,... | collective-permute-start | bytes 1179656 | tf_op jit(solution)/shard_map/ppermute | solution.py:35
  (28 other events, 167.4 us)
